TPU v7x, 512 devices: a whole 4x8x8 slice. The times are simulated.
512 devices in a mesh: seq: 16 (over x, z_lo), tensor: 32 (over z_hi, y, core).
Axes of the slice: x: 4, y: 8, z: 8 (z_hi: 2, z_lo: 4; z = z_hi * 4 + z_lo), core: 2. Of those that a mesh axis runs over, the one named last changes fastest.
Arguments:
- inputs: bfloat16 [3072, 8192], P(('seq', 'tensor')), may hold values from -6 to 6
- grad_out: bfloat16 [3072, 8192], P(('seq', 'tensor')), may hold values from -6 to 6
- up_blocks: bfloat16 [224, 8, 128, 128], P('tensor'), may hold values from -0.1875 to 0.1875
- up_index: int32 [224, 8], P('tensor'), may hold values from 0 to 63, as said below
- down_blocks: bfloat16 [224, 8, 128, 128], P('tensor'), may hold values from -0.1875 to 0.1875
- down_index: int32 [224, 8], P('tensor'), may hold values from 0 to 63, as said below
Outputs:
- grad_in: bfloat16 [3072, 8192], P(('seq', 'tensor'))
- grad_up: bfloat16 [224, 8, 128, 128], P('tensor', None, 'seq')
- grad_down: bfloat16 [224, 8, 128, 128], P('tensor', None, 'seq')
Inputs may be any that keep to these rules, and one draw needn't show every extreme that they name: `up_index`: in every row the 8 block numbers are different, and every number from 0 to 63 appears in some row. `down_index`: in every row the 8 block numbers are different, and every number from 0 to 63 appears in some row.
All inputs are finite; a program needn't handle non-finite values.
Results may differ from a plain program's by a relative error of at most 0.012.
Values may be sent and summed in bfloat16 or wider, within the bound.
No kernel may reach another device: no remote copies, remote signals or barrier semaphores. Data moves between devices by JAX's collectives and lax.ppermute only.
A program may use at most 64 MiB of HBM per device.

v0:
```python
import math

import jax
import jax.numpy as jnp
from jax import lax
from jax.sharding import PartitionSpec as P


def local(inputs, grad_out, up_blocks, up_index, down_blocks, down_index):
    tensor_count = lax.axis_size("tensor")
    seq_count = lax.axis_size("seq")
    rows_here, features = inputs.shape
    local_blocks, slots, block, _ = up_blocks.shape
    blocks_wide = features // block
    group_rows = rows_here * tensor_count
    factor = 1.0 / math.sqrt(group_rows * seq_count)
    flat_index = up_index.reshape(-1)
    in_rows = lax.all_gather(inputs, "tensor", axis=0, tiled=True)
    grad_rows = lax.all_gather(grad_out, "tensor", axis=0, tiled=True)
    piece_rows = in_rows.shape[0]
    picked = jnp.take(in_rows.reshape(piece_rows, blocks_wide, block), up_index, axis=1)
    picked_grad = jnp.take(grad_rows.reshape(piece_rows, blocks_wide, block), down_index, axis=1)
    preact = jnp.einsum("rjkc,jkch->rjh", picked, up_blocks, preferred_element_type=jnp.float32)
    hidden_grad = jnp.einsum(
        "rjko,jkho->rjh", picked_grad, down_blocks, preferred_element_type=jnp.float32
    )
    gating = jax.nn.sigmoid(preact)
    activated = (preact * gating).astype(jnp.bfloat16)
    preact_grad = (hidden_grad * gating * (1.0 + preact * (1.0 - gating))).astype(jnp.bfloat16)
    up_sum = jnp.einsum("rjkc,rjh->jkch", picked, preact_grad, preferred_element_type=jnp.float32)
    down_sum = jnp.einsum(
        "rjh,rjko->jkho", activated, picked_grad, preferred_element_type=jnp.float32
    )
    contrib = jnp.einsum(
        "rjh,jkch->rjkc", preact_grad, up_blocks, preferred_element_type=jnp.float32
    )
    contrib = contrib.reshape(piece_rows, local_blocks * slots, block)
    partial_value = (
        jnp.zeros((piece_rows, blocks_wide, block), jnp.float32).at[:, flat_index].add(contrib)
    )
    input_grad = partial_value
    up_sum, down_sum, input_grad = (up_sum, down_sum, input_grad)
    share = block // seq_count
    up_part = (
        (up_sum * factor).astype(jnp.bfloat16).reshape(local_blocks, slots, seq_count, share, block)
    )
    down_part = (
        (down_sum * factor)
        .astype(jnp.bfloat16)
        .reshape(local_blocks, slots, seq_count, share, block)
    )
    up_recv, down_recv = (
        lax.all_to_all(up_part, "seq", split_axis=2, concat_axis=2, tiled=True),
        lax.all_to_all(down_part, "seq", split_axis=2, concat_axis=2, tiled=True),
    )
    grad_up = jnp.sum(up_recv.astype(jnp.float32), axis=2).astype(jnp.bfloat16)
    grad_down = jnp.sum(down_recv.astype(jnp.float32), axis=2).astype(jnp.bfloat16)
    partial_rows = input_grad.reshape(group_rows, features).astype(jnp.bfloat16)
    pieces = partial_rows.reshape(tensor_count, rows_here, features)
    received = lax.all_to_all(pieces, "tensor", split_axis=0, concat_axis=0, tiled=True)
    grad_in = jnp.sum(received.astype(jnp.float32), axis=0).astype(jnp.bfloat16)
    return (grad_in, grad_up, grad_down)


def solution(mesh):
    return jax.shard_map(
        local,
        mesh=mesh,
        in_specs=(
            P(("seq", "tensor"), None),
            P(("seq", "tensor"), None),
            P("tensor", None, None, None),
            P("tensor", None),
            P("tensor", None, None, None),
            P("tensor", None),
        ),
        out_specs=(
            P(("seq", "tensor"), None),
            P("tensor", None, "seq", None),
            P("tensor", None, "seq", None),
        ),
        check_vma=False,
    )
```

profile of v0, /device:TPU:30, one launch (start us, length us, event | category | flops | bytes accessed | tf_op | source)
XLA Modules:
  0.0 500.2 jit_solution(10935653231558683681)
XLA Ops:
  7.2 0.0 copy-start
  7.2 0.0 all-gather.7.cloned.1.call-start
  7.2 0.7 all-gather.7.cloned.1.call-update
  7.9 0.0 all-gather.5.cloned.1.call-start
  8.0 0.7 all-gather.5.cloned.1.call-update
  8.7 0.7 compare_select_fusion.1
  9.4 0.1 reshape.101
  9.4 0.7 compare_select_fusion
  10.1 0.1 reshape.105
  10.2 0.7 compare_and_fusion.1
  10.9 0.7 compare_and_fusion
  11.6 110.3 %all-gather.7.cloned.1.call-done = bf16[32,6,8192]{2,1,0:T(8,128)(2,1)} async-done(((bf16[1,6,8192]{2,1,0:T(8,128)(2,1)}), bf16[32,6,8192]{2,1,0:T(8,128)(2,1)}) %all-gather.7.cloned.1.call-update) | async-done | bytes 3145744 | tf_op jit(solution)/shard_map/all_gather | solution.py:18
  121.9 7.9 %reshape.63 = bf16[192,64,128]{2,1,0:T(8,128)(2,1)} reshape(bf16[32,6,8192]{2,1,0:T(8,128)(2,1)} %all-gather.7.cloned.1.call-done) | data formatting | bytes 6291456 | tf_op jit(solution)/shard_map/reshape | solution.py:21
  129.7 5.6 %copy.18 = bf16[192,64,128]{2,0,1:T(8,128)(2,1)} copy(bf16[192,64,128]{2,1,0:T(8,128)(2,1)} %reshape.63) | data formatting | bytes 6291456 | tf_op jit(solution)/shard_map/reshape | solution.py:21
  135.3 90.5 %all-gather.5.cloned.1.call-done = bf16[32,6,8192]{2,1,0:T(8,128)(2,1)} async-done(((bf16[1,6,8192]{2,1,0:T(8,128)(2,1)}), bf16[32,6,8192]{2,1,0:T(8,128)(2,1)}) %all-gather.5.cloned.1.call-update) | async-done | bytes 3145744 | tf_op jit(solution)/shard_map/all_gather | solution.py:19
  225.9 7.9 %reshape.62 = bf16[192,64,128]{2,1,0:T(8,128)(2,1)} reshape(bf16[32,6,8192]{2,1,0:T(8,128)(2,1)} %all-gather.5.cloned.1.call-done) | data formatting | bytes 6291456 | tf_op jit(solution)/shard_map/reshape | solution.py:22
  233.7 5.6 %copy.17 = bf16[192,64,128]{2,0,1:T(8,128)(2,1)} copy(bf16[192,64,128]{2,1,0:T(8,128)(2,1)} %reshape.62) | data formatting | bytes 6291456 | tf_op jit(solution)/shard_map/reshape | solution.py:22
  239.3 4.4 gather_fusion
  243.7 4.4 gather_fusion.1
  248.1 0.0 copy-done
  248.1 0.0 copy-start.2
  248.1 2.9 fusion.21
  250.9 0.0 copy-done.2
  250.9 2.8 fusion.9
  253.7 3.8 copy.22
  257.5 3.3 copy.23
  260.8 5.2 %all-to-all-start.2 = ((bf16[7,8,16,8,128]{4,3,1,0,2:T(8,128)(2,1)}), bf16[7,8,16,8,128]{4,3,1,0,2:T(8,128)(2,1)}, u32[]{:S(2)}, u32[]{:S(2)}) async-start(bf16[7,8,16,8,128]{4,3,1,0,2:T(8,128)(2,1)} %copy.23), calls=%async_computation.2 | async-start | bytes 3670016 | tf_op jit(solution)/shard_map/all_to_all | solution.py:54
  266.0 0.0 copy-start.1
  266.0 3.4 fusion.33
  269.4 0.0 copy-done.1
  269.4 1.5 fusion.8
  270.9 1.7 copy.20
  272.6 0.0 copy-start.3
  272.7 36.2 %all-to-all-done.2 = bf16[7,8,16,8,128]{4,3,1,0,2:T(8,128)(2,1)} async-done(((bf16[7,8,16,8,128]{4,3,1,0,2:T(8,128)(2,1)}), bf16[7,8,16,8,128]{4,3,1,0,2:T(8,128)(2,1)}, u32[]{:S(2)}, u32[]{:S(2)}) %all-to-all-start.2) | async-done | bytes 1835040 | tf_op jit(solution)/shard_map/all_to_all | solution.py:54
  308.9 6.6 %all-to-all-start.1 = ((bf16[7,8,16,8,128]{4,3,1,0,2:T(8,128)(2,1)}), bf16[7,8,16,8,128]{4,3,1,0,2:T(8,128)(2,1)}, u32[]{:S(2)}, u32[]{:S(2)}) async-start(bf16[7,8,16,8,128]{4,3,1,0,2:T(8,128)(2,1)} %copy.20), calls=%async_computation.1 | async-start | bytes 3670016 | tf_op jit(solution)/shard_map/all_to_all | solution.py:53
  315.5 0.0 copy-done.3
  315.5 0.1 reshape.61
  315.6 3.3 fusion.43
  318.9 3.4 broadcast_in_dim.13
  322.3 16.1 %scatter_fusion = f32[192,64,128]{2,0,1:T(8,128)} fusion(f32[192,64,128]{2,0,1:T(8,128)} %broadcast_in_dim.13, s32[56]{0:T(128)S(1)} %fusion.37, f32[56,192,128]{2,1,0:T(8,128)} %bitcast.74), kind=kCustom, calls=%fused_computation.2 | custom fusion | flops 1376256 | bytes 16515296 | tf_op jit(solution)/shard_map/scatter-add | solution.py:39
  338.4 3.3 convert_element_type.29
  341.8 3.7 copy.19
  345.5 7.3 %convert_element_type.30 = bf16[32,6,8192]{2,1,0:T(8,128)(2,1)} reshape(bf16[192,64,128]{2,1,0:T(8,128)(2,1)} %copy.19) | data formatting | bytes 6291456 | tf_op jit(solution)/shard_map/convert_element_type | solution.py:58
  352.8 4.7 all-to-all-done.1
  357.5 7.1 %all-to-all-start = ((bf16[32,6,8192]{2,1,0:T(8,128)(2,1)}), bf16[32,6,8192]{2,1,0:T(8,128)(2,1)}, u32[]{:S(2)}, u32[]{:S(2)}) async-start(bf16[32,6,8192]{2,1,0:T(8,128)(2,1)} %convert_element_type.30), calls=%async_computation | async-start | bytes 8388608 | tf_op jit(solution)/shard_map/all_to_all | solution.py:60
  364.6 2.5 reduce_sum.38
  367.1 2.5 reduce_sum.37
  369.7 120.0 %all-to-all-done = bf16[32,6,8192]{2,1,0:T(8,128)(2,1)} async-done(((bf16[32,6,8192]{2,1,0:T(8,128)(2,1)}), bf16[32,6,8192]{2,1,0:T(8,128)(2,1)}, u32[]{:S(2)}, u32[]{:S(2)}) %all-to-all-start) | async-done | bytes 3145760 | tf_op jit(solution)/shard_map/all_to_all | solution.py:60
  489.7 3.7 reduce_sum.36
  (3 shorter events, 0.0 us)
Async XLA Ops:
  7.2 240.9 %copy-start = (bf16[7,8,128,128]{3,2,1,0:T(8,128)(2,1)S(1)}, bf16[7,8,128,128]{3,2,1,0:T(8,128)(2,1)}, u32[]{:S(2)}) copy-start(bf16[7,8,128,128]{3,2,1,0:T(8,128)(2,1)} %param.10) | copy-start | bytes 5505028
  7.2 114.7 %all-gather.7.cloned.1.call-start = ((), (), s32[]{:S(2)}) async-start(), calls=%async_computation.4 | async-start | bytes 4325376 | tf_op jit(solution)/shard_map/all_gather | solution.py:18
  7.9 218.0 %all-gather.5.cloned.1.call-start = ((), (), s32[]{:S(2)}) async-start(), calls=%async_computation.3 | async-start | bytes 4325376 | tf_op jit(solution)/shard_map/all_gather | solution.py:19
  248.1 2.9 copy-start.2
  260.8 48.1 %all-to-all-start.2 = ((bf16[7,8,16,8,128]{4,3,1,0,2:T(8,128)(2,1)}), bf16[7,8,16,8,128]{4,3,1,0,2:T(8,128)(2,1)}, u32[]{:S(2)}, u32[]{:S(2)}) async-start(bf16[7,8,16,8,128]{4,3,1,0,2:T(8,128)(2,1)} %copy.23), calls=%async_computation.2 | async-start | bytes 3670016 | tf_op jit(solution)/shard_map/all_to_all | solution.py:54
  266.0 3.4 copy-start.1
  272.6 42.8 %copy-start.3 = (s32[7,8]{1,0:T(8,128)S(1)}, s32[7,8]{1,0:T(8,128)}, u32[]{:S(2)}) copy-start(s32[7,8]{1,0:T(8,128)} %param.11) | copy-start | bytes 676
  308.9 48.6 %all-to-all-start.1 = ((bf16[7,8,16,8,128]{4,3,1,0,2:T(8,128)(2,1)}), bf16[7,8,16,8,128]{4,3,1,0,2:T(8,128)(2,1)}, u32[]{:S(2)}, u32[]{:S(2)}) async-start(bf16[7,8,16,8,128]{4,3,1,0,2:T(8,128)(2,1)} %copy.20), calls=%async_computation.1 | async-start | bytes 3670016 | tf_op jit(solution)/shard_map/all_to_all | solution.py:53
  357.5 132.2 %all-to-all-start = ((bf16[32,6,8192]{2,1,0:T(8,128)(2,1)}), bf16[32,6,8192]{2,1,0:T(8,128)(2,1)}, u32[]{:S(2)}, u32[]{:S(2)}) async-start(bf16[32,6,8192]{2,1,0:T(8,128)(2,1)} %convert_element_type.30), calls=%async_computation | async-start | bytes 8388608 | tf_op jit(solution)/shard_map/all_to_all | solution.py:60
Sparse Core Ops, SparseCore 0:
  11.4 110.4 all-gather.6
  125.2 100.6 all-gather.4
where the time goes:
time: 502 us; the launch traced here: 500 us
  waiting for transfers between devices  363 us (72%)
  local copies, waits for them, and re-layouts  59.2 us (12%)
  other arithmetic  31 us (6%)
  starting transfers between devices  19 us (4%)
  between operations  14.1 us (3%)
  matrix products  13.9 us (3%)
    all_to_all x1, waiting for transfers between devices, local(): lax.all_to_all(pieces, 'tensor', split_axis=0, concat_axis=0, tiled=True)  120 us
    all_gather x1, waiting for transfers between devices, local(): in_rows = lax.all_gather(inputs, 'tensor', axis=0, tiled=True)  110 us
    all_gather x1, waiting for transfers between devices, local(): grad_rows = lax.all_gather(grad_out, 'tensor', axis=0, tiled=True)  90.5 us
    all_to_all x1, waiting for transfers between devices, local(): lax.all_to_all(down_part, 'seq', split_axis=2, concat_axis=2, tiled=True)  36.2 us
    scatter-add x1, other arithmetic, local(): jnp.zeros((piece_rows, blocks_wide, block), jnp.float32).at[:, flat_index]  16.1 us
    reshape x2, local copies, waits for them, and re-layouts, local(): in_rows.reshape(piece_rows, blocks_wide, block)  13.5 us
    reshape x2, local copies, waits for them, and re-layouts, local(): grad_rows.reshape(piece_rows, blocks_wide, block)  13.4 us
    convert_element_type x2, local copies, waits for them, and re-layouts, local(): partial_rows = input_grad.reshape(group_rows, features).astype(jnp.bfloat16)  11.1 us
  transfers between devices with their start and end apart: 5, of which 5 were waited for; matrix products, arithmetic and copies ran while one was open for 13% of the time, Pallas kernels for 0%

commit v1 on v0

v1 whole, which is shorter than its diff:
```python
import functools
import math

import jax
import jax.numpy as jnp
from jax import lax
from jax.experimental import pallas as pl
from jax.experimental.pallas import tpu as pltpu
from jax.sharding import PartitionSpec as P

Z_HI, Y, CORE = 2, 8, 2
X, Z_LO = 4, 4
VMEM_LIMIT = 40 * 1024 * 1024


def tensor_id(zh, y, c):
    return (zh * Y + y) * CORE + c


def tensor_pairs(move):
    return [
        (tensor_id(zh, y, c), tensor_id(*move(zh, y, c)))
        for zh in range(Z_HI)
        for y in range(Y)
        for c in range(CORE)
    ]


SIBLING = tensor_pairs(lambda zh, y, c: (zh, y, 1 - c))
Z_PARTNER = tensor_pairs(lambda zh, y, c: (1 - zh, y, c))
Y_UP = tensor_pairs(lambda zh, y, c: (zh, (y + 1) % Y, c))
Y_DOWN = tensor_pairs(lambda zh, y, c: (zh, (y - 1) % Y, c))
Y_GROUPS = [[tensor_id(zh, y, c) for y in range(Y)] for zh in range(Z_HI) for c in range(CORE)]
X_GROUPS = [[x * Z_LO + z for x in range(X)] for z in range(Z_LO)]
Z_GROUPS = [[x * Z_LO + z for z in range(Z_LO)] for x in range(X)]

NT = (((1,), (1,)), ((), ()))
TN = (((0,), (0,)), ((), ()))


def weight_kernel(factor, core_ref, upi_ref, downi_ref, mine_ref, other_ref, up_ref, down_ref,
                  parts_ref, pg_ref, x_ref, g_ref, xj_ref, gj_ref, wj_ref, sem):
    j = pl.program_id(0)
    slots = up_ref.shape[1]
    block = up_ref.shape[2]
    share = parts_ref.shape[4]

    @pl.when(j == 0)
    def _():
        @pl.when(core_ref[0] == 0)
        def _():
            first = pltpu.make_async_copy(mine_ref, x_ref, sem.at[0])
            second = pltpu.make_async_copy(other_ref, g_ref, sem.at[1])
            first.start()
            second.start()
            first.wait()
            second.wait()

        @pl.when(core_ref[0] != 0)
        def _():
            first = pltpu.make_async_copy(other_ref, x_ref, sem.at[0])
            second = pltpu.make_async_copy(mine_ref, g_ref, sem.at[1])
            first.start()
            second.start()
            first.wait()
            second.wait()

    for k in range(slots):
        here = pl.ds(k * block, block)
        at = pl.multiple_of(upi_ref[j, k] * block, block)
        xj_ref[:, here] = x_ref[:, pl.ds(at, block)]
        at = pl.multiple_of(downi_ref[j, k] * block, block)
        gj_ref[:, here] = g_ref[:, pl.ds(at, block)]
        wj_ref[:, here] = down_ref[0, k]
    xj = xj_ref[...]
    gj = gj_ref[...]
    preact = jnp.dot(xj, up_ref[0].reshape(slots * block, block), preferred_element_type=jnp.float32)
    hidden = lax.dot_general(gj, wj_ref[...], NT, preferred_element_type=jnp.float32)
    gating = jax.nn.sigmoid(preact)
    activated = (preact * gating).astype(jnp.bfloat16)
    pg = (hidden * gating * (1.0 + preact * (1.0 - gating))).astype(jnp.bfloat16)
    pg_ref[0] = pg
    up_sum = lax.dot_general(xj, pg, TN, preferred_element_type=jnp.float32)
    up_sum = (up_sum * factor).astype(jnp.bfloat16)
    down_sum = lax.dot_general(activated, gj, TN, preferred_element_type=jnp.float32)
    down_sum = (down_sum * factor).astype(jnp.bfloat16)
    for q in range(parts_ref.shape[0]):
        for k in range(slots):
            parts_ref[q, 0, 0, k] = up_sum[k * block + q * share:k * block + (q + 1) * share]
            parts_ref[q, 1, 0, k] = down_sum[q * share:(q + 1) * share, k * block:(k + 1) * block]


def input_kernel(core_ref, upi_ref, pg_ref, up_ref, keep_ref, send_ref, acc_ref):
    j = pl.program_id(0)
    slots = up_ref.shape[1]
    block = up_ref.shape[2]
    half = keep_ref.shape[1]

    @pl.when(j == 0)
    def _():
        acc_ref[...] = jnp.zeros_like(acc_ref)

    terms = lax.dot_general(pg_ref[0], up_ref[0].reshape(slots * block, block), NT,
                            preferred_element_type=jnp.float32)
    for k in range(slots):
        at = pl.multiple_of(upi_ref[j, k] * block, block)
        acc_ref[:, pl.ds(at, block)] += terms[:, k * block:(k + 1) * block]

    @pl.when(j == pl.num_programs(0) - 1)
    def _():
        own = pl.multiple_of(core_ref[0] * half, half)
        rest = pl.multiple_of((1 - core_ref[0]) * half, half)
        keep_ref[...] = acc_ref[:, pl.ds(own, half)].astype(jnp.bfloat16)
        send_ref[...] = acc_ref[:, pl.ds(rest, half)].astype(jnp.bfloat16)


def weight_parts(factor, core, up_index, down_index, mine, other, up_blocks, down_blocks):
    hidden, slots, block, _ = up_blocks.shape
    rows, features = mine.shape
    share = block // X
    whole = pl.BlockSpec((1, slots, block, block), lambda j, *_: (j, 0, 0, 0))
    flops = 4 * 2 * rows * hidden * slots * block * block
    return pl.pallas_call(
        functools.partial(weight_kernel, factor),
        grid_spec=pltpu.PrefetchScalarGridSpec(
            num_scalar_prefetch=3,
            grid=(hidden,),
            in_specs=[pl.BlockSpec(memory_space=pl.ANY), pl.BlockSpec(memory_space=pl.ANY), whole, whole],
            out_specs=[
                pl.BlockSpec((X, 2, 1, slots, share, block), lambda j, *_: (0, 0, j, 0, 0, 0)),
                pl.BlockSpec((1, rows, block), lambda j, *_: (j, 0, 0)),
            ],
            scratch_shapes=[
                pltpu.VMEM((rows, features), jnp.bfloat16),
                pltpu.VMEM((rows, features), jnp.bfloat16),
                pltpu.VMEM((rows, slots * block), jnp.bfloat16),
                pltpu.VMEM((rows, slots * block), jnp.bfloat16),
                pltpu.VMEM((block, slots * block), jnp.bfloat16),
                pltpu.SemaphoreType.DMA((2,)),
            ],
        ),
        out_shape=[
            jax.ShapeDtypeStruct((X, 2, hidden, slots, share, block), jnp.bfloat16),
            jax.ShapeDtypeStruct((hidden, rows, block), jnp.bfloat16),
        ],
        compiler_params=pltpu.CompilerParams(vmem_limit_bytes=VMEM_LIMIT),
        cost_estimate=pl.CostEstimate(flops=flops, bytes_accessed=14 * 2**20, transcendentals=0),
        name="weight_parts",
    )(core, up_index, down_index, mine, other, up_blocks, down_blocks)


def input_parts(core, up_index, pg, up_blocks, features):
    hidden, slots, block, _ = up_blocks.shape
    rows = pg.shape[1]
    half = features // 2
    flops = 2 * rows * hidden * slots * block * block
    out = pl.BlockSpec((rows, half), lambda j, *_: (0, 0))
    return pl.pallas_call(
        input_kernel,
        grid_spec=pltpu.PrefetchScalarGridSpec(
            num_scalar_prefetch=2,
            grid=(hidden,),
            in_specs=[
                pl.BlockSpec((1, rows, block), lambda j, *_: (j, 0, 0)),
                pl.BlockSpec((1, slots, block, block), lambda j, *_: (j, 0, 0, 0)),
            ],
            out_specs=[out, out],
            scratch_shapes=[pltpu.VMEM((rows, features), jnp.float32)],
        ),
        out_shape=[jax.ShapeDtypeStruct((rows, half), jnp.bfloat16)] * 2,
        compiler_params=pltpu.CompilerParams(vmem_limit_bytes=VMEM_LIMIT),
        cost_estimate=pl.CostEstimate(flops=flops, bytes_accessed=6 * 2**20, transcendentals=0),
        name="input_parts",
    )(core, up_index, pg, up_blocks)


def in_order(first_is_mine, mine, other):
    a = jnp.where(first_is_mine, mine, other)
    b = jnp.where(first_is_mine, other, mine)
    return jnp.concatenate([a, b], axis=0)


def add(a, b):
    return (a.astype(jnp.float32) + b.astype(jnp.float32)).astype(jnp.bfloat16)


def gather_rows(inputs, grad_out, core, y, z_hi):
    send = jnp.where(core == 0, grad_out, inputs)
    keep = jnp.where(core == 0, inputs, grad_out)
    pair = in_order(core == 0, keep, lax.ppermute(send, "tensor", SIBLING))
    chunk = in_order(z_hi == 0, pair, lax.ppermute(pair, "tensor", Z_PARTNER))
    rows, features = chunk.shape
    half = features // 2
    whole = jnp.zeros((Y, rows, features), chunk.dtype)

    def place(whole, piece, steps, column=0):
        return lax.dynamic_update_slice(whole, piece[None], ((y - steps) & (Y - 1), 0, column))

    whole = place(whole, chunk, 0)
    up = down = chunk
    for step in range(1, Y // 2):
        up = lax.ppermute(up, "tensor", Y_UP)
        down = lax.ppermute(down, "tensor", Y_DOWN)
        whole = place(whole, up, step)
        whole = place(whole, down, Y - step)
    last_up = lax.ppermute(up[:, :half], "tensor", Y_UP)
    last_down = lax.ppermute(down[:, half:], "tensor", Y_DOWN)
    whole = place(whole, last_up, Y // 2)
    whole = place(whole, last_down, Y // 2, half)
    return whole.reshape(Y * rows, features)


def reduce_weights(parts):
    _, kinds, hidden, slots, share, block = parts.shape
    units = kinds * hidden * slots
    part = lax.all_to_all(parts.reshape(X, units, share, block), "seq", 0, 0,
                          axis_index_groups=X_GROUPS, tiled=True)
    part = jnp.sum(part.astype(jnp.float32), axis=0).astype(jnp.bfloat16)
    part = part.reshape(units, Z_LO, share // Z_LO, block).transpose(1, 0, 2, 3)
    part = lax.all_to_all(part, "seq", 0, 0, axis_index_groups=Z_GROUPS, tiled=True)
    part = jnp.sum(part.astype(jnp.float32), axis=0).astype(jnp.bfloat16)
    part = part.reshape(kinds, hidden, slots, share // Z_LO, block)
    return part[0], part[1]


def reduce_inputs(keep, send, core, z_hi):
    part = add(keep, lax.ppermute(send, "tensor", SIBLING))
    part = lax.psum_scatter(part, "tensor", axis_index_groups=Y_GROUPS, tiled=True)
    rows = part.shape[0] // 2
    mine = lax.dynamic_slice_in_dim(part, z_hi * rows, rows)
    theirs = lax.dynamic_slice_in_dim(part, (1 - z_hi) * rows, rows)
    part = add(mine, lax.ppermute(theirs, "tensor", Z_PARTNER))
    rows = rows // 2
    mine = lax.dynamic_slice_in_dim(part, core * rows, rows)
    theirs = lax.dynamic_slice_in_dim(part, (1 - core) * rows, rows)
    other = lax.ppermute(theirs, "tensor", SIBLING)
    left = jnp.where(core == 0, mine, other)
    right = jnp.where(core == 0, other, mine)
    return jnp.concatenate([left, right], axis=1)


def local(inputs, grad_out, up_blocks, up_index, down_blocks, down_index):
    t = lax.axis_index("tensor")
    core = t & (CORE - 1)
    y = (t >> 1) & (Y - 1)
    z_hi = t >> 4
    rows_here, features = inputs.shape
    factor = 1.0 / math.sqrt(rows_here * lax.axis_size("tensor") * lax.axis_size("seq"))
    mine = gather_rows(inputs, grad_out, core, y, z_hi)
    other = lax.ppermute(mine, "tensor", SIBLING)
    core_arg = core.reshape(1).astype(jnp.int32)
    parts, pg = weight_parts(factor, core_arg, up_index, down_index, mine, other, up_blocks, down_blocks)
    keep, send = input_parts(core_arg, up_index, pg, up_blocks, features)
    grad_up, grad_down = reduce_weights(parts)
    grad_in = reduce_inputs(keep, send, core, z_hi)
    return (grad_in, grad_up, grad_down)


def solution(mesh):
    return jax.shard_map(
        local,
        mesh=mesh,
        in_specs=(
            P(("seq", "tensor"), None),
            P(("seq", "tensor"), None),
            P("tensor", None, None, None),
            P("tensor", None),
            P("tensor", None, None, None),
            P("tensor", None),
        ),
        out_specs=(
            P(("seq", "tensor"), None),
            P("tensor", None, "seq", None),
            P("tensor", None, "seq", None),
        ),
        check_vma=False,
    )
```

time: 502 us -> 213 us (0.42)
  the two profiles are of different devices: /device:TPU:30 before, /device:TPU:25 now
where the time goes in v1:
time: 213 us; the launch traced here: 212 us
  waiting for transfers between devices  91.2 us (43%)
  starting transfers between devices  76.4 us (36%)
  between operations  14.4 us (7%)
  Pallas kernels  12.1 us (6%)
  other arithmetic  11.3 us (5%)
  local copies, waits for them, and re-layouts  6.31 us (3%)
    all_to_all x1, waiting for transfers between devices, reduce_weights(): lax.all_to_all(parts.reshape(X, units, share, block), 'seq', 0, 0, axis_i...  40 us
    all_to_all x1, waiting for transfers between devices, reduce_weights(): lax.all_to_all(part, 'seq', 0, 0, axis_index_groups=Z_GROUPS, tiled=True)  20.3 us
    ppermute x3, starting transfers between devices, gather_rows(): up = lax.ppermute(up, 'tensor', Y_UP)  14.3 us
    ppermute x1, starting transfers between devices, local(): other = lax.ppermute(mine, 'tensor', SIBLING)  12 us
    ppermute x1, starting transfers between devices, gather_rows(): chunk = in_order(z_hi == 0, pair, lax.ppermute(pair, 'tensor', Z_PARTNER))  10.6 us
    ppermute x3, waiting for transfers between devices, gather_rows(): up = lax.ppermute(up, 'tensor', Y_UP)  9.45 us
    pallas_call x1, Pallas kernels, weight_parts(): pl.pallas_call(functools.partial(weight_kernel, factor), grid_spec=pltpu....  8.19 us
    all_to_all x1, starting transfers between devices, reduce_weights(): lax.all_to_all(part, 'seq', 0, 0, axis_index_groups=Z_GROUPS, tiled=True)  6.96 us
  transfers between devices with their start and end apart: 17, of which 13 were waited for; matrix products, arithmetic and copies ran while one was open for 5% of the time, Pallas kernels for 0%

profile of v1, /device:TPU:25, one launch (start us, length us, event | category | flops | bytes accessed | tf_op | source)
XLA Modules:
  0.0 211.8 jit_solution(12621237467373608707)
XLA Ops:
  7.2 0.9 broadcast_select_fusion.4
  8.1 2.6 %collective-permute-start = (bf16[6,8192]{1,0:T(8,128)(2,1)S(1)}, bf16[6,8192]{1,0:T(8,128)(2,1)S(1)}, u32[]{:S(2)}, u32[]{:S(2)}) collective-permute-start(bf16[6,8192]{1,0:T(8,128)(2,1)S(1)} %broadcast_select_fusion.4), channel_id=1, source_target_pairs={{0,1},{1,0},{2,3},{3,2},{4,5},{5,4},{6,7},{7,6},{8,9},{9,8},{10,11... | collective-permute-start | bytes 294920 | tf_op jit(solution)/shard_map/ppermute | solution.py:190
  10.7 1.0 collective-permute-done
  11.7 0.9 broadcast_select_fusion.3
  12.6 0.1 pad_maximum_fusion.1
  12.7 10.6 %collective-permute-start.1 = (bf16[12,8192]{1,0:T(8,128)(2,1)S(1)}, bf16[12,8192]{1,0:T(8,128)(2,1)S(1)}, u32[]{:S(2)}, u32[]{:S(2)}) collective-permute-start(bf16[12,8192]{1,0:T(8,128)(2,1)S(1)} %pad_maximum_fusion.1), channel_id=1, source_target_pairs={{0,16},{1,17},{2,18},{3,19},{4,20},{5,21},{6,22},{7,23},{8,24},{9,... | collective-permute-start | bytes 589832 | tf_op jit(solution)/shard_map/ppermute | solution.py:191
  23.3 6.4 %collective-permute-done.1 = bf16[12,8192]{1,0:T(8,128)(2,1)S(1)} collective-permute-done((bf16[12,8192]{1,0:T(8,128)(2,1)S(1)}, bf16[12,8192]{1,0:T(8,128)(2,1)S(1)}, u32[]{:S(2)}, u32[]{:S(2)}) %collective-permute-start.1) | collective-permute-done | bytes 196640 | tf_op jit(solution)/shard_map/ppermute | solution.py:191
  29.7 0.1 broadcast_select_fusion.1
  29.9 0.3 broadcast_in_dim.30
  30.2 0.9 bitcast_dynamic-update-slice_fusion.6
  31.1 4.4 %collective-permute-start.2 = (bf16[24,8192]{1,0:T(8,128)(2,1)}, bf16[24,8192]{1,0:T(8,128)(2,1)}, u32[]{:S(2)}, u32[]{:S(2)}) collective-permute-start(bf16[24,8192]{1,0:T(8,128)(2,1)} %get-tuple-element.12), channel_id=1, source_target_pairs={{0,2},{1,3},{2,4},{3,5},{4,6},{5,7},{6,8},{7,9},{8,10},{9,11},{10,... | collective-permute-start | bytes 1179656 | tf_op jit(solution)/shard_map/ppermute | solution.py:202
  35.5 1.9 collective-permute-start.3
  37.4 3.1 %collective-permute-done.2 = bf16[24,8192]{1,0:T(8,128)(2,1)} collective-permute-done((bf16[24,8192]{1,0:T(8,128)(2,1)}, bf16[24,8192]{1,0:T(8,128)(2,1)}, u32[]{:S(2)}, u32[]{:S(2)}) %collective-permute-start.2) | collective-permute-done | bytes 393248 | tf_op jit(solution)/shard_map/ppermute | solution.py:202
  40.5 5.0 %collective-permute-start.4 = (bf16[24,8192]{1,0:T(8,128)(2,1)}, bf16[24,8192]{1,0:T(8,128)(2,1)S(1)}, u32[]{:S(2)}, u32[]{:S(2)}) collective-permute-start(bf16[24,8192]{1,0:T(8,128)(2,1)} %collective-permute-done.2), channel_id=1, source_target_pairs={{0,2},{1,3},{2,4},{3,5},{4,6},{5,7},{6,8},{7,9},{8,10},{9,11},{10,... | collective-permute-start | bytes 1179656 | tf_op jit(solution)/shard_map/ppermute | solution.py:202
  45.5 0.0 collective-permute-done.3
  45.5 1.9 collective-permute-start.5
  47.5 0.0 copy-start
  47.5 0.0 copy-start.2
  47.5 0.0 copy-start.3
  47.5 0.0 copy-start.4
  47.5 1.2 bitcast_dynamic-update-slice_fusion.5
  48.7 2.2 %collective-permute-done.4 = bf16[24,8192]{1,0:T(8,128)(2,1)S(1)} collective-permute-done((bf16[24,8192]{1,0:T(8,128)(2,1)}, bf16[24,8192]{1,0:T(8,128)(2,1)S(1)}, u32[]{:S(2)}, u32[]{:S(2)}) %collective-permute-start.4) | collective-permute-done | bytes 393248 | tf_op jit(solution)/shard_map/ppermute | solution.py:202
  50.9 4.9 %collective-permute-start.6 = (bf16[24,8192]{1,0:T(8,128)(2,1)S(1)}, bf16[24,8192]{1,0:T(8,128)(2,1)S(1)}, u32[]{:S(2)}, u32[]{:S(2)}) collective-permute-start(bf16[24,8192]{1,0:T(8,128)(2,1)S(1)} %collective-permute-done.4), channel_id=1, source_target_pairs={{0,2},{1,3},{2,4},{3,5},{4,6},{5,7},{6,8},{7,9},{8,10},{9,11},{10,... | collective-permute-start | bytes 1179656 | tf_op jit(solution)/shard_map/ppermute | solution.py:202
  55.8 0.3 collective-permute-done.5
  56.1 1.9 collective-permute-start.7
  58.1 4.2 %collective-permute-done.6 = bf16[24,8192]{1,0:T(8,128)(2,1)S(1)} collective-permute-done((bf16[24,8192]{1,0:T(8,128)(2,1)S(1)}, bf16[24,8192]{1,0:T(8,128)(2,1)S(1)}, u32[]{:S(2)}, u32[]{:S(2)}) %collective-permute-start.6) | collective-permute-done | bytes 393248 | tf_op jit(solution)/shard_map/ppermute | solution.py:202
  62.3 5.0 %collective-permute-start.8 = (bf16[24,4096]{1,0:T(8,128)(2,1)S(1)}, bf16[24,4096]{1,0:T(8,128)(2,1)S(1)}, u32[]{:S(2)}, u32[]{:S(2)}) collective-permute-start(bf16[24,4096]{1,0:T(8,128)(2,1)S(1)} %slice.18), channel_id=1, source_target_pairs={{0,2},{1,3},{2,4},{3,5},{4,6},{5,7},{6,8},{7,9},{8,10},{9,11},{10,... | collective-permute-start | bytes 589832 | tf_op jit(solution)/shard_map/ppermute | solution.py:206
  67.4 0.4 collective-permute-done.7
  67.8 1.9 collective-permute-start.9
  69.8 2.3 %collective-permute-done.8 = bf16[24,4096]{1,0:T(8,128)(2,1)S(1)} collective-permute-done((bf16[24,4096]{1,0:T(8,128)(2,1)S(1)}, bf16[24,4096]{1,0:T(8,128)(2,1)S(1)}, u32[]{:S(2)}, u32[]{:S(2)}) %collective-permute-start.8) | collective-permute-done | bytes 196640 | tf_op jit(solution)/shard_map/ppermute | solution.py:206
  72.1 5.7 %collective-permute-done.9 = bf16[24,4096]{1,0:T(8,128)(2,1)S(1)} collective-permute-done((bf16[24,4096]{1,0:T(8,128)(2,1)S(1)}, bf16[24,4096]{1,0:T(8,128)(2,1)S(1)}, u32[]{:S(2)}, u32[]{:S(2)}) %collective-permute-start.9) | collective-permute-done | bytes 196640 | tf_op jit(solution)/shard_map/ppermute | solution.py:207
  77.9 12.0 %collective-permute-start.10 = (bf16[192,8192]{1,0:T(8,128)(2,1)S(1)}, bf16[192,8192]{1,0:T(8,128)(2,1)S(1)}, u32[]{:S(2)}, u32[]{:S(2)}) collective-permute-start(bf16[192,8192]{1,0:T(8,128)(2,1)S(1)} %bitcast.26), channel_id=1, source_target_pairs={{0,1},{1,0},{2,3},{3,2},{4,5},{5,4},{6,7},{7,6},{8,9},{9,8},{10,11... | collective-permute-start | bytes 9437192 | tf_op jit(solution)/shard_map/ppermute | solution.py:250
  89.8 5.3 %collective-permute-done.10.other_ref = bf16[192,8192]{1,0:T(8,128)(2,1)S(1)} collective-permute-done((bf16[192,8192]{1,0:T(8,128)(2,1)S(1)}, bf16[192,8192]{1,0:T(8,128)(2,1)S(1)}, u32[]{:S(2)}, u32[]{:S(2)}) %collective-permute-start.10) | collective-permute-done | bytes 3145760 | tf_op jit(solution)/shard_map/ppermute | solution.py:250
  95.1 0.0 copy-done
  95.1 0.0 copy-done.2
  95.1 0.0 copy-done.3
  95.1 0.0 copy-done.4
  95.1 8.2 %weight_parts.1 = (bf16[4,2,7,8,32,128]{5,4,3,2,1,0:T(8,128)(2,1)S(1)}, bf16[7,192,128]{2,1,0:T(8,128)(2,1)S(1)}) custom-call(s32[1]{0:T(128)} %bitcast.core_ref, s32[7,8]{1,0:T(8,128)S(1)} %copy-done.3, s32[7,8]{1,0:T(8,128)S(1)} %copy-done.4, bf16[192,8192]{1,0:T(8,128)(2,1)S(1)} %bitcast.27, bf16[192,8192]{1,0:T(8,128)(2,1)S(1)} %collective-permute-done.10.other_ref, ...), custom_call_target="tpu_custom_call" | custom-call | flops 1409286144 | bytes 14680064 | tf_op jit(solution)/shard_map/weight_parts/pallas_call | solution.py:123
  103.3 0.0 copy-start.1
  103.3 1.8 copy-done.1
  105.1 4.0 %input_parts.1 = (bf16[192,4096]{1,0:T(8,128)(2,1)S(1)}, bf16[192,4096]{1,0:T(8,128)(2,1)S(1)}) custom-call(s32[1]{0:T(128)} %bitcast.core_ref, s32[7,8]{1,0:T(8,128)S(1)} %copy-done.3, bf16[7,192,128]{2,1,0:T(8,128)(2,1)S(1)} %get-tuple-element.7.pg_ref, bf16[7,8,128,128]{3,2,1,0:T(8,128)(2,1)S(1)} %copy-done), custom_call_target="tpu_custom_call" | custom-call | flops 352321536 | bytes 6291456 | tf_op jit(solution)/shard_map/input_parts/pallas_call | solution.py:158
  109.1 2.3 %collective-permute-start.11 = (bf16[192,4096]{1,0:T(8,128)(2,1)S(1)}, bf16[192,4096]{1,0:T(8,128)(2,1)}, u32[]{:S(2)}, u32[]{:S(2)}) collective-permute-start(bf16[192,4096]{1,0:T(8,128)(2,1)S(1)} %get-tuple-element.9), channel_id=1, source_target_pairs={{0,1},{1,0},{2,3},{3,2},{4,5},{5,4},{6,7},{7,6},{8,9},{9,8},{10,11... | collective-permute-start | bytes 4718600 | tf_op jit(solution)/shard_map/ppermute | solution.py:227
  111.4 4.8 %all-to-all-start = ((bf16[4,112,32,128]{3,2,1,0:T(8,128)(2,1)}), bf16[4,112,32,128]{3,2,1,0:T(8,128)(2,1)}, u32[]{:S(2)}, u32[]{:S(2)}) async-start(bf16[4,112,32,128]{3,2,1,0:T(8,128)(2,1)} %bitcast.28), calls=%async_computation.1 | async-start | bytes 7340032 | tf_op jit(solution)/shard_map/all_to_all | solution.py:216
  116.1 0.0 reduce-scatter.2.cloned.1.call-start
  116.2 0.0 collective-permute-done.11
  116.2 3.2 %add_convert_fusion = bf16[192,4096]{1,0:T(8,128)(2,1)} fusion(bf16[192,4096]{1,0:T(8,128)(2,1)} %collective-permute-done.11, bf16[192,4096]{1,0:T(8,128)(2,1)S(1)} %get-tuple-element.8), kind=kLoop, calls=%fused_computation | loop fusion | flops 3145728 | bytes 4718592 | tf_op jit(solution)/shard_map/convert_element_type | solution.py:184
  119.3 0.0 reduce-scatter.2.cloned.1.call-update
  119.4 40.0 %all-to-all-done = bf16[4,112,32,128]{3,2,1,0:T(8,128)(2,1)} async-done(((bf16[4,112,32,128]{3,2,1,0:T(8,128)(2,1)}), bf16[4,112,32,128]{3,2,1,0:T(8,128)(2,1)}, u32[]{:S(2)}, u32[]{:S(2)}) %all-to-all-start) | async-done | bytes 3670048 | tf_op jit(solution)/shard_map/all_to_all | solution.py:216
  159.4 3.2 %reduce_sum.24 = bf16[112,32,128]{2,1,0:T(8,128)(2,1)S(1)} reduce(bf16[4,112,32,128]{3,2,1,0:T(8,128)(2,1)} %all-to-all-done, bf16[]{:T(256)} %constant.13.clone.1), dimensions={0}, to_apply=%region_1.2 | reduce | flops 1376256 | bytes 4587522 | tf_op jit(solution)/shard_map/reduce_sum | solution.py:218
  162.6 1.1 copy.9
  163.7 7.0 %all-to-all-start.1 = ((bf16[4,112,8,128]{3,2,1,0:T(8,128)(2,1)}), bf16[4,112,8,128]{3,2,1,0:T(8,128)(2,1)S(1)}, u32[]{:S(2)}, u32[]{:S(2)}) async-start(bf16[4,112,8,128]{3,2,1,0:T(8,128)(2,1)} %copy.9), calls=%async_computation.2 | async-start | bytes 1835008 | tf_op jit(solution)/shard_map/all_to_all | solution.py:220
  170.6 0.0 reduce-scatter.2.cloned.1.call-done
  170.6 0.9 constant_dynamic-slice_fusion.1
  171.6 6.8 %collective-permute-start.12 = (bf16[12,4096]{1,0:T(8,128)(2,1)S(1)}, bf16[12,4096]{1,0:T(8,128)(2,1)S(1)}, u32[]{:S(2)}, u32[]{:S(2)}) collective-permute-start(bf16[12,4096]{1,0:T(8,128)(2,1)S(1)} %constant_dynamic-slice_fusion.1), channel_id=1, source_target_pairs={{0,16},{1,17},{2,18},{3,19},{4,20},{5,21},{6,22},{7,23},{8,24},{9,... | collective-permute-start | bytes 294920 | tf_op jit(solution)/shard_map/ppermute | solution.py:232
  178.4 20.3 %all-to-all-done.1 = bf16[4,112,8,128]{3,2,1,0:T(8,128)(2,1)S(1)} async-done(((bf16[4,112,8,128]{3,2,1,0:T(8,128)(2,1)}), bf16[4,112,8,128]{3,2,1,0:T(8,128)(2,1)S(1)}, u32[]{:S(2)}, u32[]{:S(2)}) %all-to-all-start.1) | async-done | bytes 917536 | tf_op jit(solution)/shard_map/all_to_all | solution.py:220
  198.7 0.2 reduce_sum.25
  198.9 0.0 collective-permute-done.12
  198.9 1.0 add_convert_fusion.1
  199.9 3.4 %collective-permute-start.13 = (bf16[6,4096]{1,0:T(8,128)(2,1)S(1)}, bf16[6,4096]{1,0:T(8,128)(2,1)S(1)}, u32[]{:S(2)}, u32[]{:S(2)}) collective-permute-start(bf16[6,4096]{1,0:T(8,128)(2,1)S(1)} %constant_dynamic-slice_fusion), channel_id=1, source_target_pairs={{0,1},{1,0},{2,3},{3,2},{4,5},{5,4},{6,7},{7,6},{8,9},{9,8},{10,11... | collective-permute-start | bytes 147464 | tf_op jit(solution)/shard_map/ppermute | solution.py:236
  203.3 0.7 fusion
  204.0 0.2 collective-permute-done.13
  204.2 0.1 broadcast_select_fusion.7
  204.2 0.7 pad_maximum_fusion.2
  (10 shorter events, 0.3 us)
Async XLA Ops:
  8.1 3.6 %collective-permute-start = (bf16[6,8192]{1,0:T(8,128)(2,1)S(1)}, bf16[6,8192]{1,0:T(8,128)(2,1)S(1)}, u32[]{:S(2)}, u32[]{:S(2)}) collective-permute-start(bf16[6,8192]{1,0:T(8,128)(2,1)S(1)} %broadcast_select_fusion.4), channel_id=1, source_target_pairs={{0,1},{1,0},{2,3},{3,2},{4,5},{5,4},{6,7},{7,6},{8,9},{9,8},{10,11... | collective-permute-start | bytes 294920 | tf_op jit(solution)/shard_map/ppermute | solution.py:190
  12.7 17.0 %collective-permute-start.1 = (bf16[12,8192]{1,0:T(8,128)(2,1)S(1)}, bf16[12,8192]{1,0:T(8,128)(2,1)S(1)}, u32[]{:S(2)}, u32[]{:S(2)}) collective-permute-start(bf16[12,8192]{1,0:T(8,128)(2,1)S(1)} %pad_maximum_fusion.1), channel_id=1, source_target_pairs={{0,16},{1,17},{2,18},{3,19},{4,20},{5,21},{6,22},{7,23},{8,24},{9,... | collective-permute-start | bytes 589832 | tf_op jit(solution)/shard_map/ppermute | solution.py:191
  31.1 9.4 %collective-permute-start.2 = (bf16[24,8192]{1,0:T(8,128)(2,1)}, bf16[24,8192]{1,0:T(8,128)(2,1)}, u32[]{:S(2)}, u32[]{:S(2)}) collective-permute-start(bf16[24,8192]{1,0:T(8,128)(2,1)} %get-tuple-element.12), channel_id=1, source_target_pairs={{0,2},{1,3},{2,4},{3,5},{4,6},{5,7},{6,8},{7,9},{8,10},{9,11},{10,... | collective-permute-start | bytes 1179656 | tf_op jit(solution)/shard_map/ppermute | solution.py:202
  35.5 10.0 %collective-permute-start.3 = (bf16[24,8192]{1,0:T(8,128)(2,1)}, bf16[24,8192]{1,0:T(8,128)(2,1)S(1)}, u32[]{:S(2)}, u32[]{:S(2)}) collective-permute-start(bf16[24,8192]{1,0:T(8,128)(2,1)} %get-tuple-element.12), channel_id=1, source_target_pairs={{0,14},{1,15},{2,0},{3,1},{4,2},{5,3},{6,4},{7,5},{8,6},{9,7},{10,... | collective-permute-start | bytes 1179656 | tf_op jit(solution)/shard_map/ppermute | solution.py:203
  40.5 10.4 %collective-permute-start.4 = (bf16[24,8192]{1,0:T(8,128)(2,1)}, bf16[24,8192]{1,0:T(8,128)(2,1)S(1)}, u32[]{:S(2)}, u32[]{:S(2)}) collective-permute-start(bf16[24,8192]{1,0:T(8,128)(2,1)} %collective-permute-done.2), channel_id=1, source_target_pairs={{0,2},{1,3},{2,4},{3,5},{4,6},{5,7},{6,8},{7,9},{8,10},{9,11},{10,... | collective-permute-start | bytes 1179656 | tf_op jit(solution)/shard_map/ppermute | solution.py:202
  45.5 10.6 %collective-permute-start.5 = (bf16[24,8192]{1,0:T(8,128)(2,1)S(1)}, bf16[24,8192]{1,0:T(8,128)(2,1)S(1)}, u32[]{:S(2)}, u32[]{:S(2)}) collective-permute-start(bf16[24,8192]{1,0:T(8,128)(2,1)S(1)} %collective-permute-done.3), channel_id=1, source_target_pairs={{0,14},{1,15},{2,0},{3,1},{4,2},{5,3},{6,4},{7,5},{8,6},{9,7},{10,... | collective-permute-start | bytes 1179656 | tf_op jit(solution)/shard_map/ppermute | solution.py:203
  47.5 47.6 %copy-start = (bf16[7,8,128,128]{3,2,1,0:T(8,128)(2,1)S(1)}, bf16[7,8,128,128]{3,2,1,0:T(8,128)(2,1)}, u32[]{:S(2)}) copy-start(bf16[7,8,128,128]{3,2,1,0:T(8,128)(2,1)} %up_ref.3) | copy-start | bytes 5505028
  47.5 47.6 %copy-start.2 = (bf16[7,8,128,128]{3,2,1,0:T(8,128)(2,1)S(1)}, bf16[7,8,128,128]{3,2,1,0:T(8,128)(2,1)}, u32[]{:S(2)}) copy-start(bf16[7,8,128,128]{3,2,1,0:T(8,128)(2,1)} %down_ref.1) | copy-start | bytes 5505028
  47.5 47.6 %copy-start.3 = (s32[7,8]{1,0:T(8,128)S(1)}, s32[7,8]{1,0:T(8,128)}, u32[]{:S(2)}) copy-start(s32[7,8]{1,0:T(8,128)} %upi_ref.3) | copy-start | bytes 676
  47.5 47.6 %copy-start.4 = (s32[7,8]{1,0:T(8,128)S(1)}, s32[7,8]{1,0:T(8,128)}, u32[]{:S(2)}) copy-start(s32[7,8]{1,0:T(8,128)} %downi_ref.1) | copy-start | bytes 676
  50.9 11.4 %collective-permute-start.6 = (bf16[24,8192]{1,0:T(8,128)(2,1)S(1)}, bf16[24,8192]{1,0:T(8,128)(2,1)S(1)}, u32[]{:S(2)}, u32[]{:S(2)}) collective-permute-start(bf16[24,8192]{1,0:T(8,128)(2,1)S(1)} %collective-permute-done.4), channel_id=1, source_target_pairs={{0,2},{1,3},{2,4},{3,5},{4,6},{5,7},{6,8},{7,9},{8,10},{9,11},{10,... | collective-permute-start | bytes 1179656 | tf_op jit(solution)/shard_map/ppermute | solution.py:202
  56.1 11.7 %collective-permute-start.7 = (bf16[24,8192]{1,0:T(8,128)(2,1)S(1)}, bf16[24,8192]{1,0:T(8,128)(2,1)S(1)}, u32[]{:S(2)}, u32[]{:S(2)}) collective-permute-start(bf16[24,8192]{1,0:T(8,128)(2,1)S(1)} %collective-permute-done.5), channel_id=1, source_target_pairs={{0,14},{1,15},{2,0},{3,1},{4,2},{5,3},{6,4},{7,5},{8,6},{9,7},{10,... | collective-permute-start | bytes 1179656 | tf_op jit(solution)/shard_map/ppermute | solution.py:203
  62.3 9.8 %collective-permute-start.8 = (bf16[24,4096]{1,0:T(8,128)(2,1)S(1)}, bf16[24,4096]{1,0:T(8,128)(2,1)S(1)}, u32[]{:S(2)}, u32[]{:S(2)}) collective-permute-start(bf16[24,4096]{1,0:T(8,128)(2,1)S(1)} %slice.18), channel_id=1, source_target_pairs={{0,2},{1,3},{2,4},{3,5},{4,6},{5,7},{6,8},{7,9},{8,10},{9,11},{10,... | collective-permute-start | bytes 589832 | tf_op jit(solution)/shard_map/ppermute | solution.py:206
  67.8 10.0 %collective-permute-start.9 = (bf16[24,4096]{1,0:T(8,128)(2,1)S(1)}, bf16[24,4096]{1,0:T(8,128)(2,1)S(1)}, u32[]{:S(2)}, u32[]{:S(2)}) collective-permute-start(bf16[24,4096]{1,0:T(8,128)(2,1)S(1)} %slice.19), channel_id=1, source_target_pairs={{0,14},{1,15},{2,0},{3,1},{4,2},{5,3},{6,4},{7,5},{8,6},{9,7},{10,... | collective-permute-start | bytes 589832 | tf_op jit(solution)/shard_map/ppermute | solution.py:207
  77.9 17.2 %collective-permute-start.10 = (bf16[192,8192]{1,0:T(8,128)(2,1)S(1)}, bf16[192,8192]{1,0:T(8,128)(2,1)S(1)}, u32[]{:S(2)}, u32[]{:S(2)}) collective-permute-start(bf16[192,8192]{1,0:T(8,128)(2,1)S(1)} %bitcast.26), channel_id=1, source_target_pairs={{0,1},{1,0},{2,3},{3,2},{4,5},{5,4},{6,7},{7,6},{8,9},{9,8},{10,11... | collective-permute-start | bytes 9437192 | tf_op jit(solution)/shard_map/ppermute | solution.py:250
  103.3 1.8 copy-start.1
  109.1 7.1 %collective-permute-start.11 = (bf16[192,4096]{1,0:T(8,128)(2,1)S(1)}, bf16[192,4096]{1,0:T(8,128)(2,1)}, u32[]{:S(2)}, u32[]{:S(2)}) collective-permute-start(bf16[192,4096]{1,0:T(8,128)(2,1)S(1)} %get-tuple-element.9), channel_id=1, source_target_pairs={{0,1},{1,0},{2,3},{3,2},{4,5},{5,4},{6,7},{7,6},{8,9},{9,8},{10,11... | collective-permute-start | bytes 4718600 | tf_op jit(solution)/shard_map/ppermute | solution.py:227
  111.4 48.0 %all-to-all-start = ((bf16[4,112,32,128]{3,2,1,0:T(8,128)(2,1)}), bf16[4,112,32,128]{3,2,1,0:T(8,128)(2,1)}, u32[]{:S(2)}, u32[]{:S(2)}) async-start(bf16[4,112,32,128]{3,2,1,0:T(8,128)(2,1)} %bitcast.28), calls=%async_computation.1 | async-start | bytes 7340032 | tf_op jit(solution)/shard_map/all_to_all | solution.py:216
  116.1 54.5 %reduce-scatter.2.cloned.1.call-start = ((), (), s32[]{:S(2)}) async-start(), calls=%async_computation.3 | async-start | bytes 1769472 | tf_op jit(solution)/shard_map/reduce_scatter | solution.py:228
  163.7 35.0 %all-to-all-start.1 = ((bf16[4,112,8,128]{3,2,1,0:T(8,128)(2,1)}), bf16[4,112,8,128]{3,2,1,0:T(8,128)(2,1)S(1)}, u32[]{:S(2)}, u32[]{:S(2)}) async-start(bf16[4,112,8,128]{3,2,1,0:T(8,128)(2,1)} %copy.9), calls=%async_computation.2 | async-start | bytes 1835008 | tf_op jit(solution)/shard_map/all_to_all | solution.py:220
  171.6 27.3 %collective-permute-start.12 = (bf16[12,4096]{1,0:T(8,128)(2,1)S(1)}, bf16[12,4096]{1,0:T(8,128)(2,1)S(1)}, u32[]{:S(2)}, u32[]{:S(2)}) collective-permute-start(bf16[12,4096]{1,0:T(8,128)(2,1)S(1)} %constant_dynamic-slice_fusion.1), channel_id=1, source_target_pairs={{0,16},{1,17},{2,18},{3,19},{4,20},{5,21},{6,22},{7,23},{8,24},{9,... | collective-permute-start | bytes 294920 | tf_op jit(solution)/shard_map/ppermute | solution.py:232
  199.9 4.3 %collective-permute-start.13 = (bf16[6,4096]{1,0:T(8,128)(2,1)S(1)}, bf16[6,4096]{1,0:T(8,128)(2,1)S(1)}, u32[]{:S(2)}, u32[]{:S(2)}) collective-permute-start(bf16[6,4096]{1,0:T(8,128)(2,1)S(1)} %constant_dynamic-slice_fusion), channel_id=1, source_target_pairs={{0,1},{1,0},{2,3},{3,2},{4,5},{5,4},{6,7},{7,6},{8,9},{9,8},{10,11... | collective-permute-start | bytes 147464 | tf_op jit(solution)/shard_map/ppermute | solution.py:236
Sparse Core Ops, SparseCore 0:
  119.8 40.5 reduce-scatter.1

commit v2 on v0

v2 whole, which is shorter than its diff:
```python
import functools
import math

import jax
import jax.numpy as jnp
from jax import lax
from jax.experimental import pallas as pl
from jax.experimental.pallas import tpu as pltpu
from jax.sharding import PartitionSpec as P

Z_HI, Y, CORE = 2, 8, 2
X, Z_LO = 4, 4


def tensor_id(zh, y, c):
    return (zh * Y + y) * CORE + c


def tensor_pairs(move):
    return [
        (tensor_id(zh, y, c), tensor_id(*move(zh, y, c)))
        for zh in range(Z_HI)
        for y in range(Y)
        for c in range(CORE)
    ]


SIBLING = tensor_pairs(lambda zh, y, c: (zh, y, 1 - c))
Z_PARTNER = tensor_pairs(lambda zh, y, c: (1 - zh, y, c))
Y_UP = tensor_pairs(lambda zh, y, c: (zh, (y + 1) % Y, c))
Y_DOWN = tensor_pairs(lambda zh, y, c: (zh, (y - 1) % Y, c))
ROW_GROUPS = [[tensor_id(zh, y, c) for zh in range(Z_HI) for y in range(Y)] for c in range(CORE)]


def seq_pairs(dx, dz):
    return [(x * Z_LO + z, (x ^ dx) * Z_LO + (z ^ dz)) for x in range(X) for z in range(Z_LO)]


X_EVEN = seq_pairs(1, 0)
X_ODD = seq_pairs(3, 0)
Z_TRADE = [seq_pairs(0, r) for r in range(Z_LO)]

NT = (((1,), (1,)), ((), ()))


def columns(rows, index_ref, j, k, block):
    side_by_side = []
    for slot in (k, k + 1):
        at = pl.multiple_of(index_ref[j, slot] * block, block)
        side_by_side.append(rows[:, pl.ds(at, block)])
    return jnp.concatenate(side_by_side, axis=1)


def block_kernel(factor, place_ref, upi_ref, downi_ref, mine_hbm, other_hbm, up_hbm, down_hbm,
                 send_ref, keep_ref, up0, up1, up2, up3, down0, down1, down2, down3,
                 parts_ref, inputs, grads, acc_ref, up_ref, down_ref, pg_ref, act_ref, us_ref, ds_ref, sems, out_sem):
    hidden, slots, block, _ = up_ref.shape
    pieces, rows, quarter = keep_ref.shape
    share = up0.shape[2]
    outs = (up0, up1, up2, up3, down0, down1, down2, down3)

    def load_rows(first, second):
        pltpu.make_async_copy(first, inputs, sems.at[2, 0]).start()
        pltpu.make_async_copy(second, grads, sems.at[2, 1]).start()

    @pl.when(place_ref[0] == 0)
    def _():
        load_rows(mine_hbm, other_hbm)

    @pl.when(place_ref[0] != 0)
    def _():
        load_rows(other_hbm, mine_hbm)

    loads = []
    for j in range(hidden):
        for at, (far, near) in enumerate(((up_hbm, up_ref), (down_hbm, down_ref))):
            loads.append(pltpu.make_async_copy(far.at[j], near.at[j], sems.at[at, j]))
            loads[-1].start()
    acc_ref[...] = jnp.zeros_like(acc_ref)
    pltpu.make_async_copy(mine_hbm, inputs, sems.at[2, 0]).wait()
    pltpu.make_async_copy(other_hbm, grads, sems.at[2, 1]).wait()

    for j in range(hidden):
        loads[2 * j].wait()
        loads[2 * j + 1].wait()
        preact = hidden_grad = 0.0
        for k in range(0, slots, 2):
            weights = up_ref[j, k:k + 2].reshape(2 * block, block)
            preact = preact + jnp.dot(columns(inputs, upi_ref, j, k, block), weights,
                                      preferred_element_type=jnp.float32)
            weights = jnp.concatenate([down_ref[j, k], down_ref[j, k + 1]], axis=1)
            hidden_grad = hidden_grad + lax.dot_general(
                columns(grads, downi_ref, j, k, block), weights, NT, preferred_element_type=jnp.float32)
        gating = jax.nn.sigmoid(preact)
        act_ref[j] = (preact * gating).astype(jnp.bfloat16).T
        pg = (hidden_grad * gating * (1.0 + preact * (1.0 - gating))).astype(jnp.bfloat16)
        pg_ref[j] = pg.T
        for k in range(0, slots, 2):
            terms = lax.dot_general(pg, up_ref[j, k:k + 2].reshape(2 * block, block), NT,
                                    preferred_element_type=jnp.float32)
            for slot in (k, k + 1):
                at = pl.multiple_of(upi_ref[j, slot] * block, block)
                acc_ref[:, pl.ds(at, block)] += terms[:, (slot - k) * block:(slot - k + 1) * block]

    @pl.loop(0, hidden)
    def _(j):
        pg = pg_ref[j]
        act = act_ref[j]
        for k in range(0, slots, 2):
            sums = jnp.dot(pg, columns(inputs, upi_ref, j, k, block), preferred_element_type=jnp.float32)
            sums = sums * factor
            for slot in (k, k + 1):
                us_ref[slot] = sums[:, (slot - k) * block:(slot - k + 1) * block].T
            sums = jnp.dot(act, columns(grads, downi_ref, j, k, block), preferred_element_type=jnp.float32)
            sums = sums * factor
            for slot in (k, k + 1):
                ds_ref[slot] = sums[:, (slot - k) * block:(slot - k + 1) * block]
        for q in range(X):
            row = pl.multiple_of((place_ref[1] ^ q) * share, share)
            parts_ref[q, j] = us_ref[:, pl.ds(row, share), :].astype(jnp.bfloat16)
            parts_ref[X + q, j] = ds_ref[:, pl.ds(row, share), :].astype(jnp.bfloat16)

    stores = [pltpu.make_async_copy(parts_ref.at[n], out, out_sem.at[n]) for n, out in enumerate(outs)]
    for store in stores:
        store.start()

    z_hi = place_ref[4]
    for out, core in ((send_ref, 1 - place_ref[0]), (keep_ref, place_ref[0])):
        left = pl.multiple_of(core * 2 * quarter, quarter)
        right = pl.multiple_of(core * 2 * quarter + quarter, quarter)
        for k in range(Y):
            owner = (place_ref[3] - k) & (Y - 1)
            here = slice(k * rows, (k + 1) * rows)
            a = acc_ref[here, pl.ds(left, quarter)]
            b = acc_ref[here, pl.ds(right, quarter)]
            half = rows // 2
            out[z_hi * Y + owner] = jnp.concatenate([a[:half], b[:half]], axis=0).astype(jnp.bfloat16)
            out[(1 - z_hi) * Y + owner] = jnp.concatenate([a[half:], b[half:]], axis=0).astype(jnp.bfloat16)
    for store in stores:
        store.wait()


def x_sum_kernel(place_ref, up_own, up_a, up_b, down_own, down_a, down_b, *refs):
    outs, sum_ref = refs[:Z_LO], refs[Z_LO]
    _, slots, share, block = up_own.shape
    rows = share // Z_LO
    for kind, parts in enumerate(((up_own, up_a, up_b), (down_own, down_a, down_b))):
        total = sum(part[0].astype(jnp.float32) for part in parts)
        sum_ref[kind] = total.reshape(slots * share, block)
        for r, out in enumerate(outs):
            row = pl.multiple_of((place_ref[2] ^ r) * rows, rows)
            piece = [sum_ref[kind, pl.ds(k * share + row, rows), :] for k in range(slots)]
            out[kind, 0] = jnp.concatenate(piece, axis=0).astype(jnp.bfloat16)


def add_kernel(a_ref, b_ref, out_ref):
    out_ref[...] = (a_ref[...].astype(jnp.float32) + b_ref[...].astype(jnp.float32)).astype(jnp.bfloat16)


def total_kernel(parts_ref, out_ref):
    total = sum(parts_ref[n].astype(jnp.float32) for n in range(parts_ref.shape[0]))
    out_ref[...] = total.astype(jnp.bfloat16)


SMEM = pl.BlockSpec(memory_space=pltpu.SMEM)
VMEM = pl.BlockSpec(memory_space=pltpu.VMEM)
HBM = pl.BlockSpec(memory_space=pltpu.HBM)


def block_parts(factor, place, up_index, down_index, mine, other, up_blocks, down_blocks):
    hidden, slots, block, _ = up_blocks.shape
    rows, features = mine.shape
    flops = 5 * 2 * rows * hidden * slots * block * block
    terms = jax.ShapeDtypeStruct((Z_HI * Y, rows // Y, features // 4), jnp.bfloat16)
    part = jax.ShapeDtypeStruct((hidden, slots, block // X, block), jnp.bfloat16)
    return pl.pallas_call(
        functools.partial(block_kernel, factor),
        in_specs=[SMEM] * 3 + [pl.BlockSpec(memory_space=pl.ANY)] * 2 + [HBM] * 2,
        out_specs=[VMEM] * 2 + [HBM] * 8,
        out_shape=[terms] * 2 + [part] * 8,
        scratch_shapes=[
            pltpu.VMEM((2 * X,) + part.shape, jnp.bfloat16),
            pltpu.VMEM((rows, features), jnp.bfloat16),
            pltpu.VMEM((rows, features), jnp.bfloat16),
            pltpu.VMEM((rows, features), jnp.float32),
            pltpu.VMEM(up_blocks.shape, jnp.bfloat16),
            pltpu.VMEM(down_blocks.shape, jnp.bfloat16),
            pltpu.VMEM((hidden, block, rows), jnp.bfloat16),
            pltpu.VMEM((hidden, block, rows), jnp.bfloat16),
            pltpu.VMEM((slots, block, block), jnp.float32),
            pltpu.VMEM((slots, block, block), jnp.float32),
            pltpu.SemaphoreType.DMA((3, hidden)),
            pltpu.SemaphoreType.DMA((2 * X,)),
        ],
        compiler_params=pltpu.CompilerParams(vmem_limit_bytes=52 * 2**20),
        cost_estimate=pl.CostEstimate(flops=flops, bytes_accessed=16 * 2**20, transcendentals=0),
        name="block_parts",
    )(place, up_index, down_index, mine, other, up_blocks, down_blocks)


def x_sum(place, *parts):
    hidden, slots, share, block = parts[0].shape
    rows = slots * share // Z_LO
    part = pl.BlockSpec((1, slots, share, block), lambda j, *_: (j, 0, 0, 0))
    return pl.pallas_call(
        x_sum_kernel,
        grid_spec=pltpu.PrefetchScalarGridSpec(
            num_scalar_prefetch=1,
            grid=(hidden,),
            in_specs=[part] * 6,
            out_specs=[pl.BlockSpec((2, 1, rows, block), lambda j, *_: (0, j, 0, 0))] * Z_LO,
            scratch_shapes=[pltpu.VMEM((2, slots * share, block), jnp.float32)],
        ),
        out_shape=[jax.ShapeDtypeStruct((2, hidden, rows, block), jnp.bfloat16)] * Z_LO,
        compiler_params=pltpu.CompilerParams(vmem_limit_bytes=8 * 2**20),
        cost_estimate=pl.CostEstimate(flops=2**21, bytes_accessed=4 * 2**20, transcendentals=0),
        name="x_sum",
    )(place, *parts)


def cost(microseconds):
    return pl.CostEstimate(flops=microseconds * 10**9, bytes_accessed=2**20, transcendentals=0)


SMALL = pltpu.CompilerParams(vmem_limit_bytes=6 * 2**20)


def add_terms(a, b, microseconds, name):
    half = a.shape[0] // 2 if a.shape[0] % 2 == 0 else a.shape[0]
    spec = pl.BlockSpec((half,) + a.shape[1:], lambda i: (i,) + (0,) * (a.ndim - 1))
    return pl.pallas_call(
        add_kernel, grid=(a.shape[0] // half,), in_specs=[spec] * 2, out_specs=spec,
        out_shape=jax.ShapeDtypeStruct(a.shape, jnp.bfloat16), cost_estimate=cost(microseconds), name=name,
        compiler_params=SMALL,
    )(a, b)


def total_terms(parts):
    pieces, rows, width = parts.shape
    share = width // 4
    return pl.pallas_call(
        total_kernel, grid=(4,),
        in_specs=[pl.BlockSpec((pieces, rows, share), lambda i: (0, 0, i))],
        out_specs=pl.BlockSpec((rows, share), lambda i: (0, i)),
        out_shape=jax.ShapeDtypeStruct((rows, width), jnp.bfloat16), cost_estimate=cost(30), name="total_terms", compiler_params=SMALL,
    )(parts)


def in_order(first_is_mine, mine, other):
    a = jnp.where(first_is_mine, mine, other)
    b = jnp.where(first_is_mine, other, mine)
    return jnp.concatenate([a, b], axis=0)


def gather_rows(inputs, grad_out, core, zero):
    send = jnp.where(core == 0, grad_out, inputs)
    keep = jnp.where(core == 0, inputs, grad_out)
    pair = in_order(core == 0, keep, lax.ppermute(send, "tensor", SIBLING))
    rows, features = pair.shape
    half = features // 2
    pair = jnp.concatenate([pair[:, :half], pair[:, half:]], axis=0)
    other = lax.ppermute(pair, "tensor", Z_PARTNER)
    left = jnp.concatenate([pair[:rows], other[:rows]], axis=0)
    right = jnp.concatenate([pair[rows:], other[rows:]], axis=0)
    chunk = jnp.concatenate([left, right], axis=1)
    whole = jnp.zeros((Y, 2 * rows, features), chunk.dtype)

    def place(whole, piece, at, column=0):
        return lax.dynamic_update_slice(whole, piece[None], (zero + at, 0, column))

    whole = place(whole, chunk, 0)
    up = down = chunk
    for step in range(1, Y // 2):
        up = lax.ppermute(up, "tensor", Y_UP)
        down = lax.ppermute(down, "tensor", Y_DOWN)
        whole = place(place(whole, up, step), down, Y - step)
    whole = place(whole, lax.ppermute(up[:, :half], "tensor", Y_UP), Y // 2)
    whole = place(whole, lax.ppermute(down[:, half:], "tensor", Y_DOWN), Y // 2, half)
    return whole.reshape(-1, features)


def reduce_weights_x(place, up, down):
    far_up = lax.ppermute(up[2], "seq", X_EVEN)
    far_down = lax.ppermute(down[2], "seq", X_ODD)
    up_a = lax.ppermute(up[1], "seq", X_EVEN)
    down_b = lax.ppermute(down[3], "seq", X_ODD)
    up_b = lax.ppermute(add_terms(up[3], far_up, 20, "add_up"), "seq", X_ODD)
    down_a = lax.ppermute(add_terms(down[1], far_down, 20, "add_down"), "seq", X_EVEN)
    return x_sum(place, up[0], up_a, up_b, down[0], down_a, down_b)


def reduce_inputs(keep, send):
    part = add_terms(keep, lax.ppermute(send, "tensor", SIBLING), 15, "add_cores")
    return lax.all_to_all(part, "tensor", 0, 0, axis_index_groups=ROW_GROUPS, tiled=True)


def own_rows(part, core):
    part = total_terms(part)
    rows = part.shape[0] // 4
    pair = jnp.concatenate([part[:2 * rows], part[2 * rows:]], axis=1)
    mine = jnp.where(core == 0, pair[:rows], pair[rows:])
    other = lax.ppermute(jnp.where(core == 0, pair[rows:], pair[:rows]), "tensor", SIBLING)
    left = jnp.where(core == 0, mine, other)
    right = jnp.where(core == 0, other, mine)
    return jnp.concatenate([left, right], axis=1)


def local(inputs, grad_out, up_blocks, up_index, down_blocks, down_index):
    t = lax.axis_index("tensor")
    core = t & (CORE - 1)
    z_hi = t >> 4
    rows_here, _ = inputs.shape
    factor = 1.0 / math.sqrt(rows_here * lax.axis_size("tensor") * lax.axis_size("seq"))
    mine = gather_rows(inputs, grad_out, core, t >> 5)
    other = lax.ppermute(mine, "tensor", SIBLING)
    seq = lax.axis_index("seq")
    y = (t >> 1) & (Y - 1)
    place = jnp.stack([core, seq >> 2, seq & (Z_LO - 1), y, z_hi]).astype(jnp.int32)
    send, keep, *parts = block_parts(factor, place, up_index, down_index, mine, other, up_blocks, down_blocks)
    hidden, slots, block, _ = up_blocks.shape
    shape = (hidden, slots, block // (X * Z_LO), block)
    input_terms = reduce_inputs(keep, send)
    pieces = reduce_weights_x(place, parts[:4], parts[4:])
    first = pieces[0]
    input_terms, first = lax.optimization_barrier((input_terms, first))
    grad_in = own_rows(input_terms, core)
    pieces = [first] + [lax.ppermute(pieces[r], "seq", Z_TRADE[r]) for r in (2, 3, 1)]
    total = sum(piece.astype(jnp.float32) for piece in pieces).astype(jnp.bfloat16)
    grad_up, grad_down = total[0].reshape(shape), total[1].reshape(shape)
    return (grad_in, grad_up, grad_down)


def solution(mesh):
    return jax.shard_map(
        local,
        mesh=mesh,
        in_specs=(
            P(("seq", "tensor"), None),
            P(("seq", "tensor"), None),
            P("tensor", None, None, None),
            P("tensor", None),
            P("tensor", None, None, None),
            P("tensor", None),
        ),
        out_specs=(
            P(("seq", "tensor"), None),
            P("tensor", None, "seq", None),
            P("tensor", None, "seq", None),
        ),
        check_vma=False,
    )
```

time: 502 us -> 197 us (0.39)
  the two profiles are of different devices: /device:TPU:30 before, /device:TPU:169 now
where the time goes in v2:
time: 197 us; the launch traced here: 196 us
  starting transfers between devices  91.2 us (46%)
  waiting for transfers between devices  64.2 us (33%)
  Pallas kernels  23.7 us (12%)
  local copies, waits for them, and re-layouts  12.2 us (6%)
  other arithmetic  3.79 us (2%)
    pallas_call x1, Pallas kernels, block_parts(): pl.pallas_call(functools.partial(block_kernel, factor), in_specs=[SMEM] *...  16.1 us
    ppermute x3, waiting for transfers between devices, gather_rows(): up = lax.ppermute(up, 'tensor', Y_UP)  14.8 us
    all_to_all x1, starting transfers between devices, reduce_inputs(): lax.all_to_all(part, 'tensor', 0, 0, axis_index_groups=ROW_GROUPS, tiled=...  14.4 us
    ppermute x3, waiting for transfers between devices, local(): lax.ppermute(pieces[r], 'seq', Z_TRADE[r])  14.3 us
    ppermute x3, starting transfers between devices, gather_rows(): down = lax.ppermute(down, 'tensor', Y_DOWN)  11.1 us
    ppermute x1, waiting for transfers between devices, gather_rows(): other = lax.ppermute(pair, 'tensor', Z_PARTNER)  9.58 us
    ppermute x3, starting transfers between devices, local(): lax.ppermute(pieces[r], 'seq', Z_TRADE[r])  9.26 us
    ppermute x1, starting transfers between devices, gather_rows(): other = lax.ppermute(pair, 'tensor', Z_PARTNER)  8.84 us
  transfers between devices with their start and end apart: 23, of which 12 were waited for; matrix products, arithmetic and copies ran while one was open for 3% of the time, Pallas kernels for 4%

profile of v2, /device:TPU:169, one launch (start us, length us, event | category | flops | bytes accessed | tf_op | source)
XLA Modules:
  0.0 196.1 jit_solution(14510069896800473817)
XLA Ops:
  0.6 0.9 broadcast_select_fusion.2
  1.6 2.6 %collective-permute-start = (bf16[6,8192]{1,0:T(8,128)(2,1)S(1)}, bf16[6,8192]{1,0:T(8,128)(2,1)S(1)}, u32[]{:S(2)}, u32[]{:S(2)}) collective-permute-start(bf16[6,8192]{1,0:T(8,128)(2,1)S(1)} %broadcast_select_fusion.2), channel_id=1, source_target_pairs={{0,1},{1,0},{2,3},{3,2},{4,5},{5,4},{6,7},{7,6},{8,9},{9,8},{10,11... | collective-permute-start | bytes 294920 | tf_op jit(solution)/shard_map/ppermute | solution.py:258
  4.2 1.0 collective-permute-done
  5.1 0.9 broadcast_select_fusion.1
  6.1 0.1 fusion
  6.2 0.1 pad_maximum_fusion
  6.2 8.8 %collective-permute-start.1 = (bf16[24,4096]{1,0:T(8,128)(2,1)S(1)}, bf16[24,4096]{1,0:T(8,128)(2,1)S(1)}, u32[]{:S(2)}, u32[]{:S(2)}) collective-permute-start(bf16[24,4096]{1,0:T(8,128)(2,1)S(1)} %pad_maximum_fusion), channel_id=1, source_target_pairs={{0,16},{1,17},{2,18},{3,19},{4,20},{5,21},{6,22},{7,23},{8,24},{9,... | collective-permute-start | bytes 589832 | tf_op jit(solution)/shard_map/ppermute | solution.py:262
  15.1 9.6 %collective-permute-done.1 = bf16[24,4096]{1,0:T(8,128)(2,1)S(1)} collective-permute-done((bf16[24,4096]{1,0:T(8,128)(2,1)S(1)}, bf16[24,4096]{1,0:T(8,128)(2,1)S(1)}, u32[]{:S(2)}, u32[]{:S(2)}) %collective-permute-start.1) | collective-permute-done | bytes 196640 | tf_op jit(solution)/shard_map/ppermute | solution.py:262
  24.7 2.0 %broadcast_in_dim.30 = bf16[8,24,8192]{2,1,0:T(8,128)(2,1)} broadcast(bf16[]{:T(256)} %constant.33.clone.1), dimensions={} | broadcast | bytes 3145730 | tf_op jit(solution)/shard_map/broadcast_in_dim | solution.py:266
  26.7 0.9 bitcast_dynamic-update-slice_fusion.6
  27.6 2.3 %collective-permute-start.2 = (bf16[24,8192]{1,0:T(8,128)(2,1)S(1)}, bf16[24,8192]{1,0:T(8,128)(2,1)S(1)}, u32[]{:S(2)}, u32[]{:S(2)}) collective-permute-start(bf16[24,8192]{1,0:T(8,128)(2,1)S(1)} %get-tuple-element.36), channel_id=1, source_target_pairs={{0,2},{1,3},{2,4},{3,5},{4,6},{5,7},{6,8},{7,9},{8,10},{9,11},{10,... | collective-permute-start | bytes 1179656 | tf_op jit(solution)/shard_map/ppermute | solution.py:274
  29.9 3.0 %collective-permute-start.3 = (bf16[24,8192]{1,0:T(8,128)(2,1)S(1)}, bf16[24,8192]{1,0:T(8,128)(2,1)S(1)}, u32[]{:S(2)}, u32[]{:S(2)}) collective-permute-start(bf16[24,8192]{1,0:T(8,128)(2,1)S(1)} %get-tuple-element.36), channel_id=1, source_target_pairs={{0,14},{1,15},{2,0},{3,1},{4,2},{5,3},{6,4},{7,5},{8,6},{9,7},{10,... | collective-permute-start | bytes 1179656 | tf_op jit(solution)/shard_map/ppermute | solution.py:275
  32.9 6.7 %collective-permute-done.2 = bf16[24,8192]{1,0:T(8,128)(2,1)S(1)} collective-permute-done((bf16[24,8192]{1,0:T(8,128)(2,1)S(1)}, bf16[24,8192]{1,0:T(8,128)(2,1)S(1)}, u32[]{:S(2)}, u32[]{:S(2)}) %collective-permute-start.2) | collective-permute-done | bytes 393248 | tf_op jit(solution)/shard_map/ppermute | solution.py:274
  39.6 2.3 %collective-permute-start.4 = (bf16[24,8192]{1,0:T(8,128)(2,1)S(1)}, bf16[24,8192]{1,0:T(8,128)(2,1)S(1)}, u32[]{:S(2)}, u32[]{:S(2)}) collective-permute-start(bf16[24,8192]{1,0:T(8,128)(2,1)S(1)} %collective-permute-done.2), channel_id=1, source_target_pairs={{0,2},{1,3},{2,4},{3,5},{4,6},{5,7},{6,8},{7,9},{8,10},{9,11},{10,... | collective-permute-start | bytes 1179656 | tf_op jit(solution)/shard_map/ppermute | solution.py:274
  41.9 3.8 %collective-permute-start.5 = (bf16[24,8192]{1,0:T(8,128)(2,1)S(1)}, bf16[24,8192]{1,0:T(8,128)(2,1)S(1)}, u32[]{:S(2)}, u32[]{:S(2)}) collective-permute-start(bf16[24,8192]{1,0:T(8,128)(2,1)S(1)} %collective-permute-done.3), channel_id=1, source_target_pairs={{0,14},{1,15},{2,0},{3,1},{4,2},{5,3},{6,4},{7,5},{8,6},{9,7},{10,... | collective-permute-start | bytes 1179656 | tf_op jit(solution)/shard_map/ppermute | solution.py:275
  45.7 0.0 copy-start.1
  45.7 0.0 copy-start.2
  45.8 0.8 bitcast_dynamic-update-slice_fusion.5
  46.5 0.8 bitcast_dynamic-update-slice_fusion.4
  47.3 4.5 %collective-permute-done.4 = bf16[24,8192]{1,0:T(8,128)(2,1)S(1)} collective-permute-done((bf16[24,8192]{1,0:T(8,128)(2,1)S(1)}, bf16[24,8192]{1,0:T(8,128)(2,1)S(1)}, u32[]{:S(2)}, u32[]{:S(2)}) %collective-permute-start.4) | collective-permute-done | bytes 393248 | tf_op jit(solution)/shard_map/ppermute | solution.py:274
  51.8 1.9 collective-permute-start.6
  53.7 4.3 %collective-permute-start.7 = (bf16[24,8192]{1,0:T(8,128)(2,1)S(1)}, bf16[24,8192]{1,0:T(8,128)(2,1)S(1)}, u32[]{:S(2)}, u32[]{:S(2)}) collective-permute-start(bf16[24,8192]{1,0:T(8,128)(2,1)S(1)} %collective-permute-done.5), channel_id=1, source_target_pairs={{0,14},{1,15},{2,0},{3,1},{4,2},{5,3},{6,4},{7,5},{8,6},{9,7},{10,... | collective-permute-start | bytes 1179656 | tf_op jit(solution)/shard_map/ppermute | solution.py:275
  58.0 0.8 bitcast_dynamic-update-slice_fusion.3
  58.8 0.8 bitcast_dynamic-update-slice_fusion.2
  59.6 3.6 %collective-permute-done.6 = bf16[24,8192]{1,0:T(8,128)(2,1)S(1)} collective-permute-done((bf16[24,8192]{1,0:T(8,128)(2,1)S(1)}, bf16[24,8192]{1,0:T(8,128)(2,1)S(1)}, u32[]{:S(2)}, u32[]{:S(2)}) %collective-permute-start.6) | collective-permute-done | bytes 393248 | tf_op jit(solution)/shard_map/ppermute | solution.py:274
  63.2 1.9 collective-permute-start.8
  65.2 4.3 %collective-permute-start.9 = (bf16[24,4096]{1,0:T(8,128)(2,1)S(1)}, bf16[24,4096]{1,0:T(8,128)(2,1)S(1)}, u32[]{:S(2)}, u32[]{:S(2)}) collective-permute-start(bf16[24,4096]{1,0:T(8,128)(2,1)S(1)} %slice.55), channel_id=1, source_target_pairs={{0,14},{1,15},{2,0},{3,1},{4,2},{5,3},{6,4},{7,5},{8,6},{9,7},{10,... | collective-permute-start | bytes 589832 | tf_op jit(solution)/shard_map/ppermute | solution.py:278
  69.5 0.8 bitcast_dynamic-update-slice_fusion.1
  70.2 0.8 bitcast_dynamic-update-slice_fusion
  71.0 0.7 bitcast_dynamic-update-slice_fusion.8
  71.7 0.4 collective-permute-done.9
  72.1 0.7 bitcast_dynamic-update-slice_fusion.7
  72.7 6.0 %collective-permute-start.10 = (bf16[192,8192]{1,0:T(8,128)(2,1)}, bf16[192,8192]{1,0:T(8,128)(2,1)}, u32[]{:S(2)}, u32[]{:S(2)}) collective-permute-start(bf16[192,8192]{1,0:T(8,128)(2,1)} %bitcast.14.mine_hbm), channel_id=1, source_target_pairs={{0,1},{1,0},{2,3},{3,2},{4,5},{5,4},{6,7},{7,6},{8,9},{9,8},{10,11... | collective-permute-start | bytes 9437192 | tf_op jit(solution)/shard_map/ppermute | solution.py:315
  78.8 0.1 stack.23.place_ref
  78.8 5.5 %collective-permute-done.10.other_hbm = bf16[192,8192]{1,0:T(8,128)(2,1)} collective-permute-done((bf16[192,8192]{1,0:T(8,128)(2,1)}, bf16[192,8192]{1,0:T(8,128)(2,1)}, u32[]{:S(2)}, u32[]{:S(2)}) %collective-permute-start.10) | collective-permute-done | bytes 3145760 | tf_op jit(solution)/shard_map/ppermute | solution.py:315
  84.4 16.1 %block_parts.1 = (bf16[16,24,2048]{2,1,0:T(8,128)(2,1)}, bf16[16,24,2048]{2,1,0:T(8,128)(2,1)}, bf16[7,8,32,128]{3,2,1,0:T(8,128)(2,1)S(1)}, bf16[7,8,32,128]{3,...) custom-call(s32[5]{0:T(128)S(1)} %stack.23.place_ref, ...), custom_call_target="tpu_custom_call" | custom-call | flops 1761607680 | bytes 16777216 | tf_op jit(solution)/shard_map/block_parts/pallas_call | solution.py:176
  100.5 0.8 copy-done.5
  101.2 2.3 %collective-permute-start.11 = (bf16[16,24,2048]{2,1,0:T(8,128)(2,1)}, bf16[16,24,2048]{2,1,0:T(8,128)(2,1)S(1)}, u32[]{:S(2)}, u32[]{:S(2)}) collective-permute-start(bf16[16,24,2048]{2,1,0:T(8,128)(2,1)} %get-tuple-element.20), channel_id=1, source_target_pairs={{0,1},{1,0},{2,3},{3,2},{4,5},{5,4},{6,7},{7,6},{8,9},{9,8},{10,11... | collective-permute-start | bytes 4718600 | tf_op jit(solution)/shard_map/ppermute | solution.py:293
  103.5 3.1 %collective-permute-start.12 = (bf16[7,8,32,128]{3,2,1,0:T(8,128)(2,1)}, bf16[7,8,32,128]{3,2,1,0:T(8,128)(2,1)S(1)}, u32[]{:S(2)}, u32[]{:S(2)}) collective-permute-start(bf16[7,8,32,128]{3,2,1,0:T(8,128)(2,1)} %get-tuple-element.22), channel_id=1, source_target_pairs={{0,128},{32,160},{64,192},{96,224},{128,0},{160,32},{192,64},{224,... | collective-permute-start | bytes 1376264 | tf_op jit(solution)/shard_map/ppermute | solution.py:285
  106.6 2.2 %collective-permute-start.13 = (bf16[7,8,32,128]{3,2,1,0:T(8,128)(2,1)}, bf16[7,8,32,128]{3,2,1,0:T(8,128)(2,1)}, u32[]{:S(2)}, u32[]{:S(2)}) collective-permute-start(bf16[7,8,32,128]{3,2,1,0:T(8,128)(2,1)} %get-tuple-element.24), channel_id=1, source_target_pairs={{0,128},{32,160},{64,192},{96,224},{128,0},{160,32},{192,64},{224,... | collective-permute-start | bytes 1376264 | tf_op jit(solution)/shard_map/ppermute | solution.py:283
  108.8 4.4 %collective-permute-start.15 = (bf16[7,8,32,128]{3,2,1,0:T(8,128)(2,1)}, bf16[7,8,32,128]{3,2,1,0:T(8,128)(2,1)}, u32[]{:S(2)}, u32[]{:S(2)}) collective-permute-start(bf16[7,8,32,128]{3,2,1,0:T(8,128)(2,1)} %get-tuple-element.27), channel_id=1, source_target_pairs={{0,384},{32,416},{64,448},{96,480},{128,256},{160,288},{192,320},{... | collective-permute-start | bytes 1376264 | tf_op jit(solution)/shard_map/ppermute | solution.py:284
  113.2 2.1 %collective-permute-start.17 = (bf16[7,8,32,128]{3,2,1,0:T(8,128)(2,1)}, bf16[7,8,32,128]{3,2,1,0:T(8,128)(2,1)S(1)}, u32[]{:S(2)}, u32[]{:S(2)}) collective-permute-start(bf16[7,8,32,128]{3,2,1,0:T(8,128)(2,1)} %get-tuple-element.28), channel_id=1, source_target_pairs={{0,384},{32,416},{64,448},{96,480},{128,256},{160,288},{192,320},{... | collective-permute-start | bytes 1376264 | tf_op jit(solution)/shard_map/ppermute | solution.py:286
  115.3 1.4 copy-done.3
  116.7 1.4 add_cores.1
  118.1 14.4 %all-to-all-start = ((bf16[16,24,2048]{2,1,0:T(8,128)(2,1)}), bf16[16,24,2048]{2,1,0:T(8,128)(2,1)S(1)}, u32[]{:S(2)}, u32[]{:S(2)}) async-start(bf16[16,24,2048]{2,1,0:T(8,128)(2,1)} %add_cores.1), calls=%async_computation | async-start | bytes 3145728 | tf_op jit(solution)/shard_map/all_to_all | solution.py:294
  132.6 1.0 copy-done.6
  133.6 1.2 add_up.1
  134.8 4.4 %collective-permute-start.14 = (bf16[7,8,32,128]{3,2,1,0:T(8,128)(2,1)S(1)}, bf16[7,8,32,128]{3,2,1,0:T(8,128)(2,1)S(1)}, u32[]{:S(2)}, u32[]{:S(2)}) collective-permute-start(bf16[7,8,32,128]{3,2,1,0:T(8,128)(2,1)S(1)} %add_up.1), channel_id=1, source_target_pairs={{0,384},{32,416},{64,448},{96,480},{128,256},{160,288},{192,320},{... | collective-permute-start | bytes 1376264 | tf_op jit(solution)/shard_map/ppermute | solution.py:287
  139.2 1.2 add_down.1
  140.4 1.9 collective-permute-start.16
  142.3 5.8 %collective-permute-done.14.up_b = bf16[7,8,32,128]{3,2,1,0:T(8,128)(2,1)S(1)} collective-permute-done((bf16[7,8,32,128]{3,2,1,0:T(8,128)(2,1)S(1)}, bf16[7,8,32,128]{3,2,1,0:T(8,128)(2,1)S(1)}, u32[]{:S(2)}, u32[]{:S(2)}) %collective-permute-start.14) | collective-permute-done | bytes 458784 | tf_op jit(solution)/shard_map/ppermute | solution.py:287
  148.1 4.1 %collective-permute-done.16.down_a = bf16[7,8,32,128]{3,2,1,0:T(8,128)(2,1)S(1)} collective-permute-done((bf16[7,8,32,128]{3,2,1,0:T(8,128)(2,1)S(1)}, bf16[7,8,32,128]{3,2,1,0:T(8,128)(2,1)S(1)}, u32[]{:S(2)}, u32[]{:S(2)}) %collective-permute-start.16) | collective-permute-done | bytes 458784 | tf_op jit(solution)/shard_map/ppermute | solution.py:288
  152.3 3.5 %x_sum.1 = (bf16[2,7,64,128]{3,2,1,0:T(8,128)(2,1)S(1)}, bf16[2,7,64,128]{3,2,1,0:T(8,128)(2,1)S(1)}, bf16[2,7,64,128]{3,2,1,0:T(8,128)(2,1)}, bf16[2,7,64,128]{3,2,1,0:T(8,128)(2,1)}) custom-call(s32[5]{0:T(128)S(1)} %stack.23.place_ref, bf16[7,8,32,128]{3,2,1,0:T(8,128)(2,1)S(1)} %get-tuple-element.21.up_own, ...), custom_call_target="tpu_custom_call" | custom-call | flops 2097152 | bytes 4194304 | tf_op jit(solution)/shard_map/x_sum/pallas_call | solution.py:205
  155.7 1.9 collective-permute-start.19
  157.7 1.9 collective-permute-start.20
  159.6 5.4 %collective-permute-start.21 = (bf16[2,7,64,128]{3,2,1,0:T(8,128)(2,1)S(1)}, bf16[2,7,64,128]{3,2,1,0:T(8,128)(2,1)S(1)}, u32[]{:S(2)}, u32[]{:S(2)}) collective-permute-start(bf16[2,7,64,128]{3,2,1,0:T(8,128)(2,1)S(1)} %get-tuple-element.34), channel_id=1, source_target_pairs={{0,32},{32,0},{64,96},{96,64},{128,160},{160,128},{192,224},{224,1... | collective-permute-start | bytes 688136 | tf_op jit(solution)/shard_map/ppermute | solution.py:327
  165.0 8.8 %all-to-all-done.parts_ref = bf16[16,24,2048]{2,1,0:T(8,128)(2,1)S(1)} async-done(((bf16[16,24,2048]{2,1,0:T(8,128)(2,1)}), bf16[16,24,2048]{2,1,0:T(8,128)(2,1)S(1)}, u32[]{:S(2)}, u32[]{:S(2)}) %all-to-all-start) | async-done | bytes 1572896 | tf_op jit(solution)/shard_map/all_to_all | solution.py:294
  173.8 0.4 total_terms.1
  174.3 5.9 %collective-permute-start.18 = (bf16[6,4096]{1,0:T(8,128)(2,1)S(1)}, bf16[6,4096]{1,0:T(8,128)(2,1)S(1)}, u32[]{:S(2)}, u32[]{:S(2)}) collective-permute-start(bf16[6,4096]{1,0:T(8,128)(2,1)S(1)} %broadcast_select_fusion.6), channel_id=1, source_target_pairs={{0,1},{1,0},{2,3},{3,2},{4,5},{5,4},{6,7},{7,6},{8,9},{9,8},{10,11... | collective-permute-start | bytes 147464 | tf_op jit(solution)/shard_map/ppermute | solution.py:302
  180.3 2.7 %collective-permute-done.19 = bf16[2,7,64,128]{3,2,1,0:T(8,128)(2,1)S(1)} collective-permute-done((bf16[2,7,64,128]{3,2,1,0:T(8,128)(2,1)}, bf16[2,7,64,128]{3,2,1,0:T(8,128)(2,1)S(1)}, u32[]{:S(2)}, u32[]{:S(2)}) %collective-permute-start.19) | collective-permute-done | bytes 229408 | tf_op jit(solution)/shard_map/ppermute | solution.py:327
  183.0 11.6 %collective-permute-done.20 = bf16[2,7,64,128]{3,2,1,0:T(8,128)(2,1)S(1)} collective-permute-done((bf16[2,7,64,128]{3,2,1,0:T(8,128)(2,1)}, bf16[2,7,64,128]{3,2,1,0:T(8,128)(2,1)S(1)}, u32[]{:S(2)}, u32[]{:S(2)}) %collective-permute-start.20) | collective-permute-done | bytes 229408 | tf_op jit(solution)/shard_map/ppermute | solution.py:327
  194.6 0.1 add_convert_fusion
  194.7 0.7 slice_bitcast_fusion
  195.5 0.7 pad_maximum_fusion.2
  (26 shorter events, 0.2 us)
Async XLA Ops:
  1.6 3.6 %collective-permute-start = (bf16[6,8192]{1,0:T(8,128)(2,1)S(1)}, bf16[6,8192]{1,0:T(8,128)(2,1)S(1)}, u32[]{:S(2)}, u32[]{:S(2)}) collective-permute-start(bf16[6,8192]{1,0:T(8,128)(2,1)S(1)} %broadcast_select_fusion.2), channel_id=1, source_target_pairs={{0,1},{1,0},{2,3},{3,2},{4,5},{5,4},{6,7},{7,6},{8,9},{9,8},{10,11... | collective-permute-start | bytes 294920 | tf_op jit(solution)/shard_map/ppermute | solution.py:258
  6.2 18.4 %collective-permute-start.1 = (bf16[24,4096]{1,0:T(8,128)(2,1)S(1)}, bf16[24,4096]{1,0:T(8,128)(2,1)S(1)}, u32[]{:S(2)}, u32[]{:S(2)}) collective-permute-start(bf16[24,4096]{1,0:T(8,128)(2,1)S(1)} %pad_maximum_fusion), channel_id=1, source_target_pairs={{0,16},{1,17},{2,18},{3,19},{4,20},{5,21},{6,22},{7,23},{8,24},{9,... | collective-permute-start | bytes 589832 | tf_op jit(solution)/shard_map/ppermute | solution.py:262
  27.6 12.0 %collective-permute-start.2 = (bf16[24,8192]{1,0:T(8,128)(2,1)S(1)}, bf16[24,8192]{1,0:T(8,128)(2,1)S(1)}, u32[]{:S(2)}, u32[]{:S(2)}) collective-permute-start(bf16[24,8192]{1,0:T(8,128)(2,1)S(1)} %get-tuple-element.36), channel_id=1, source_target_pairs={{0,2},{1,3},{2,4},{3,5},{4,6},{5,7},{6,8},{7,9},{8,10},{9,11},{10,... | collective-permute-start | bytes 1179656 | tf_op jit(solution)/shard_map/ppermute | solution.py:274
  29.9 12.0 %collective-permute-start.3 = (bf16[24,8192]{1,0:T(8,128)(2,1)S(1)}, bf16[24,8192]{1,0:T(8,128)(2,1)S(1)}, u32[]{:S(2)}, u32[]{:S(2)}) collective-permute-start(bf16[24,8192]{1,0:T(8,128)(2,1)S(1)} %get-tuple-element.36), channel_id=1, source_target_pairs={{0,14},{1,15},{2,0},{3,1},{4,2},{5,3},{6,4},{7,5},{8,6},{9,7},{10,... | collective-permute-start | bytes 1179656 | tf_op jit(solution)/shard_map/ppermute | solution.py:275
  39.6 12.2 %collective-permute-start.4 = (bf16[24,8192]{1,0:T(8,128)(2,1)S(1)}, bf16[24,8192]{1,0:T(8,128)(2,1)S(1)}, u32[]{:S(2)}, u32[]{:S(2)}) collective-permute-start(bf16[24,8192]{1,0:T(8,128)(2,1)S(1)} %collective-permute-done.2), channel_id=1, source_target_pairs={{0,2},{1,3},{2,4},{3,5},{4,6},{5,7},{6,8},{7,9},{8,10},{9,11},{10,... | collective-permute-start | bytes 1179656 | tf_op jit(solution)/shard_map/ppermute | solution.py:274
  41.9 11.8 %collective-permute-start.5 = (bf16[24,8192]{1,0:T(8,128)(2,1)S(1)}, bf16[24,8192]{1,0:T(8,128)(2,1)S(1)}, u32[]{:S(2)}, u32[]{:S(2)}) collective-permute-start(bf16[24,8192]{1,0:T(8,128)(2,1)S(1)} %collective-permute-done.3), channel_id=1, source_target_pairs={{0,14},{1,15},{2,0},{3,1},{4,2},{5,3},{6,4},{7,5},{8,6},{9,7},{10,... | collective-permute-start | bytes 1179656 | tf_op jit(solution)/shard_map/ppermute | solution.py:275
  45.7 38.6 %copy-start.1 = (s32[7,8]{1,0:T(8,128)S(1)}, s32[7,8]{1,0:T(8,128)}, u32[]{:S(2)}) copy-start(s32[7,8]{1,0:T(8,128)} %upi_ref.1) | copy-start | bytes 676
  45.7 38.6 %copy-start.2 = (s32[7,8]{1,0:T(8,128)S(1)}, s32[7,8]{1,0:T(8,128)}, u32[]{:S(2)}) copy-start(s32[7,8]{1,0:T(8,128)} %downi_ref.1) | copy-start | bytes 676
  51.8 11.4 %collective-permute-start.6 = (bf16[24,8192]{1,0:T(8,128)(2,1)S(1)}, bf16[24,8192]{1,0:T(8,128)(2,1)S(1)}, u32[]{:S(2)}, u32[]{:S(2)}) collective-permute-start(bf16[24,8192]{1,0:T(8,128)(2,1)S(1)} %collective-permute-done.4), channel_id=1, source_target_pairs={{0,2},{1,3},{2,4},{3,5},{4,6},{5,7},{6,8},{7,9},{8,10},{9,11},{10,... | collective-permute-start | bytes 1179656 | tf_op jit(solution)/shard_map/ppermute | solution.py:274
  53.7 11.4 %collective-permute-start.7 = (bf16[24,8192]{1,0:T(8,128)(2,1)S(1)}, bf16[24,8192]{1,0:T(8,128)(2,1)S(1)}, u32[]{:S(2)}, u32[]{:S(2)}) collective-permute-start(bf16[24,8192]{1,0:T(8,128)(2,1)S(1)} %collective-permute-done.5), channel_id=1, source_target_pairs={{0,14},{1,15},{2,0},{3,1},{4,2},{5,3},{6,4},{7,5},{8,6},{9,7},{10,... | collective-permute-start | bytes 1179656 | tf_op jit(solution)/shard_map/ppermute | solution.py:275
  63.2 7.8 %collective-permute-start.8 = (bf16[24,4096]{1,0:T(8,128)(2,1)S(1)}, bf16[24,4096]{1,0:T(8,128)(2,1)S(1)}, u32[]{:S(2)}, u32[]{:S(2)}) collective-permute-start(bf16[24,4096]{1,0:T(8,128)(2,1)S(1)} %slice.54), channel_id=1, source_target_pairs={{0,2},{1,3},{2,4},{3,5},{4,6},{5,7},{6,8},{7,9},{8,10},{9,11},{10,... | collective-permute-start | bytes 589832 | tf_op jit(solution)/shard_map/ppermute | solution.py:277
  65.2 6.9 %collective-permute-start.9 = (bf16[24,4096]{1,0:T(8,128)(2,1)S(1)}, bf16[24,4096]{1,0:T(8,128)(2,1)S(1)}, u32[]{:S(2)}, u32[]{:S(2)}) collective-permute-start(bf16[24,4096]{1,0:T(8,128)(2,1)S(1)} %slice.55), channel_id=1, source_target_pairs={{0,14},{1,15},{2,0},{3,1},{4,2},{5,3},{6,4},{7,5},{8,6},{9,7},{10,... | collective-permute-start | bytes 589832 | tf_op jit(solution)/shard_map/ppermute | solution.py:278
  72.7 11.6 %collective-permute-start.10 = (bf16[192,8192]{1,0:T(8,128)(2,1)}, bf16[192,8192]{1,0:T(8,128)(2,1)}, u32[]{:S(2)}, u32[]{:S(2)}) collective-permute-start(bf16[192,8192]{1,0:T(8,128)(2,1)} %bitcast.14.mine_hbm), channel_id=1, source_target_pairs={{0,1},{1,0},{2,3},{3,2},{4,5},{5,4},{6,7},{7,6},{8,9},{9,8},{10,11... | collective-permute-start | bytes 9437192 | tf_op jit(solution)/shard_map/ppermute | solution.py:315
  100.5 0.8 copy-start.5
  101.2 14.1 %collective-permute-start.11 = (bf16[16,24,2048]{2,1,0:T(8,128)(2,1)}, bf16[16,24,2048]{2,1,0:T(8,128)(2,1)S(1)}, u32[]{:S(2)}, u32[]{:S(2)}) collective-permute-start(bf16[16,24,2048]{2,1,0:T(8,128)(2,1)} %get-tuple-element.20), channel_id=1, source_target_pairs={{0,1},{1,0},{2,3},{3,2},{4,5},{5,4},{6,7},{7,6},{8,9},{9,8},{10,11... | collective-permute-start | bytes 4718600 | tf_op jit(solution)/shard_map/ppermute | solution.py:293
  103.5 38.8 %collective-permute-start.12 = (bf16[7,8,32,128]{3,2,1,0:T(8,128)(2,1)}, bf16[7,8,32,128]{3,2,1,0:T(8,128)(2,1)S(1)}, u32[]{:S(2)}, u32[]{:S(2)}) collective-permute-start(bf16[7,8,32,128]{3,2,1,0:T(8,128)(2,1)} %get-tuple-element.22), channel_id=1, source_target_pairs={{0,128},{32,160},{64,192},{96,224},{128,0},{160,32},{192,64},{224,... | collective-permute-start | bytes 1376264 | tf_op jit(solution)/shard_map/ppermute | solution.py:285
  106.6 25.9 %collective-permute-start.13 = (bf16[7,8,32,128]{3,2,1,0:T(8,128)(2,1)}, bf16[7,8,32,128]{3,2,1,0:T(8,128)(2,1)}, u32[]{:S(2)}, u32[]{:S(2)}) collective-permute-start(bf16[7,8,32,128]{3,2,1,0:T(8,128)(2,1)} %get-tuple-element.24), channel_id=1, source_target_pairs={{0,128},{32,160},{64,192},{96,224},{128,0},{160,32},{192,64},{224,... | collective-permute-start | bytes 1376264 | tf_op jit(solution)/shard_map/ppermute | solution.py:283
  108.8 30.4 %collective-permute-start.15 = (bf16[7,8,32,128]{3,2,1,0:T(8,128)(2,1)}, bf16[7,8,32,128]{3,2,1,0:T(8,128)(2,1)}, u32[]{:S(2)}, u32[]{:S(2)}) collective-permute-start(bf16[7,8,32,128]{3,2,1,0:T(8,128)(2,1)} %get-tuple-element.27), channel_id=1, source_target_pairs={{0,384},{32,416},{64,448},{96,480},{128,256},{160,288},{192,320},{... | collective-permute-start | bytes 1376264 | tf_op jit(solution)/shard_map/ppermute | solution.py:284
  113.2 29.1 %collective-permute-start.17 = (bf16[7,8,32,128]{3,2,1,0:T(8,128)(2,1)}, bf16[7,8,32,128]{3,2,1,0:T(8,128)(2,1)S(1)}, u32[]{:S(2)}, u32[]{:S(2)}) collective-permute-start(bf16[7,8,32,128]{3,2,1,0:T(8,128)(2,1)} %get-tuple-element.28), channel_id=1, source_target_pairs={{0,384},{32,416},{64,448},{96,480},{128,256},{160,288},{192,320},{... | collective-permute-start | bytes 1376264 | tf_op jit(solution)/shard_map/ppermute | solution.py:286
  115.3 1.4 copy-start.3
  118.1 55.7 %all-to-all-start = ((bf16[16,24,2048]{2,1,0:T(8,128)(2,1)}), bf16[16,24,2048]{2,1,0:T(8,128)(2,1)S(1)}, u32[]{:S(2)}, u32[]{:S(2)}) async-start(bf16[16,24,2048]{2,1,0:T(8,128)(2,1)} %add_cores.1), calls=%async_computation | async-start | bytes 3145728 | tf_op jit(solution)/shard_map/all_to_all | solution.py:294
  132.6 1.0 copy-start.6
  133.6 5.6 %copy-start.4 = (bf16[7,8,32,128]{3,2,1,0:T(8,128)(2,1)S(1)}, bf16[7,8,32,128]{3,2,1,0:T(8,128)(2,1)}, u32[]{:S(2)}) copy-start(bf16[7,8,32,128]{3,2,1,0:T(8,128)(2,1)} %get-tuple-element.26.a_ref) | copy-start | bytes 1376260
  134.8 13.4 %collective-permute-start.14 = (bf16[7,8,32,128]{3,2,1,0:T(8,128)(2,1)S(1)}, bf16[7,8,32,128]{3,2,1,0:T(8,128)(2,1)S(1)}, u32[]{:S(2)}, u32[]{:S(2)}) collective-permute-start(bf16[7,8,32,128]{3,2,1,0:T(8,128)(2,1)S(1)} %add_up.1), channel_id=1, source_target_pairs={{0,384},{32,416},{64,448},{96,480},{128,256},{160,288},{192,320},{... | collective-permute-start | bytes 1376264 | tf_op jit(solution)/shard_map/ppermute | solution.py:287
  139.2 13.1 %copy-start = (bf16[7,8,32,128]{3,2,1,0:T(8,128)(2,1)S(1)}, bf16[7,8,32,128]{3,2,1,0:T(8,128)(2,1)}, u32[]{:S(2)}) copy-start(bf16[7,8,32,128]{3,2,1,0:T(8,128)(2,1)} %get-tuple-element.25.down_own) | copy-start | bytes 1376260
  140.4 11.9 %collective-permute-start.16 = (bf16[7,8,32,128]{3,2,1,0:T(8,128)(2,1)S(1)}, bf16[7,8,32,128]{3,2,1,0:T(8,128)(2,1)S(1)}, u32[]{:S(2)}, u32[]{:S(2)}) collective-permute-start(bf16[7,8,32,128]{3,2,1,0:T(8,128)(2,1)S(1)} %add_down.1), channel_id=1, source_target_pairs={{0,128},{32,160},{64,192},{96,224},{128,0},{160,32},{192,64},{224,... | collective-permute-start | bytes 1376264 | tf_op jit(solution)/shard_map/ppermute | solution.py:288
  155.7 27.2 %collective-permute-start.19 = (bf16[2,7,64,128]{3,2,1,0:T(8,128)(2,1)}, bf16[2,7,64,128]{3,2,1,0:T(8,128)(2,1)S(1)}, u32[]{:S(2)}, u32[]{:S(2)}) collective-permute-start(bf16[2,7,64,128]{3,2,1,0:T(8,128)(2,1)} %get-tuple-element.32), channel_id=1, source_target_pairs={{0,64},{32,96},{64,0},{96,32},{128,192},{160,224},{192,128},{224,1... | collective-permute-start | bytes 688136 | tf_op jit(solution)/shard_map/ppermute | solution.py:327
  157.7 36.9 %collective-permute-start.20 = (bf16[2,7,64,128]{3,2,1,0:T(8,128)(2,1)}, bf16[2,7,64,128]{3,2,1,0:T(8,128)(2,1)S(1)}, u32[]{:S(2)}, u32[]{:S(2)}) collective-permute-start(bf16[2,7,64,128]{3,2,1,0:T(8,128)(2,1)} %get-tuple-element.33), channel_id=1, source_target_pairs={{0,96},{32,64},{64,32},{96,0},{128,224},{160,192},{192,160},{224,1... | collective-permute-start | bytes 688136 | tf_op jit(solution)/shard_map/ppermute | solution.py:327
  159.6 35.0 %collective-permute-start.21 = (bf16[2,7,64,128]{3,2,1,0:T(8,128)(2,1)S(1)}, bf16[2,7,64,128]{3,2,1,0:T(8,128)(2,1)S(1)}, u32[]{:S(2)}, u32[]{:S(2)}) collective-permute-start(bf16[2,7,64,128]{3,2,1,0:T(8,128)(2,1)S(1)} %get-tuple-element.34), channel_id=1, source_target_pairs={{0,32},{32,0},{64,96},{96,64},{128,160},{160,128},{192,224},{224,1... | collective-permute-start | bytes 688136 | tf_op jit(solution)/shard_map/ppermute | solution.py:327
  174.3 21.1 %collective-permute-start.18 = (bf16[6,4096]{1,0:T(8,128)(2,1)S(1)}, bf16[6,4096]{1,0:T(8,128)(2,1)S(1)}, u32[]{:S(2)}, u32[]{:S(2)}) collective-permute-start(bf16[6,4096]{1,0:T(8,128)(2,1)S(1)} %broadcast_select_fusion.6), channel_id=1, source_target_pairs={{0,1},{1,0},{2,3},{3,2},{4,5},{5,4},{6,7},{7,6},{8,9},{9,8},{10,11... | collective-permute-start | bytes 147464 | tf_op jit(solution)/shard_map/ppermute | solution.py:302

commit v3 on v2

--- a/solution.py
+++ b/solution.py
@@ -43,6 +43,10 @@
 NT = (((1,), (1,)), ((), ()))
 
 
+UP_PLACE = (4, 1, 0, 5)
+DOWN_PLACE = (6, 7, 2, 3)
+
+
 def columns(rows, index_ref, j, k, block):
     side_by_side = []
     for slot in (k, k + 1):
@@ -51,43 +55,56 @@
     return jnp.concatenate(side_by_side, axis=1)
 
 
-def block_kernel(factor, place_ref, upi_ref, downi_ref, mine_hbm, other_hbm, up_hbm, down_hbm,
-                 send_ref, keep_ref, up0, up1, up2, up3, down0, down1, down2, down3,
-                 parts_ref, inputs, grads, acc_ref, up_ref, down_ref, pg_ref, act_ref, us_ref, ds_ref, sems, out_sem):
+def block_kernel(factor, place_ref, upi_ref, downi_ref, mine_a, mine_b, other_a, other_b, up_hbm, down_hbm,
+                 send_ref, keep_ref, even_out, odd_out, up0, up3, down0, down1,
+                 parts_ref, inputs, grads, acc_ref, up_ref, down_ref, pre_ref, pg_ref, act_ref, us_ref, ds_ref, sems, out_sem):
     hidden, slots, block, _ = up_ref.shape
     pieces, rows, quarter = keep_ref.shape
     share = up0.shape[2]
-    outs = (up0, up1, up2, up3, down0, down1, down2, down3)
-
-    def load_rows(first, second):
-        pltpu.make_async_copy(first, inputs, sems.at[2, 0]).start()
-        pltpu.make_async_copy(second, grads, sems.at[2, 1]).start()
-
-    @pl.when(place_ref[0] == 0)
-    def _():
-        load_rows(mine_hbm, other_hbm)
-
-    @pl.when(place_ref[0] != 0)
-    def _():
-        load_rows(other_hbm, mine_hbm)
-
-    loads = []
+
+    split = mine_a.shape[0]
+
+    def row_copies(parts, into, at):
+        return [pltpu.make_async_copy(parts[0], into.at[0:split], sems.at[at, 0]),
+                pltpu.make_async_copy(parts[1], into.at[split:], sems.at[at, 1])]
+
+    def start_rows(into, at, wanted):
+        @pl.when(place_ref[0] == wanted)
+        def _():
+            for load in row_copies((mine_a, mine_b), into, at):
+                load.start()
+
+        @pl.when(place_ref[0] != wanted)
+        def _():
+            for load in row_copies((other_a, other_b), into, at):
+                load.start()
+
+    start_rows(inputs, 2, 0)
+    up_loads = [pltpu.make_async_copy(up_hbm.at[j], up_ref.at[j], sems.at[0, j]) for j in range(hidden)]
+    down_loads = [pltpu.make_async_copy(down_hbm.at[j], down_ref.at[j], sems.at[1, j]) for j in range(hidden)]
+    for load in up_loads:
+        load.start()
+    start_rows(grads, 3, 1)
+    for load in down_loads:
+        load.start()
+    acc_ref[...] = jnp.zeros_like(acc_ref)
+    for load in row_copies((mine_a, mine_b), inputs, 2):
+        load.wait()
     for j in range(hidden):
-        for at, (far, near) in enumerate(((up_hbm, up_ref), (down_hbm, down_ref))):
-            loads.append(pltpu.make_async_copy(far.at[j], near.at[j], sems.at[at, j]))
-            loads[-1].start()
-    acc_ref[...] = jnp.zeros_like(acc_ref)
-    pltpu.make_async_copy(mine_hbm, inputs, sems.at[2, 0]).wait()
-    pltpu.make_async_copy(other_hbm, grads, sems.at[2, 1]).wait()
-
-    for j in range(hidden):
-        loads[2 * j].wait()
-        loads[2 * j + 1].wait()
-        preact = hidden_grad = 0.0
+        up_loads[j].wait()
+        preact = 0.0
         for k in range(0, slots, 2):
             weights = up_ref[j, k:k + 2].reshape(2 * block, block)
             preact = preact + jnp.dot(columns(inputs, upi_ref, j, k, block), weights,
                                       preferred_element_type=jnp.float32)
+        pre_ref[j] = preact
+    for load in row_copies((mine_a, mine_b), grads, 3):
+        load.wait()
+
+    for j in range(hidden):
+        down_loads[j].wait()
+        preact, hidden_grad = pre_ref[j], 0.0
+        for k in range(0, slots, 2):
             weights = jnp.concatenate([down_ref[j, k], down_ref[j, k + 1]], axis=1)
             hidden_grad = hidden_grad + lax.dot_general(
                 columns(grads, downi_ref, j, k, block), weights, NT, preferred_element_type=jnp.float32)
@@ -108,19 +125,21 @@
         act = act_ref[j]
         for k in range(0, slots, 2):
             sums = jnp.dot(pg, columns(inputs, upi_ref, j, k, block), preferred_element_type=jnp.float32)
-            sums = sums * factor
+            sums = (sums * factor).astype(jnp.bfloat16)
             for slot in (k, k + 1):
                 us_ref[slot] = sums[:, (slot - k) * block:(slot - k + 1) * block].T
             sums = jnp.dot(act, columns(grads, downi_ref, j, k, block), preferred_element_type=jnp.float32)
-            sums = sums * factor
+            sums = (sums * factor).astype(jnp.bfloat16)
             for slot in (k, k + 1):
                 ds_ref[slot] = sums[:, (slot - k) * block:(slot - k + 1) * block]
         for q in range(X):
             row = pl.multiple_of((place_ref[1] ^ q) * share, share)
-            parts_ref[q, j] = us_ref[:, pl.ds(row, share), :].astype(jnp.bfloat16)
-            parts_ref[X + q, j] = ds_ref[:, pl.ds(row, share), :].astype(jnp.bfloat16)
-
-    stores = [pltpu.make_async_copy(parts_ref.at[n], out, out_sem.at[n]) for n, out in enumerate(outs)]
+            parts_ref[UP_PLACE[q], j] = us_ref[:, pl.ds(row, share), :]
+            parts_ref[DOWN_PLACE[q], j] = ds_ref[:, pl.ds(row, share), :]
+
+    pairs = [(parts_ref.at[0:2], even_out), (parts_ref.at[2:4], odd_out)]
+    pairs += [(parts_ref.at[4 + n], out) for n, out in enumerate((up0, up3, down0, down1))]
+    stores = [pltpu.make_async_copy(*pair, out_sem.at[n]) for n, pair in enumerate(pairs)]
     for store in stores:
         store.start()
 
@@ -128,9 +147,9 @@
     for out, core in ((send_ref, 1 - place_ref[0]), (keep_ref, place_ref[0])):
         left = pl.multiple_of(core * 2 * quarter, quarter)
         right = pl.multiple_of(core * 2 * quarter + quarter, quarter)
-        for k in range(Y):
+        for at, k in enumerate(FIRST + SECOND):
             owner = (place_ref[3] - k) & (Y - 1)
-            here = slice(k * rows, (k + 1) * rows)
+            here = slice(at * rows, (at + 1) * rows)
             a = acc_ref[here, pl.ds(left, quarter)]
             b = acc_ref[here, pl.ds(right, quarter)]
             half = rows // 2
@@ -142,15 +161,16 @@
 
 def x_sum_kernel(place_ref, up_own, up_a, up_b, down_own, down_a, down_b, *refs):
     outs, sum_ref = refs[:Z_LO], refs[Z_LO]
-    _, slots, share, block = up_own.shape
+    hidden, slots, share, block = up_own.shape
     rows = share // Z_LO
-    for kind, parts in enumerate(((up_own, up_a, up_b), (down_own, down_a, down_b))):
-        total = sum(part[0].astype(jnp.float32) for part in parts)
-        sum_ref[kind] = total.reshape(slots * share, block)
-        for r, out in enumerate(outs):
-            row = pl.multiple_of((place_ref[2] ^ r) * rows, rows)
-            piece = [sum_ref[kind, pl.ds(k * share + row, rows), :] for k in range(slots)]
-            out[kind, 0] = jnp.concatenate(piece, axis=0).astype(jnp.bfloat16)
+    for kind, parts in enumerate(((up_own, up_a.at[1], up_b), (down_own, down_a, down_b.at[1]))):
+        for j in range(hidden):
+            total = sum(part[j].astype(jnp.float32) for part in parts)
+            sum_ref[kind, j] = total.reshape(slots * share, block)
+            for r, out in enumerate(outs):
+                row = pl.multiple_of((place_ref[2] ^ r) * rows, rows)
+                piece = [sum_ref[kind, j, pl.ds(k * share + row, rows), :] for k in range(slots)]
+                out[kind, j] = jnp.concatenate(piece, axis=0).astype(jnp.bfloat16)
 
 
 def add_kernel(a_ref, b_ref, out_ref):
@@ -167,17 +187,19 @@
 HBM = pl.BlockSpec(memory_space=pltpu.HBM)
 
 
-def block_parts(factor, place, up_index, down_index, mine, other, up_blocks, down_blocks):
+def block_parts(factor, place, up_index, down_index, gathered, up_blocks, down_blocks):
     hidden, slots, block, _ = up_blocks.shape
-    rows, features = mine.shape
+    rows = gathered[0].shape[0] + gathered[1].shape[0]
+    features = gathered[0].shape[1]
     flops = 5 * 2 * rows * hidden * slots * block * block
     terms = jax.ShapeDtypeStruct((Z_HI * Y, rows // Y, features // 4), jnp.bfloat16)
     part = jax.ShapeDtypeStruct((hidden, slots, block // X, block), jnp.bfloat16)
+    both = jax.ShapeDtypeStruct((2,) + part.shape, jnp.bfloat16)
     return pl.pallas_call(
         functools.partial(block_kernel, factor),
-        in_specs=[SMEM] * 3 + [pl.BlockSpec(memory_space=pl.ANY)] * 2 + [HBM] * 2,
-        out_specs=[VMEM] * 2 + [HBM] * 8,
-        out_shape=[terms] * 2 + [part] * 8,
+        in_specs=[SMEM] * 3 + [HBM] * 6,
+        out_specs=[VMEM] * 2 + [HBM] * 6,
+        out_shape=[terms] * 2 + [both] * 2 + [part] * 4,
         scratch_shapes=[
             pltpu.VMEM((2 * X,) + part.shape, jnp.bfloat16),
             pltpu.VMEM((rows, features), jnp.bfloat16),
@@ -185,33 +207,29 @@
             pltpu.VMEM((rows, features), jnp.float32),
             pltpu.VMEM(up_blocks.shape, jnp.bfloat16),
             pltpu.VMEM(down_blocks.shape, jnp.bfloat16),
+            pltpu.VMEM((hidden, rows, block), jnp.float32),
             pltpu.VMEM((hidden, block, rows), jnp.bfloat16),
             pltpu.VMEM((hidden, block, rows), jnp.bfloat16),
-            pltpu.VMEM((slots, block, block), jnp.float32),
-            pltpu.VMEM((slots, block, block), jnp.float32),
-            pltpu.SemaphoreType.DMA((3, hidden)),
+            pltpu.VMEM((slots, block, block), jnp.bfloat16),
+            pltpu.VMEM((slots, block, block), jnp.bfloat16),
+            pltpu.SemaphoreType.DMA((4, hidden)),
             pltpu.SemaphoreType.DMA((2 * X,)),
         ],
-        compiler_params=pltpu.CompilerParams(vmem_limit_bytes=52 * 2**20),
+        compiler_params=pltpu.CompilerParams(vmem_limit_bytes=58 * 2**20),
         cost_estimate=pl.CostEstimate(flops=flops, bytes_accessed=16 * 2**20, transcendentals=0),
         name="block_parts",
-    )(place, up_index, down_index, mine, other, up_blocks, down_blocks)
+    )(place, up_index, down_index, *gathered, up_blocks, down_blocks)
 
 
 def x_sum(place, *parts):
     hidden, slots, share, block = parts[0].shape
     rows = slots * share // Z_LO
-    part = pl.BlockSpec((1, slots, share, block), lambda j, *_: (j, 0, 0, 0))
     return pl.pallas_call(
         x_sum_kernel,
-        grid_spec=pltpu.PrefetchScalarGridSpec(
-            num_scalar_prefetch=1,
-            grid=(hidden,),
-            in_specs=[part] * 6,
-            out_specs=[pl.BlockSpec((2, 1, rows, block), lambda j, *_: (0, j, 0, 0))] * Z_LO,
-            scratch_shapes=[pltpu.VMEM((2, slots * share, block), jnp.float32)],
-        ),
+        in_specs=[SMEM] + [VMEM] * 6,
+        out_specs=[VMEM] * Z_LO,
         out_shape=[jax.ShapeDtypeStruct((2, hidden, rows, block), jnp.bfloat16)] * Z_LO,
+        scratch_shapes=[pltpu.VMEM((2, hidden, slots * share, block), jnp.float32)],
         compiler_params=pltpu.CompilerParams(vmem_limit_bytes=8 * 2**20),
         cost_estimate=pl.CostEstimate(flops=2**21, bytes_accessed=4 * 2**20, transcendentals=0),
         name="x_sum",
@@ -227,9 +245,11 @@
 
 def add_terms(a, b, microseconds, name):
     half = a.shape[0] // 2 if a.shape[0] % 2 == 0 else a.shape[0]
-    spec = pl.BlockSpec((half,) + a.shape[1:], lambda i: (i,) + (0,) * (a.ndim - 1))
+    rest = (0,) * (a.ndim - 1)
+    spec = pl.BlockSpec((half,) + a.shape[1:], lambda i: (i,) + rest)
+    first = pl.BlockSpec((None, half) + a.shape[1:], lambda i: (0, i) + rest)
     return pl.pallas_call(
-        add_kernel, grid=(a.shape[0] // half,), in_specs=[spec] * 2, out_specs=spec,
+        add_kernel, grid=(a.shape[0] // half,), in_specs=[spec, first if b.ndim > a.ndim else spec], out_specs=spec,
         out_shape=jax.ShapeDtypeStruct(a.shape, jnp.bfloat16), cost_estimate=cost(microseconds), name=name,
         compiler_params=SMALL,
     )(a, b)
@@ -250,6 +270,10 @@
     a = jnp.where(first_is_mine, mine, other)
     b = jnp.where(first_is_mine, other, mine)
     return jnp.concatenate([a, b], axis=0)
+
+
+FIRST = (0, 1, 7, 2, 6, 3)
+SECOND = (5, 4)
 
 
 def gather_rows(inputs, grad_out, core, zero):
@@ -262,31 +286,33 @@
     other = lax.ppermute(pair, "tensor", Z_PARTNER)
     left = jnp.concatenate([pair[:rows], other[:rows]], axis=0)
     right = jnp.concatenate([pair[rows:], other[rows:]], axis=0)
-    chunk = jnp.concatenate([left, right], axis=1)
-    whole = jnp.zeros((Y, 2 * rows, features), chunk.dtype)
+    chunk = lax.optimization_barrier(jnp.concatenate([left, right], axis=1))
+    first = jnp.zeros((len(FIRST), 2 * rows, features), chunk.dtype)
+    second = jnp.zeros((len(SECOND), 2 * rows, features), chunk.dtype)
 
     def place(whole, piece, at, column=0):
         return lax.dynamic_update_slice(whole, piece[None], (zero + at, 0, column))
 
-    whole = place(whole, chunk, 0)
+    first = place(first, chunk, FIRST.index(0))
     up = down = chunk
     for step in range(1, Y // 2):
         up = lax.ppermute(up, "tensor", Y_UP)
         down = lax.ppermute(down, "tensor", Y_DOWN)
-        whole = place(place(whole, up, step), down, Y - step)
-    whole = place(whole, lax.ppermute(up[:, :half], "tensor", Y_UP), Y // 2)
-    whole = place(whole, lax.ppermute(down[:, half:], "tensor", Y_DOWN), Y // 2, half)
-    return whole.reshape(-1, features)
-
-
-def reduce_weights_x(place, up, down):
-    far_up = lax.ppermute(up[2], "seq", X_EVEN)
-    far_down = lax.ppermute(down[2], "seq", X_ODD)
-    up_a = lax.ppermute(up[1], "seq", X_EVEN)
-    down_b = lax.ppermute(down[3], "seq", X_ODD)
-    up_b = lax.ppermute(add_terms(up[3], far_up, 20, "add_up"), "seq", X_ODD)
-    down_a = lax.ppermute(add_terms(down[1], far_down, 20, "add_down"), "seq", X_EVEN)
-    return x_sum(place, up[0], up_a, up_b, down[0], down_a, down_b)
+        first = place(first, up, FIRST.index(step))
+        if Y - step in FIRST:
+            first = place(first, down, FIRST.index(Y - step))
+    second = place(second, down, SECOND.index(Y // 2 + 1))
+    second = place(second, lax.ppermute(up[:, :half], "tensor", Y_UP), SECOND.index(Y // 2))
+    second = place(second, lax.ppermute(down[:, half:], "tensor", Y_DOWN), SECOND.index(Y // 2), half)
+    return first.reshape(-1, features), second.reshape(-1, features)
+
+
+def reduce_weights_x(place, even, odd, up_own, up_odd, down_own, down_even):
+    even = lax.ppermute(even, "seq", X_EVEN)
+    odd = lax.ppermute(odd, "seq", X_ODD)
+    up_odd = lax.ppermute(add_terms(up_odd, even, 20, "add_up"), "seq", X_ODD)
+    down_even = lax.ppermute(add_terms(down_even, odd, 20, "add_down"), "seq", X_EVEN)
+    return x_sum(place, up_own, even, up_odd, down_own, down_even, odd)
 
 
 def reduce_inputs(keep, send):
@@ -311,16 +337,16 @@
     z_hi = t >> 4
     rows_here, _ = inputs.shape
     factor = 1.0 / math.sqrt(rows_here * lax.axis_size("tensor") * lax.axis_size("seq"))
-    mine = gather_rows(inputs, grad_out, core, t >> 5)
-    other = lax.ppermute(mine, "tensor", SIBLING)
+    first, second = gather_rows(inputs, grad_out, core, t >> 5)
+    gathered = (first, second, lax.ppermute(first, "tensor", SIBLING), lax.ppermute(second, "tensor", SIBLING))
     seq = lax.axis_index("seq")
     y = (t >> 1) & (Y - 1)
     place = jnp.stack([core, seq >> 2, seq & (Z_LO - 1), y, z_hi]).astype(jnp.int32)
-    send, keep, *parts = block_parts(factor, place, up_index, down_index, mine, other, up_blocks, down_blocks)
+    send, keep, *parts = block_parts(factor, place, up_index, down_index, gathered, up_blocks, down_blocks)
     hidden, slots, block, _ = up_blocks.shape
     shape = (hidden, slots, block // (X * Z_LO), block)
     input_terms = reduce_inputs(keep, send)
-    pieces = reduce_weights_x(place, parts[:4], parts[4:])
+    pieces = reduce_weights_x(place, *parts)
     first = pieces[0]
     input_terms, first = lax.optimization_barrier((input_terms, first))
     grad_in = own_rows(input_terms, core)

time: 197 us -> 184 us (0.934)
  the two profiles are of different devices: /device:TPU:169 before, /device:TPU:185 now
where the time goes in v3:
time: 184 us; the launch traced here: 183 us
  starting transfers between devices  87.3 us (47%)
  waiting for transfers between devices  66 us (36%)
  Pallas kernels  20.5 us (11%)
  local copies, waits for them, and re-layouts  5.12 us (3%)
  other arithmetic  3.03 us (2%)
    ppermute x3, waiting for transfers between devices, gather_rows(): down = lax.ppermute(down, 'tensor', Y_DOWN)  16.9 us
    pallas_call x1, Pallas kernels, block_parts(): pl.pallas_call(functools.partial(block_kernel, factor), in_specs=[SMEM] *...  16.6 us
    ppermute x3, waiting for transfers between devices, local(): lax.ppermute(pieces[r], 'seq', Z_TRADE[r])  15.1 us
    ppermute x3, starting transfers between devices, gather_rows(): up = lax.ppermute(up, 'tensor', Y_UP)  12.7 us
    all_to_all x1, starting transfers between devices, reduce_inputs(): lax.all_to_all(part, 'tensor', 0, 0, axis_index_groups=ROW_GROUPS, tiled=...  12.1 us
    ppermute x1, waiting for transfers between devices, gather_rows(): other = lax.ppermute(pair, 'tensor', Z_PARTNER)  9.58 us
    ppermute x3, starting transfers between devices, local(): lax.ppermute(pieces[r], 'seq', Z_TRADE[r])  9.26 us
    all_to_all x1, waiting for transfers between devices, reduce_inputs(): lax.all_to_all(part, 'tensor', 0, 0, axis_index_groups=ROW_GROUPS, tiled=...  8.92 us
  transfers between devices with their start and end apart: 22, of which 12 were waited for; matrix products, arithmetic and copies ran while one was open for 1% of the time, Pallas kernels for 2%

profile of v3, /device:TPU:185, one launch (start us, length us, event | category | flops | bytes accessed | tf_op | source)
XLA Modules:
  0.0 183.1 jit_solution(9960237081244499646)
XLA Ops:
  0.6 0.9 broadcast_select_fusion.2
  1.6 2.6 %collective-permute-start = (bf16[6,8192]{1,0:T(8,128)(2,1)S(1)}, bf16[6,8192]{1,0:T(8,128)(2,1)S(1)}, u32[]{:S(2)}, u32[]{:S(2)}) collective-permute-start(bf16[6,8192]{1,0:T(8,128)(2,1)S(1)} %broadcast_select_fusion.2), channel_id=1, source_target_pairs={{0,1},{1,0},{2,3},{3,2},{4,5},{5,4},{6,7},{7,6},{8,9},{9,8},{10,11... | collective-permute-start | bytes 294920 | tf_op jit(solution)/shard_map/ppermute | solution.py:282
  4.2 1.0 collective-permute-done
  5.1 0.9 broadcast_select_fusion.1
  6.1 0.1 fusion
  6.2 0.1 pad_maximum_fusion
  6.2 8.8 %collective-permute-start.1 = (bf16[24,4096]{1,0:T(8,128)(2,1)S(1)}, bf16[24,4096]{1,0:T(8,128)(2,1)S(1)}, u32[]{:S(2)}, u32[]{:S(2)}) collective-permute-start(bf16[24,4096]{1,0:T(8,128)(2,1)S(1)} %pad_maximum_fusion), channel_id=1, source_target_pairs={{0,16},{1,17},{2,18},{3,19},{4,20},{5,21},{6,22},{7,23},{8,24},{9,... | collective-permute-start | bytes 589832 | tf_op jit(solution)/shard_map/ppermute | solution.py:286
  15.1 9.6 %collective-permute-done.1 = bf16[24,4096]{1,0:T(8,128)(2,1)S(1)} collective-permute-done((bf16[24,4096]{1,0:T(8,128)(2,1)S(1)}, bf16[24,4096]{1,0:T(8,128)(2,1)S(1)}, u32[]{:S(2)}, u32[]{:S(2)}) %collective-permute-start.1) | collective-permute-done | bytes 196640 | tf_op jit(solution)/shard_map/ppermute | solution.py:286
  24.7 0.1 maximum_maximum_fusion
  24.8 3.0 %collective-permute-start.3 = (bf16[24,8192]{1,0:T(8,128)(2,1)S(1)}, bf16[24,8192]{1,0:T(8,128)(2,1)S(1)}, u32[]{:S(2)}, u32[]{:S(2)}) collective-permute-start(bf16[24,8192]{1,0:T(8,128)(2,1)S(1)} %maximum_maximum_fusion), channel_id=1, source_target_pairs={{0,14},{1,15},{2,0},{3,1},{4,2},{5,3},{6,4},{7,5},{8,6},{9,7},{10,... | collective-permute-start | bytes 1179656 | tf_op jit(solution)/shard_map/ppermute | solution.py:300
  27.8 3.5 %collective-permute-start.2 = (bf16[24,8192]{1,0:T(8,128)(2,1)S(1)}, bf16[24,8192]{1,0:T(8,128)(2,1)S(1)}, u32[]{:S(2)}, u32[]{:S(2)}) collective-permute-start(bf16[24,8192]{1,0:T(8,128)(2,1)S(1)} %maximum_maximum_fusion), channel_id=1, source_target_pairs={{0,2},{1,3},{2,4},{3,5},{4,6},{5,7},{6,8},{7,9},{8,10},{9,11},{10,... | collective-permute-start | bytes 1179656 | tf_op jit(solution)/shard_map/ppermute | solution.py:299
  31.3 0.2 broadcast_in_dim.33
  31.6 6.4 %collective-permute-done.3 = bf16[24,8192]{1,0:T(8,128)(2,1)S(1)} collective-permute-done((bf16[24,8192]{1,0:T(8,128)(2,1)S(1)}, bf16[24,8192]{1,0:T(8,128)(2,1)S(1)}, u32[]{:S(2)}, u32[]{:S(2)}) %collective-permute-start.3) | collective-permute-done | bytes 393248 | tf_op jit(solution)/shard_map/ppermute | solution.py:300
  38.0 1.9 %collective-permute-start.5 = (bf16[24,8192]{1,0:T(8,128)(2,1)S(1)}, bf16[24,8192]{1,0:T(8,128)(2,1)S(1)}, u32[]{:S(2)}, u32[]{:S(2)}) collective-permute-start(bf16[24,8192]{1,0:T(8,128)(2,1)S(1)} %collective-permute-done.3), channel_id=1, source_target_pairs={{0,14},{1,15},{2,0},{3,1},{4,2},{5,3},{6,4},{7,5},{8,6},{9,7},{10,... | collective-permute-start | bytes 1179656 | tf_op jit(solution)/shard_map/ppermute | solution.py:300
  40.0 0.0 collective-permute-done.2
  40.0 4.6 %collective-permute-start.4 = (bf16[24,8192]{1,0:T(8,128)(2,1)S(1)}, bf16[24,8192]{1,0:T(8,128)(2,1)S(1)}, u32[]{:S(2)}, u32[]{:S(2)}) collective-permute-start(bf16[24,8192]{1,0:T(8,128)(2,1)S(1)} %collective-permute-done.2), channel_id=1, source_target_pairs={{0,2},{1,3},{2,4},{3,5},{4,6},{5,7},{6,8},{7,9},{8,10},{9,11},{10,... | collective-permute-start | bytes 1179656 | tf_op jit(solution)/shard_map/ppermute | solution.py:299
  44.6 5.7 %collective-permute-done.5 = bf16[24,8192]{1,0:T(8,128)(2,1)S(1)} collective-permute-done((bf16[24,8192]{1,0:T(8,128)(2,1)S(1)}, bf16[24,8192]{1,0:T(8,128)(2,1)S(1)}, u32[]{:S(2)}, u32[]{:S(2)}) %collective-permute-start.5) | collective-permute-done | bytes 393248 | tf_op jit(solution)/shard_map/ppermute | solution.py:300
  50.3 1.9 %collective-permute-start.7 = (bf16[24,8192]{1,0:T(8,128)(2,1)S(1)}, bf16[24,8192]{1,0:T(8,128)(2,1)S(1)}, u32[]{:S(2)}, u32[]{:S(2)}) collective-permute-start(bf16[24,8192]{1,0:T(8,128)(2,1)S(1)} %collective-permute-done.5), channel_id=1, source_target_pairs={{0,14},{1,15},{2,0},{3,1},{4,2},{5,3},{6,4},{7,5},{8,6},{9,7},{10,... | collective-permute-start | bytes 1179656 | tf_op jit(solution)/shard_map/ppermute | solution.py:300
  52.2 0.0 collective-permute-done.4
  52.3 4.6 %collective-permute-start.6 = (bf16[24,8192]{1,0:T(8,128)(2,1)S(1)}, bf16[24,8192]{1,0:T(8,128)(2,1)S(1)}, u32[]{:S(2)}, u32[]{:S(2)}) collective-permute-start(bf16[24,8192]{1,0:T(8,128)(2,1)S(1)} %collective-permute-done.4), channel_id=1, source_target_pairs={{0,2},{1,3},{2,4},{3,5},{4,6},{5,7},{6,8},{7,9},{8,10},{9,11},{10,... | collective-permute-start | bytes 1179656 | tf_op jit(solution)/shard_map/ppermute | solution.py:299
  56.9 4.8 %collective-permute-done.7 = bf16[24,8192]{1,0:T(8,128)(2,1)S(1)} collective-permute-done((bf16[24,8192]{1,0:T(8,128)(2,1)S(1)}, bf16[24,8192]{1,0:T(8,128)(2,1)S(1)}, u32[]{:S(2)}, u32[]{:S(2)}) %collective-permute-start.7) | collective-permute-done | bytes 393248 | tf_op jit(solution)/shard_map/ppermute | solution.py:300
  61.7 1.9 %collective-permute-start.9 = (bf16[24,4096]{1,0:T(8,128)(2,1)S(1)}, bf16[24,4096]{1,0:T(8,128)(2,1)S(1)}, u32[]{:S(2)}, u32[]{:S(2)}) collective-permute-start(bf16[24,4096]{1,0:T(8,128)(2,1)S(1)} %slice.55), channel_id=1, source_target_pairs={{0,14},{1,15},{2,0},{3,1},{4,2},{5,3},{6,4},{7,5},{8,6},{9,7},{10,... | collective-permute-start | bytes 589832 | tf_op jit(solution)/shard_map/ppermute | solution.py:306
  63.7 0.0 collective-permute-done.6
  63.7 4.6 %collective-permute-start.8 = (bf16[24,4096]{1,0:T(8,128)(2,1)S(1)}, bf16[24,4096]{1,0:T(8,128)(2,1)S(1)}, u32[]{:S(2)}, u32[]{:S(2)}) collective-permute-start(bf16[24,4096]{1,0:T(8,128)(2,1)S(1)} %slice.54), channel_id=1, source_target_pairs={{0,2},{1,3},{2,4},{3,5},{4,6},{5,7},{6,8},{7,9},{8,10},{9,11},{10,... | collective-permute-start | bytes 589832 | tf_op jit(solution)/shard_map/ppermute | solution.py:305
  68.3 5.7 %collective-permute-start.10 = (bf16[144,8192]{1,0:T(8,128)(2,1)S(1)}, bf16[144,8192]{1,0:T(8,128)(2,1)}, u32[]{:S(2)}, u32[]{:S(2)}) collective-permute-start(bf16[144,8192]{1,0:T(8,128)(2,1)S(1)} %bitcast.29), channel_id=1, source_target_pairs={{0,1},{1,0},{2,3},{3,2},{4,5},{5,4},{6,7},{7,6},{8,9},{9,8},{10,11... | collective-permute-start | bytes 7077896 | tf_op jit(solution)/shard_map/ppermute | solution.py:341
  74.0 0.1 broadcast_in_dim.40
  74.1 0.0 collective-permute-done.8
  74.2 0.0 collective-permute-done.9
  74.2 3.0 %collective-permute-start.11 = (bf16[48,8192]{1,0:T(8,128)(2,1)S(1)}, bf16[48,8192]{1,0:T(8,128)(2,1)}, u32[]{:S(2)}, u32[]{:S(2)}) collective-permute-start(bf16[48,8192]{1,0:T(8,128)(2,1)S(1)} %bitcast.31), channel_id=1, source_target_pairs={{0,1},{1,0},{2,3},{3,2},{4,5},{5,4},{6,7},{7,6},{8,9},{9,8},{10,11... | collective-permute-start | bytes 2359304 | tf_op jit(solution)/shard_map/ppermute | solution.py:341
  77.2 0.6 stack.23.place_ref
  77.8 1.6 collective-permute-done.11.other_b
  79.4 0.0 collective-permute-done.10.other_a
  79.4 16.6 %block_parts.1 = (bf16[16,24,2048]{2,1,0:T(8,128)(2,1)}, bf16[16,24,2048]{2,1,0:T(8,128)(2,1)}, bf16[2,7,8,32,128]{4,3,2,1,0:T(8,128)(2,1)}, bf16[2,7,8,32,128]{...) custom-call(s32[5]{0:T(128)} %stack.23.place_ref, ...), custom_call_target="tpu_custom_call" | custom-call | flops 1761607680 | bytes 16777216 | tf_op jit(solution)/shard_map/block_parts/pallas_call | solution.py:198
  96.1 2.3 %collective-permute-start.12 = (bf16[16,24,2048]{2,1,0:T(8,128)(2,1)}, bf16[16,24,2048]{2,1,0:T(8,128)(2,1)S(1)}, u32[]{:S(2)}, u32[]{:S(2)}) collective-permute-start(bf16[16,24,2048]{2,1,0:T(8,128)(2,1)} %get-tuple-element.18), channel_id=1, source_target_pairs={{0,1},{1,0},{2,3},{3,2},{4,5},{5,4},{6,7},{7,6},{8,9},{9,8},{10,11... | collective-permute-start | bytes 4718600 | tf_op jit(solution)/shard_map/ppermute | solution.py:319
  98.3 3.1 %collective-permute-start.13 = (bf16[2,7,8,32,128]{4,3,2,1,0:T(8,128)(2,1)}, bf16[2,7,8,32,128]{4,3,2,1,0:T(8,128)(2,1)S(1)}, u32[]{:S(2)}, u32[]{:S(2)}) collective-permute-start(bf16[2,7,8,32,128]{4,3,2,1,0:T(8,128)(2,1)} %get-tuple-element.20), channel_id=1, source_target_pairs={{0,128},{32,160},{64,192},{96,224},{128,0},{160,32},{192,64},{224,... | collective-permute-start | bytes 2752520 | tf_op jit(solution)/shard_map/ppermute | solution.py:311
  101.5 3.7 %collective-permute-start.15 = (bf16[2,7,8,32,128]{4,3,2,1,0:T(8,128)(2,1)}, bf16[2,7,8,32,128]{4,3,2,1,0:T(8,128)(2,1)S(1)}, u32[]{:S(2)}, u32[]{:S(2)}) collective-permute-start(bf16[2,7,8,32,128]{4,3,2,1,0:T(8,128)(2,1)} %get-tuple-element.24), channel_id=1, source_target_pairs={{0,384},{32,416},{64,448},{96,480},{128,256},{160,288},{192,320},{... | collective-permute-start | bytes 2752520 | tf_op jit(solution)/shard_map/ppermute | solution.py:312
  105.2 0.0 collective-permute-done.12.b_ref
  105.2 1.4 copy-done.5
  106.6 1.4 add_cores.1
  108.0 12.1 %all-to-all-start = ((bf16[16,24,2048]{2,1,0:T(8,128)(2,1)}), bf16[16,24,2048]{2,1,0:T(8,128)(2,1)S(1)}, u32[]{:S(2)}, u32[]{:S(2)}) async-start(bf16[16,24,2048]{2,1,0:T(8,128)(2,1)} %add_cores.1), calls=%async_computation | async-start | bytes 3145728 | tf_op jit(solution)/shard_map/all_to_all | solution.py:320
  120.0 2.2 %collective-permute-done.13.b_ref.up_a = bf16[2,7,8,32,128]{4,3,2,1,0:T(8,128)(2,1)S(1)} collective-permute-done((bf16[2,7,8,32,128]{4,3,2,1,0:T(8,128)(2,1)}, bf16[2,7,8,32,128]{4,3,2,1,0:T(8,128)(2,1)S(1)}, u32[]{:S(2)}, u32[]{:S(2)}) %collective-permute-start.13) | collective-permute-done | bytes 917536 | tf_op jit(solution)/shard_map/ppermute | solution.py:311
  122.2 1.0 copy-done.7
  123.3 0.1 add_up.1
  123.4 4.5 %collective-permute-start.14 = (bf16[7,8,32,128]{3,2,1,0:T(8,128)(2,1)S(1)}, bf16[7,8,32,128]{3,2,1,0:T(8,128)(2,1)S(1)}, u32[]{:S(2)}, u32[]{:S(2)}) collective-permute-start(bf16[7,8,32,128]{3,2,1,0:T(8,128)(2,1)S(1)} %add_up.1), channel_id=1, source_target_pairs={{0,384},{32,416},{64,448},{96,480},{128,256},{160,288},{192,320},{... | collective-permute-start | bytes 1376264 | tf_op jit(solution)/shard_map/ppermute | solution.py:313
  127.9 0.0 collective-permute-done.15.b_ref.down_b
  128.0 0.1 add_down.1
  128.1 2.1 %collective-permute-start.16 = (bf16[7,8,32,128]{3,2,1,0:T(8,128)(2,1)S(1)}, bf16[7,8,32,128]{3,2,1,0:T(8,128)(2,1)S(1)}, u32[]{:S(2)}, u32[]{:S(2)}) collective-permute-start(bf16[7,8,32,128]{3,2,1,0:T(8,128)(2,1)S(1)} %add_down.1), channel_id=1, source_target_pairs={{0,128},{32,160},{64,192},{96,224},{128,0},{160,32},{192,64},{224,... | collective-permute-start | bytes 1376264 | tf_op jit(solution)/shard_map/ppermute | solution.py:314
  130.1 7.5 %collective-permute-done.14.up_b = bf16[7,8,32,128]{3,2,1,0:T(8,128)(2,1)S(1)} collective-permute-done((bf16[7,8,32,128]{3,2,1,0:T(8,128)(2,1)S(1)}, bf16[7,8,32,128]{3,2,1,0:T(8,128)(2,1)S(1)}, u32[]{:S(2)}, u32[]{:S(2)}) %collective-permute-start.14) | collective-permute-done | bytes 458784 | tf_op jit(solution)/shard_map/ppermute | solution.py:313
  137.7 3.2 %collective-permute-done.16.down_a = bf16[7,8,32,128]{3,2,1,0:T(8,128)(2,1)S(1)} collective-permute-done((bf16[7,8,32,128]{3,2,1,0:T(8,128)(2,1)S(1)}, bf16[7,8,32,128]{3,2,1,0:T(8,128)(2,1)S(1)}, u32[]{:S(2)}, u32[]{:S(2)}) %collective-permute-start.16) | collective-permute-done | bytes 458784 | tf_op jit(solution)/shard_map/ppermute | solution.py:314
  140.9 1.9 %x_sum.1 = (bf16[2,7,64,128]{3,2,1,0:T(8,128)(2,1)S(1)}, bf16[2,7,64,128]{3,2,1,0:T(8,128)(2,1)}, bf16[2,7,64,128]{3,2,1,0:T(8,128)(2,1)}, bf16[2,7,64,128]{3,2,1,0:T(8,128)(2,1)}) custom-call(s32[5]{0:T(128)S(1)} %copy-done.4, bf16[7,8,32,128]{3,2,1,0:T(8,128)(2,1)S(1)} %copy-done, bf16[2,7,8,32,128]{4,3,2,1,0:T(8,128)(2,1)S(1)} %collective-permute-done.13.b_ref.up_a, ...), custom_call_target="tpu_custom_call" | custom-call | flops 2097152 | bytes 4194304 | tf_op jit(solution)/shard_map/x_sum/pallas_call | solution.py:227
  142.8 0.7 copy-done.2
  143.5 1.9 %collective-permute-start.18 = (bf16[2,7,64,128]{3,2,1,0:T(8,128)(2,1)}, bf16[2,7,64,128]{3,2,1,0:T(8,128)(2,1)S(1)}, u32[]{:S(2)}, u32[]{:S(2)}) collective-permute-start(bf16[2,7,64,128]{3,2,1,0:T(8,128)(2,1)} %get-tuple-element.28), channel_id=1, source_target_pairs={{0,64},{32,96},{64,0},{96,32},{128,192},{160,224},{192,128},{224,1... | collective-permute-start | bytes 688136 | tf_op jit(solution)/shard_map/ppermute | solution.py:353
  145.4 1.9 %collective-permute-start.19 = (bf16[2,7,64,128]{3,2,1,0:T(8,128)(2,1)}, bf16[2,7,64,128]{3,2,1,0:T(8,128)(2,1)S(1)}, u32[]{:S(2)}, u32[]{:S(2)}) collective-permute-start(bf16[2,7,64,128]{3,2,1,0:T(8,128)(2,1)} %get-tuple-element.29), channel_id=1, source_target_pairs={{0,96},{32,64},{64,32},{96,0},{128,224},{160,192},{192,160},{224,1... | collective-permute-start | bytes 688136 | tf_op jit(solution)/shard_map/ppermute | solution.py:353
  147.3 5.4 %collective-permute-start.20 = (bf16[2,7,64,128]{3,2,1,0:T(8,128)(2,1)}, bf16[2,7,64,128]{3,2,1,0:T(8,128)(2,1)S(1)}, u32[]{:S(2)}, u32[]{:S(2)}) collective-permute-start(bf16[2,7,64,128]{3,2,1,0:T(8,128)(2,1)} %get-tuple-element.30), channel_id=1, source_target_pairs={{0,32},{32,0},{64,96},{96,64},{128,160},{160,128},{192,224},{224,1... | collective-permute-start | bytes 688136 | tf_op jit(solution)/shard_map/ppermute | solution.py:353
  152.8 8.9 %all-to-all-done.parts_ref = bf16[16,24,2048]{2,1,0:T(8,128)(2,1)S(1)} async-done(((bf16[16,24,2048]{2,1,0:T(8,128)(2,1)}), bf16[16,24,2048]{2,1,0:T(8,128)(2,1)S(1)}, u32[]{:S(2)}, u32[]{:S(2)}) %all-to-all-start) | async-done | bytes 1572896 | tf_op jit(solution)/shard_map/all_to_all | solution.py:320
  161.7 0.4 total_terms.1
  162.2 4.2 %collective-permute-start.17 = (bf16[6,4096]{1,0:T(8,128)(2,1)S(1)}, bf16[6,4096]{1,0:T(8,128)(2,1)S(1)}, u32[]{:S(2)}, u32[]{:S(2)}) collective-permute-start(bf16[6,4096]{1,0:T(8,128)(2,1)S(1)} %broadcast_select_fusion.6), channel_id=1, source_target_pairs={{0,1},{1,0},{2,3},{3,2},{4,5},{5,4},{6,7},{7,6},{8,9},{9,8},{10,11... | collective-permute-start | bytes 147464 | tf_op jit(solution)/shard_map/ppermute | solution.py:328
  166.4 5.2 %collective-permute-done.18 = bf16[2,7,64,128]{3,2,1,0:T(8,128)(2,1)S(1)} collective-permute-done((bf16[2,7,64,128]{3,2,1,0:T(8,128)(2,1)}, bf16[2,7,64,128]{3,2,1,0:T(8,128)(2,1)S(1)}, u32[]{:S(2)}, u32[]{:S(2)}) %collective-permute-start.18) | collective-permute-done | bytes 229408 | tf_op jit(solution)/shard_map/ppermute | solution.py:353
  171.6 9.8 %collective-permute-done.19 = bf16[2,7,64,128]{3,2,1,0:T(8,128)(2,1)S(1)} collective-permute-done((bf16[2,7,64,128]{3,2,1,0:T(8,128)(2,1)}, bf16[2,7,64,128]{3,2,1,0:T(8,128)(2,1)S(1)}, u32[]{:S(2)}, u32[]{:S(2)}) %collective-permute-start.19) | collective-permute-done | bytes 229408 | tf_op jit(solution)/shard_map/ppermute | solution.py:353
  181.5 0.0 collective-permute-done.20
  181.5 0.1 add_convert_fusion
  181.6 0.7 slice_bitcast_fusion
  182.3 0.0 collective-permute-done.17
  182.4 0.7 pad_maximum_fusion.2
  (32 shorter events, 0.5 us)
Async XLA Ops:
  1.6 3.6 %collective-permute-start = (bf16[6,8192]{1,0:T(8,128)(2,1)S(1)}, bf16[6,8192]{1,0:T(8,128)(2,1)S(1)}, u32[]{:S(2)}, u32[]{:S(2)}) collective-permute-start(bf16[6,8192]{1,0:T(8,128)(2,1)S(1)} %broadcast_select_fusion.2), channel_id=1, source_target_pairs={{0,1},{1,0},{2,3},{3,2},{4,5},{5,4},{6,7},{7,6},{8,9},{9,8},{10,11... | collective-permute-start | bytes 294920 | tf_op jit(solution)/shard_map/ppermute | solution.py:282
  6.2 18.4 %collective-permute-start.1 = (bf16[24,4096]{1,0:T(8,128)(2,1)S(1)}, bf16[24,4096]{1,0:T(8,128)(2,1)S(1)}, u32[]{:S(2)}, u32[]{:S(2)}) collective-permute-start(bf16[24,4096]{1,0:T(8,128)(2,1)S(1)} %pad_maximum_fusion), channel_id=1, source_target_pairs={{0,16},{1,17},{2,18},{3,19},{4,20},{5,21},{6,22},{7,23},{8,24},{9,... | collective-permute-start | bytes 589832 | tf_op jit(solution)/shard_map/ppermute | solution.py:286
  24.8 13.2 %collective-permute-start.3 = (bf16[24,8192]{1,0:T(8,128)(2,1)S(1)}, bf16[24,8192]{1,0:T(8,128)(2,1)S(1)}, u32[]{:S(2)}, u32[]{:S(2)}) collective-permute-start(bf16[24,8192]{1,0:T(8,128)(2,1)S(1)} %maximum_maximum_fusion), channel_id=1, source_target_pairs={{0,14},{1,15},{2,0},{3,1},{4,2},{5,3},{6,4},{7,5},{8,6},{9,7},{10,... | collective-permute-start | bytes 1179656 | tf_op jit(solution)/shard_map/ppermute | solution.py:300
  27.8 12.2 %collective-permute-start.2 = (bf16[24,8192]{1,0:T(8,128)(2,1)S(1)}, bf16[24,8192]{1,0:T(8,128)(2,1)S(1)}, u32[]{:S(2)}, u32[]{:S(2)}) collective-permute-start(bf16[24,8192]{1,0:T(8,128)(2,1)S(1)} %maximum_maximum_fusion), channel_id=1, source_target_pairs={{0,2},{1,3},{2,4},{3,5},{4,6},{5,7},{6,8},{7,9},{8,10},{9,11},{10,... | collective-permute-start | bytes 1179656 | tf_op jit(solution)/shard_map/ppermute | solution.py:299
  38.0 12.3 %collective-permute-start.5 = (bf16[24,8192]{1,0:T(8,128)(2,1)S(1)}, bf16[24,8192]{1,0:T(8,128)(2,1)S(1)}, u32[]{:S(2)}, u32[]{:S(2)}) collective-permute-start(bf16[24,8192]{1,0:T(8,128)(2,1)S(1)} %collective-permute-done.3), channel_id=1, source_target_pairs={{0,14},{1,15},{2,0},{3,1},{4,2},{5,3},{6,4},{7,5},{8,6},{9,7},{10,... | collective-permute-start | bytes 1179656 | tf_op jit(solution)/shard_map/ppermute | solution.py:300
  40.0 12.3 %collective-permute-start.4 = (bf16[24,8192]{1,0:T(8,128)(2,1)S(1)}, bf16[24,8192]{1,0:T(8,128)(2,1)S(1)}, u32[]{:S(2)}, u32[]{:S(2)}) collective-permute-start(bf16[24,8192]{1,0:T(8,128)(2,1)S(1)} %collective-permute-done.2), channel_id=1, source_target_pairs={{0,2},{1,3},{2,4},{3,5},{4,6},{5,7},{6,8},{7,9},{8,10},{9,11},{10,... | collective-permute-start | bytes 1179656 | tf_op jit(solution)/shard_map/ppermute | solution.py:299
  50.3 11.4 %collective-permute-start.7 = (bf16[24,8192]{1,0:T(8,128)(2,1)S(1)}, bf16[24,8192]{1,0:T(8,128)(2,1)S(1)}, u32[]{:S(2)}, u32[]{:S(2)}) collective-permute-start(bf16[24,8192]{1,0:T(8,128)(2,1)S(1)} %collective-permute-done.5), channel_id=1, source_target_pairs={{0,14},{1,15},{2,0},{3,1},{4,2},{5,3},{6,4},{7,5},{8,6},{9,7},{10,... | collective-permute-start | bytes 1179656 | tf_op jit(solution)/shard_map/ppermute | solution.py:300
  52.3 11.4 %collective-permute-start.6 = (bf16[24,8192]{1,0:T(8,128)(2,1)S(1)}, bf16[24,8192]{1,0:T(8,128)(2,1)S(1)}, u32[]{:S(2)}, u32[]{:S(2)}) collective-permute-start(bf16[24,8192]{1,0:T(8,128)(2,1)S(1)} %collective-permute-done.4), channel_id=1, source_target_pairs={{0,2},{1,3},{2,4},{3,5},{4,6},{5,7},{6,8},{7,9},{8,10},{9,11},{10,... | collective-permute-start | bytes 1179656 | tf_op jit(solution)/shard_map/ppermute | solution.py:299
  61.7 12.5 %collective-permute-start.9 = (bf16[24,4096]{1,0:T(8,128)(2,1)S(1)}, bf16[24,4096]{1,0:T(8,128)(2,1)S(1)}, u32[]{:S(2)}, u32[]{:S(2)}) collective-permute-start(bf16[24,4096]{1,0:T(8,128)(2,1)S(1)} %slice.55), channel_id=1, source_target_pairs={{0,14},{1,15},{2,0},{3,1},{4,2},{5,3},{6,4},{7,5},{8,6},{9,7},{10,... | collective-permute-start | bytes 589832 | tf_op jit(solution)/shard_map/ppermute | solution.py:306
  63.7 10.5 %collective-permute-start.8 = (bf16[24,4096]{1,0:T(8,128)(2,1)S(1)}, bf16[24,4096]{1,0:T(8,128)(2,1)S(1)}, u32[]{:S(2)}, u32[]{:S(2)}) collective-permute-start(bf16[24,4096]{1,0:T(8,128)(2,1)S(1)} %slice.54), channel_id=1, source_target_pairs={{0,2},{1,3},{2,4},{3,5},{4,6},{5,7},{6,8},{7,9},{8,10},{9,11},{10,... | collective-permute-start | bytes 589832 | tf_op jit(solution)/shard_map/ppermute | solution.py:305
  68.3 11.1 %copy-start.8 = (bf16[6,24,8192]{2,1,0:T(8,128)(2,1)}, bf16[6,24,8192]{2,1,0:T(8,128)(2,1)S(1)}, u32[]{:S(2)}) copy-start(bf16[6,24,8192]{2,1,0:T(8,128)(2,1)S(1)} %bitcast_dynamic-update-slice_fusion.1) | copy-start | bytes 7077892
  68.3 11.1 %collective-permute-start.10 = (bf16[144,8192]{1,0:T(8,128)(2,1)S(1)}, bf16[144,8192]{1,0:T(8,128)(2,1)}, u32[]{:S(2)}, u32[]{:S(2)}) collective-permute-start(bf16[144,8192]{1,0:T(8,128)(2,1)S(1)} %bitcast.29), channel_id=1, source_target_pairs={{0,1},{1,0},{2,3},{3,2},{4,5},{5,4},{6,7},{7,6},{8,9},{9,8},{10,11... | collective-permute-start | bytes 7077896 | tf_op jit(solution)/shard_map/ppermute | solution.py:341
  74.2 5.2 %copy-start.9 = (bf16[2,24,8192]{2,1,0:T(8,128)(2,1)}, bf16[2,24,8192]{2,1,0:T(8,128)(2,1)S(1)}, u32[]{:S(2)}) copy-start(bf16[2,24,8192]{2,1,0:T(8,128)(2,1)S(1)} %bitcast_dynamic-update-slice_fusion.7) | copy-start | bytes 2359300
  74.2 5.2 %collective-permute-start.11 = (bf16[48,8192]{1,0:T(8,128)(2,1)S(1)}, bf16[48,8192]{1,0:T(8,128)(2,1)}, u32[]{:S(2)}, u32[]{:S(2)}) collective-permute-start(bf16[48,8192]{1,0:T(8,128)(2,1)S(1)} %bitcast.31), channel_id=1, source_target_pairs={{0,1},{1,0},{2,3},{3,2},{4,5},{5,4},{6,7},{7,6},{8,9},{9,8},{10,11... | collective-permute-start | bytes 2359304 | tf_op jit(solution)/shard_map/ppermute | solution.py:341
  96.1 9.1 %collective-permute-start.12 = (bf16[16,24,2048]{2,1,0:T(8,128)(2,1)}, bf16[16,24,2048]{2,1,0:T(8,128)(2,1)S(1)}, u32[]{:S(2)}, u32[]{:S(2)}) collective-permute-start(bf16[16,24,2048]{2,1,0:T(8,128)(2,1)} %get-tuple-element.18), channel_id=1, source_target_pairs={{0,1},{1,0},{2,3},{3,2},{4,5},{5,4},{6,7},{7,6},{8,9},{9,8},{10,11... | collective-permute-start | bytes 4718600 | tf_op jit(solution)/shard_map/ppermute | solution.py:319
  98.3 23.9 %collective-permute-start.13 = (bf16[2,7,8,32,128]{4,3,2,1,0:T(8,128)(2,1)}, bf16[2,7,8,32,128]{4,3,2,1,0:T(8,128)(2,1)S(1)}, u32[]{:S(2)}, u32[]{:S(2)}) collective-permute-start(bf16[2,7,8,32,128]{4,3,2,1,0:T(8,128)(2,1)} %get-tuple-element.20), channel_id=1, source_target_pairs={{0,128},{32,160},{64,192},{96,224},{128,0},{160,32},{192,64},{224,... | collective-permute-start | bytes 2752520 | tf_op jit(solution)/shard_map/ppermute | solution.py:311
  101.5 26.5 %collective-permute-start.15 = (bf16[2,7,8,32,128]{4,3,2,1,0:T(8,128)(2,1)}, bf16[2,7,8,32,128]{4,3,2,1,0:T(8,128)(2,1)S(1)}, u32[]{:S(2)}, u32[]{:S(2)}) collective-permute-start(bf16[2,7,8,32,128]{4,3,2,1,0:T(8,128)(2,1)} %get-tuple-element.24), channel_id=1, source_target_pairs={{0,384},{32,416},{64,448},{96,480},{128,256},{160,288},{192,320},{... | collective-permute-start | bytes 2752520 | tf_op jit(solution)/shard_map/ppermute | solution.py:312
  105.2 1.4 copy-start.5
  108.0 53.7 %all-to-all-start = ((bf16[16,24,2048]{2,1,0:T(8,128)(2,1)}), bf16[16,24,2048]{2,1,0:T(8,128)(2,1)S(1)}, u32[]{:S(2)}, u32[]{:S(2)}) async-start(bf16[16,24,2048]{2,1,0:T(8,128)(2,1)} %add_cores.1), calls=%async_computation | async-start | bytes 3145728 | tf_op jit(solution)/shard_map/all_to_all | solution.py:320
  122.2 1.0 copy-start.7
  123.3 4.7 %copy-start.6 = (bf16[7,8,32,128]{3,2,1,0:T(8,128)(2,1)S(1)}, bf16[7,8,32,128]{3,2,1,0:T(8,128)(2,1)}, u32[]{:S(2)}) copy-start(bf16[7,8,32,128]{3,2,1,0:T(8,128)(2,1)} %get-tuple-element.23.a_ref) | copy-start | bytes 1376260
  123.4 14.3 %collective-permute-start.14 = (bf16[7,8,32,128]{3,2,1,0:T(8,128)(2,1)S(1)}, bf16[7,8,32,128]{3,2,1,0:T(8,128)(2,1)S(1)}, u32[]{:S(2)}, u32[]{:S(2)}) collective-permute-start(bf16[7,8,32,128]{3,2,1,0:T(8,128)(2,1)S(1)} %add_up.1), channel_id=1, source_target_pairs={{0,384},{32,416},{64,448},{96,480},{128,256},{160,288},{192,320},{... | collective-permute-start | bytes 1376264 | tf_op jit(solution)/shard_map/ppermute | solution.py:313
  127.9 12.9 %copy-start = (bf16[7,8,32,128]{3,2,1,0:T(8,128)(2,1)S(1)}, bf16[7,8,32,128]{3,2,1,0:T(8,128)(2,1)}, u32[]{:S(2)}) copy-start(bf16[7,8,32,128]{3,2,1,0:T(8,128)(2,1)} %get-tuple-element.19.up_own) | copy-start | bytes 1376260
  127.9 12.9 %copy-start.1 = (bf16[7,8,32,128]{3,2,1,0:T(8,128)(2,1)S(1)}, bf16[7,8,32,128]{3,2,1,0:T(8,128)(2,1)}, u32[]{:S(2)}) copy-start(bf16[7,8,32,128]{3,2,1,0:T(8,128)(2,1)} %get-tuple-element.22.down_own) | copy-start | bytes 1376260
  128.0 12.9 %copy-start.4 = (s32[5]{0:T(128)S(1)}, s32[5]{0:T(128)}, u32[]{:S(2)}) copy-start(s32[5]{0:T(128)} %stack.23.place_ref) | copy-start | bytes 64
  128.1 12.8 %collective-permute-start.16 = (bf16[7,8,32,128]{3,2,1,0:T(8,128)(2,1)S(1)}, bf16[7,8,32,128]{3,2,1,0:T(8,128)(2,1)S(1)}, u32[]{:S(2)}, u32[]{:S(2)}) collective-permute-start(bf16[7,8,32,128]{3,2,1,0:T(8,128)(2,1)S(1)} %add_down.1), channel_id=1, source_target_pairs={{0,128},{32,160},{64,192},{96,224},{128,0},{160,32},{192,64},{224,... | collective-permute-start | bytes 1376264 | tf_op jit(solution)/shard_map/ppermute | solution.py:314
  142.8 0.7 copy-start.2
  143.5 28.1 %collective-permute-start.18 = (bf16[2,7,64,128]{3,2,1,0:T(8,128)(2,1)}, bf16[2,7,64,128]{3,2,1,0:T(8,128)(2,1)S(1)}, u32[]{:S(2)}, u32[]{:S(2)}) collective-permute-start(bf16[2,7,64,128]{3,2,1,0:T(8,128)(2,1)} %get-tuple-element.28), channel_id=1, source_target_pairs={{0,64},{32,96},{64,0},{96,32},{128,192},{160,224},{192,128},{224,1... | collective-permute-start | bytes 688136 | tf_op jit(solution)/shard_map/ppermute | solution.py:353
  145.4 36.1 %collective-permute-start.19 = (bf16[2,7,64,128]{3,2,1,0:T(8,128)(2,1)}, bf16[2,7,64,128]{3,2,1,0:T(8,128)(2,1)S(1)}, u32[]{:S(2)}, u32[]{:S(2)}) collective-permute-start(bf16[2,7,64,128]{3,2,1,0:T(8,128)(2,1)} %get-tuple-element.29), channel_id=1, source_target_pairs={{0,96},{32,64},{64,32},{96,0},{128,224},{160,192},{192,160},{224,1... | collective-permute-start | bytes 688136 | tf_op jit(solution)/shard_map/ppermute | solution.py:353
  147.3 34.1 %collective-permute-start.20 = (bf16[2,7,64,128]{3,2,1,0:T(8,128)(2,1)}, bf16[2,7,64,128]{3,2,1,0:T(8,128)(2,1)S(1)}, u32[]{:S(2)}, u32[]{:S(2)}) collective-permute-start(bf16[2,7,64,128]{3,2,1,0:T(8,128)(2,1)} %get-tuple-element.30), channel_id=1, source_target_pairs={{0,32},{32,0},{64,96},{96,64},{128,160},{160,128},{192,224},{224,1... | collective-permute-start | bytes 688136 | tf_op jit(solution)/shard_map/ppermute | solution.py:353
  161.7 19.8 %copy-start.3 = (bf16[2,7,64,128]{3,2,1,0:T(8,128)(2,1)S(1)}, bf16[2,7,64,128]{3,2,1,0:T(8,128)(2,1)}, u32[]{:S(2)}) copy-start(bf16[2,7,64,128]{3,2,1,0:T(8,128)(2,1)} %copy-done.2) | copy-start | bytes 688132
  162.2 20.1 %collective-permute-start.17 = (bf16[6,4096]{1,0:T(8,128)(2,1)S(1)}, bf16[6,4096]{1,0:T(8,128)(2,1)S(1)}, u32[]{:S(2)}, u32[]{:S(2)}) collective-permute-start(bf16[6,4096]{1,0:T(8,128)(2,1)S(1)} %broadcast_select_fusion.6), channel_id=1, source_target_pairs={{0,1},{1,0},{2,3},{3,2},{4,5},{5,4},{6,7},{7,6},{8,9},{9,8},{10,11... | collective-permute-start | bytes 147464 | tf_op jit(solution)/shard_map/ppermute | solution.py:328

commit v4 on v3

--- a/solution.py
+++ b/solution.py
@@ -119,8 +119,17 @@
                 at = pl.multiple_of(upi_ref[j, slot] * block, block)
                 acc_ref[:, pl.ds(at, block)] += terms[:, (slot - k) * block:(slot - k + 1) * block]
 
-    @pl.loop(0, hidden)
-    def _(j):
+    stores = []
+
+    def store(first, last, at):
+        here = pl.ds(first, last - first)
+        pairs = [(parts_ref.at[0:2, here], even_out.at[:, here]), (parts_ref.at[2:4, here], odd_out.at[:, here])]
+        pairs += [(parts_ref.at[4 + n, here], out.at[here]) for n, out in enumerate((up0, up3, down0, down1))]
+        for n, pair in enumerate(pairs):
+            stores.append(pltpu.make_async_copy(*pair, out_sem.at[at, n]))
+            stores[-1].start()
+
+    for j in range(hidden):
         pg = pg_ref[j]
         act = act_ref[j]
         for k in range(0, slots, 2):
@@ -136,12 +145,9 @@
             row = pl.multiple_of((place_ref[1] ^ q) * share, share)
             parts_ref[UP_PLACE[q], j] = us_ref[:, pl.ds(row, share), :]
             parts_ref[DOWN_PLACE[q], j] = ds_ref[:, pl.ds(row, share), :]
-
-    pairs = [(parts_ref.at[0:2], even_out), (parts_ref.at[2:4], odd_out)]
-    pairs += [(parts_ref.at[4 + n], out) for n, out in enumerate((up0, up3, down0, down1))]
-    stores = [pltpu.make_async_copy(*pair, out_sem.at[n]) for n, pair in enumerate(pairs)]
-    for store in stores:
-        store.start()
+        if j == hidden // 2:
+            store(0, j + 1, 0)
+    store(hidden // 2 + 1, hidden, 1)
 
     z_hi = place_ref[4]
     for out, core in ((send_ref, 1 - place_ref[0]), (keep_ref, place_ref[0])):
@@ -155,8 +161,8 @@
             half = rows // 2
             out[z_hi * Y + owner] = jnp.concatenate([a[:half], b[:half]], axis=0).astype(jnp.bfloat16)
             out[(1 - z_hi) * Y + owner] = jnp.concatenate([a[half:], b[half:]], axis=0).astype(jnp.bfloat16)
-    for store in stores:
-        store.wait()
+    for copy in stores:
+        copy.wait()
 
 
 def x_sum_kernel(place_ref, up_own, up_a, up_b, down_own, down_a, down_b, *refs):
@@ -213,7 +219,7 @@
             pltpu.VMEM((slots, block, block), jnp.bfloat16),
             pltpu.VMEM((slots, block, block), jnp.bfloat16),
             pltpu.SemaphoreType.DMA((4, hidden)),
-            pltpu.SemaphoreType.DMA((2 * X,)),
+            pltpu.SemaphoreType.DMA((2, 6)),
         ],
         compiler_params=pltpu.CompilerParams(vmem_limit_bytes=58 * 2**20),
         cost_estimate=pl.CostEstimate(flops=flops, bytes_accessed=16 * 2**20, transcendentals=0),

time: 184 us -> 183 us (level)
  no operation moved by 1% of the time
where the time goes in v4:
time: 183 us; the launch traced here: 182 us
  starting transfers between devices  87.4 us (48%)
  waiting for transfers between devices  65.9 us (36%)
  Pallas kernels  19.2 us (10%)
  local copies, waits for them, and re-layouts  5.12 us (3%)
  other arithmetic  3.03 us (2%)
    ppermute x3, waiting for transfers between devices, gather_rows(): down = lax.ppermute(down, 'tensor', Y_DOWN)  16.9 us
    pallas_call x1, Pallas kernels, block_parts(): pl.pallas_call(functools.partial(block_kernel, factor), in_specs=[SMEM] *...  15.3 us
    ppermute x3, waiting for transfers between devices, local(): lax.ppermute(pieces[r], 'seq', Z_TRADE[r])  15 us
    ppermute x3, starting transfers between devices, gather_rows(): up = lax.ppermute(up, 'tensor', Y_UP)  12.7 us
    all_to_all x1, starting transfers between devices, reduce_inputs(): lax.all_to_all(part, 'tensor', 0, 0, axis_index_groups=ROW_GROUPS, tiled=...  12 us
    ppermute x1, waiting for transfers between devices, gather_rows(): other = lax.ppermute(pair, 'tensor', Z_PARTNER)  9.58 us
    ppermute x3, starting transfers between devices, local(): lax.ppermute(pieces[r], 'seq', Z_TRADE[r])  9.26 us
    ppermute x1, starting transfers between devices, gather_rows(): other = lax.ppermute(pair, 'tensor', Z_PARTNER)  8.84 us
  transfers between devices with their start and end apart: 22, of which 12 were waited for; matrix products, arithmetic and copies ran while one was open for 1% of the time, Pallas kernels for 2%

profile of v4, /device:TPU:185, one launch (start us, length us, event | category | flops | bytes accessed | tf_op | source)
XLA Modules:
  0.0 181.8 jit_solution(17271299872235348230)
XLA Ops:
  0.6 0.9 broadcast_select_fusion.2
  1.6 2.6 %collective-permute-start = (bf16[6,8192]{1,0:T(8,128)(2,1)S(1)}, bf16[6,8192]{1,0:T(8,128)(2,1)S(1)}, u32[]{:S(2)}, u32[]{:S(2)}) collective-permute-start(bf16[6,8192]{1,0:T(8,128)(2,1)S(1)} %broadcast_select_fusion.2), channel_id=1, source_target_pairs={{0,1},{1,0},{2,3},{3,2},{4,5},{5,4},{6,7},{7,6},{8,9},{9,8},{10,11... | collective-permute-start | bytes 294920 | tf_op jit(solution)/shard_map/ppermute | solution.py:288
  4.2 1.0 collective-permute-done
  5.1 0.9 broadcast_select_fusion.1
  6.1 0.1 fusion
  6.2 0.1 pad_maximum_fusion
  6.2 8.8 %collective-permute-start.1 = (bf16[24,4096]{1,0:T(8,128)(2,1)S(1)}, bf16[24,4096]{1,0:T(8,128)(2,1)S(1)}, u32[]{:S(2)}, u32[]{:S(2)}) collective-permute-start(bf16[24,4096]{1,0:T(8,128)(2,1)S(1)} %pad_maximum_fusion), channel_id=1, source_target_pairs={{0,16},{1,17},{2,18},{3,19},{4,20},{5,21},{6,22},{7,23},{8,24},{9,... | collective-permute-start | bytes 589832 | tf_op jit(solution)/shard_map/ppermute | solution.py:292
  15.1 9.6 %collective-permute-done.1 = bf16[24,4096]{1,0:T(8,128)(2,1)S(1)} collective-permute-done((bf16[24,4096]{1,0:T(8,128)(2,1)S(1)}, bf16[24,4096]{1,0:T(8,128)(2,1)S(1)}, u32[]{:S(2)}, u32[]{:S(2)}) %collective-permute-start.1) | collective-permute-done | bytes 196640 | tf_op jit(solution)/shard_map/ppermute | solution.py:292
  24.7 0.1 maximum_maximum_fusion
  24.8 3.0 %collective-permute-start.3 = (bf16[24,8192]{1,0:T(8,128)(2,1)S(1)}, bf16[24,8192]{1,0:T(8,128)(2,1)S(1)}, u32[]{:S(2)}, u32[]{:S(2)}) collective-permute-start(bf16[24,8192]{1,0:T(8,128)(2,1)S(1)} %maximum_maximum_fusion), channel_id=1, source_target_pairs={{0,14},{1,15},{2,0},{3,1},{4,2},{5,3},{6,4},{7,5},{8,6},{9,7},{10,... | collective-permute-start | bytes 1179656 | tf_op jit(solution)/shard_map/ppermute | solution.py:306
  27.8 3.5 %collective-permute-start.2 = (bf16[24,8192]{1,0:T(8,128)(2,1)S(1)}, bf16[24,8192]{1,0:T(8,128)(2,1)S(1)}, u32[]{:S(2)}, u32[]{:S(2)}) collective-permute-start(bf16[24,8192]{1,0:T(8,128)(2,1)S(1)} %maximum_maximum_fusion), channel_id=1, source_target_pairs={{0,2},{1,3},{2,4},{3,5},{4,6},{5,7},{6,8},{7,9},{8,10},{9,11},{10,... | collective-permute-start | bytes 1179656 | tf_op jit(solution)/shard_map/ppermute | solution.py:305
  31.3 0.2 broadcast_in_dim.33
  31.6 6.4 %collective-permute-done.3 = bf16[24,8192]{1,0:T(8,128)(2,1)S(1)} collective-permute-done((bf16[24,8192]{1,0:T(8,128)(2,1)S(1)}, bf16[24,8192]{1,0:T(8,128)(2,1)S(1)}, u32[]{:S(2)}, u32[]{:S(2)}) %collective-permute-start.3) | collective-permute-done | bytes 393248 | tf_op jit(solution)/shard_map/ppermute | solution.py:306
  38.0 1.9 %collective-permute-start.5 = (bf16[24,8192]{1,0:T(8,128)(2,1)S(1)}, bf16[24,8192]{1,0:T(8,128)(2,1)S(1)}, u32[]{:S(2)}, u32[]{:S(2)}) collective-permute-start(bf16[24,8192]{1,0:T(8,128)(2,1)S(1)} %collective-permute-done.3), channel_id=1, source_target_pairs={{0,14},{1,15},{2,0},{3,1},{4,2},{5,3},{6,4},{7,5},{8,6},{9,7},{10,... | collective-permute-start | bytes 1179656 | tf_op jit(solution)/shard_map/ppermute | solution.py:306
  40.0 0.0 collective-permute-done.2
  40.0 4.6 %collective-permute-start.4 = (bf16[24,8192]{1,0:T(8,128)(2,1)S(1)}, bf16[24,8192]{1,0:T(8,128)(2,1)S(1)}, u32[]{:S(2)}, u32[]{:S(2)}) collective-permute-start(bf16[24,8192]{1,0:T(8,128)(2,1)S(1)} %collective-permute-done.2), channel_id=1, source_target_pairs={{0,2},{1,3},{2,4},{3,5},{4,6},{5,7},{6,8},{7,9},{8,10},{9,11},{10,... | collective-permute-start | bytes 1179656 | tf_op jit(solution)/shard_map/ppermute | solution.py:305
  44.6 5.7 %collective-permute-done.5 = bf16[24,8192]{1,0:T(8,128)(2,1)S(1)} collective-permute-done((bf16[24,8192]{1,0:T(8,128)(2,1)S(1)}, bf16[24,8192]{1,0:T(8,128)(2,1)S(1)}, u32[]{:S(2)}, u32[]{:S(2)}) %collective-permute-start.5) | collective-permute-done | bytes 393248 | tf_op jit(solution)/shard_map/ppermute | solution.py:306
  50.3 1.9 %collective-permute-start.7 = (bf16[24,8192]{1,0:T(8,128)(2,1)S(1)}, bf16[24,8192]{1,0:T(8,128)(2,1)S(1)}, u32[]{:S(2)}, u32[]{:S(2)}) collective-permute-start(bf16[24,8192]{1,0:T(8,128)(2,1)S(1)} %collective-permute-done.5), channel_id=1, source_target_pairs={{0,14},{1,15},{2,0},{3,1},{4,2},{5,3},{6,4},{7,5},{8,6},{9,7},{10,... | collective-permute-start | bytes 1179656 | tf_op jit(solution)/shard_map/ppermute | solution.py:306
  52.2 0.0 collective-permute-done.4
  52.3 4.6 %collective-permute-start.6 = (bf16[24,8192]{1,0:T(8,128)(2,1)S(1)}, bf16[24,8192]{1,0:T(8,128)(2,1)S(1)}, u32[]{:S(2)}, u32[]{:S(2)}) collective-permute-start(bf16[24,8192]{1,0:T(8,128)(2,1)S(1)} %collective-permute-done.4), channel_id=1, source_target_pairs={{0,2},{1,3},{2,4},{3,5},{4,6},{5,7},{6,8},{7,9},{8,10},{9,11},{10,... | collective-permute-start | bytes 1179656 | tf_op jit(solution)/shard_map/ppermute | solution.py:305
  56.9 4.8 %collective-permute-done.7 = bf16[24,8192]{1,0:T(8,128)(2,1)S(1)} collective-permute-done((bf16[24,8192]{1,0:T(8,128)(2,1)S(1)}, bf16[24,8192]{1,0:T(8,128)(2,1)S(1)}, u32[]{:S(2)}, u32[]{:S(2)}) %collective-permute-start.7) | collective-permute-done | bytes 393248 | tf_op jit(solution)/shard_map/ppermute | solution.py:306
  61.7 1.9 %collective-permute-start.9 = (bf16[24,4096]{1,0:T(8,128)(2,1)S(1)}, bf16[24,4096]{1,0:T(8,128)(2,1)S(1)}, u32[]{:S(2)}, u32[]{:S(2)}) collective-permute-start(bf16[24,4096]{1,0:T(8,128)(2,1)S(1)} %slice.55), channel_id=1, source_target_pairs={{0,14},{1,15},{2,0},{3,1},{4,2},{5,3},{6,4},{7,5},{8,6},{9,7},{10,... | collective-permute-start | bytes 589832 | tf_op jit(solution)/shard_map/ppermute | solution.py:312
  63.7 0.0 collective-permute-done.6
  63.7 4.6 %collective-permute-start.8 = (bf16[24,4096]{1,0:T(8,128)(2,1)S(1)}, bf16[24,4096]{1,0:T(8,128)(2,1)S(1)}, u32[]{:S(2)}, u32[]{:S(2)}) collective-permute-start(bf16[24,4096]{1,0:T(8,128)(2,1)S(1)} %slice.54), channel_id=1, source_target_pairs={{0,2},{1,3},{2,4},{3,5},{4,6},{5,7},{6,8},{7,9},{8,10},{9,11},{10,... | collective-permute-start | bytes 589832 | tf_op jit(solution)/shard_map/ppermute | solution.py:311
  68.3 5.7 %collective-permute-start.10 = (bf16[144,8192]{1,0:T(8,128)(2,1)S(1)}, bf16[144,8192]{1,0:T(8,128)(2,1)}, u32[]{:S(2)}, u32[]{:S(2)}) collective-permute-start(bf16[144,8192]{1,0:T(8,128)(2,1)S(1)} %bitcast.29), channel_id=1, source_target_pairs={{0,1},{1,0},{2,3},{3,2},{4,5},{5,4},{6,7},{7,6},{8,9},{9,8},{10,11... | collective-permute-start | bytes 7077896 | tf_op jit(solution)/shard_map/ppermute | solution.py:347
  74.0 0.1 broadcast_in_dim.40
  74.1 0.0 collective-permute-done.8
  74.2 0.0 collective-permute-done.9
  74.2 3.0 %collective-permute-start.11 = (bf16[48,8192]{1,0:T(8,128)(2,1)S(1)}, bf16[48,8192]{1,0:T(8,128)(2,1)}, u32[]{:S(2)}, u32[]{:S(2)}) collective-permute-start(bf16[48,8192]{1,0:T(8,128)(2,1)S(1)} %bitcast.31), channel_id=1, source_target_pairs={{0,1},{1,0},{2,3},{3,2},{4,5},{5,4},{6,7},{7,6},{8,9},{9,8},{10,11... | collective-permute-start | bytes 2359304 | tf_op jit(solution)/shard_map/ppermute | solution.py:347
  77.2 0.6 stack.23.place_ref
  77.8 1.6 collective-permute-done.11.other_b
  79.4 0.0 collective-permute-done.10.other_a
  79.4 15.3 %block_parts.1 = (bf16[16,24,2048]{2,1,0:T(8,128)(2,1)}, bf16[16,24,2048]{2,1,0:T(8,128)(2,1)}, bf16[2,7,8,32,128]{4,3,2,1,0:T(8,128)(2,1)}, bf16[2,7,8,32,128]{...) custom-call(s32[5]{0:T(128)} %stack.23.place_ref, ...), custom_call_target="tpu_custom_call" | custom-call | flops 1761607680 | bytes 16777216 | tf_op jit(solution)/shard_map/block_parts/pallas_call | solution.py:204
  94.8 2.3 %collective-permute-start.12 = (bf16[16,24,2048]{2,1,0:T(8,128)(2,1)}, bf16[16,24,2048]{2,1,0:T(8,128)(2,1)S(1)}, u32[]{:S(2)}, u32[]{:S(2)}) collective-permute-start(bf16[16,24,2048]{2,1,0:T(8,128)(2,1)} %get-tuple-element.18), channel_id=1, source_target_pairs={{0,1},{1,0},{2,3},{3,2},{4,5},{5,4},{6,7},{7,6},{8,9},{9,8},{10,11... | collective-permute-start | bytes 4718600 | tf_op jit(solution)/shard_map/ppermute | solution.py:325
  97.1 3.1 %collective-permute-start.13 = (bf16[2,7,8,32,128]{4,3,2,1,0:T(8,128)(2,1)}, bf16[2,7,8,32,128]{4,3,2,1,0:T(8,128)(2,1)S(1)}, u32[]{:S(2)}, u32[]{:S(2)}) collective-permute-start(bf16[2,7,8,32,128]{4,3,2,1,0:T(8,128)(2,1)} %get-tuple-element.20), channel_id=1, source_target_pairs={{0,128},{32,160},{64,192},{96,224},{128,0},{160,32},{192,64},{224,... | collective-permute-start | bytes 2752520 | tf_op jit(solution)/shard_map/ppermute | solution.py:317
  100.3 3.7 %collective-permute-start.15 = (bf16[2,7,8,32,128]{4,3,2,1,0:T(8,128)(2,1)}, bf16[2,7,8,32,128]{4,3,2,1,0:T(8,128)(2,1)S(1)}, u32[]{:S(2)}, u32[]{:S(2)}) collective-permute-start(bf16[2,7,8,32,128]{4,3,2,1,0:T(8,128)(2,1)} %get-tuple-element.24), channel_id=1, source_target_pairs={{0,384},{32,416},{64,448},{96,480},{128,256},{160,288},{192,320},{... | collective-permute-start | bytes 2752520 | tf_op jit(solution)/shard_map/ppermute | solution.py:318
  104.0 0.0 collective-permute-done.12.b_ref
  104.0 1.4 copy-done.5
  105.4 1.4 add_cores.1
  106.8 12.0 %all-to-all-start = ((bf16[16,24,2048]{2,1,0:T(8,128)(2,1)}), bf16[16,24,2048]{2,1,0:T(8,128)(2,1)S(1)}, u32[]{:S(2)}, u32[]{:S(2)}) async-start(bf16[16,24,2048]{2,1,0:T(8,128)(2,1)} %add_cores.1), calls=%async_computation | async-start | bytes 3145728 | tf_op jit(solution)/shard_map/all_to_all | solution.py:326
  118.8 2.4 %collective-permute-done.13.b_ref.up_a = bf16[2,7,8,32,128]{4,3,2,1,0:T(8,128)(2,1)S(1)} collective-permute-done((bf16[2,7,8,32,128]{4,3,2,1,0:T(8,128)(2,1)}, bf16[2,7,8,32,128]{4,3,2,1,0:T(8,128)(2,1)S(1)}, u32[]{:S(2)}, u32[]{:S(2)}) %collective-permute-start.13) | collective-permute-done | bytes 917536 | tf_op jit(solution)/shard_map/ppermute | solution.py:317
  121.1 1.0 copy-done.7
  122.2 0.1 add_up.1
  122.3 4.5 %collective-permute-start.14 = (bf16[7,8,32,128]{3,2,1,0:T(8,128)(2,1)S(1)}, bf16[7,8,32,128]{3,2,1,0:T(8,128)(2,1)S(1)}, u32[]{:S(2)}, u32[]{:S(2)}) collective-permute-start(bf16[7,8,32,128]{3,2,1,0:T(8,128)(2,1)S(1)} %add_up.1), channel_id=1, source_target_pairs={{0,384},{32,416},{64,448},{96,480},{128,256},{160,288},{192,320},{... | collective-permute-start | bytes 1376264 | tf_op jit(solution)/shard_map/ppermute | solution.py:319
  126.8 0.0 collective-permute-done.15.b_ref.down_b
  126.8 0.1 add_down.1
  127.0 2.1 %collective-permute-start.16 = (bf16[7,8,32,128]{3,2,1,0:T(8,128)(2,1)S(1)}, bf16[7,8,32,128]{3,2,1,0:T(8,128)(2,1)S(1)}, u32[]{:S(2)}, u32[]{:S(2)}) collective-permute-start(bf16[7,8,32,128]{3,2,1,0:T(8,128)(2,1)S(1)} %add_down.1), channel_id=1, source_target_pairs={{0,128},{32,160},{64,192},{96,224},{128,0},{160,32},{192,64},{224,... | collective-permute-start | bytes 1376264 | tf_op jit(solution)/shard_map/ppermute | solution.py:320
  129.0 7.7 %collective-permute-done.14.up_b = bf16[7,8,32,128]{3,2,1,0:T(8,128)(2,1)S(1)} collective-permute-done((bf16[7,8,32,128]{3,2,1,0:T(8,128)(2,1)S(1)}, bf16[7,8,32,128]{3,2,1,0:T(8,128)(2,1)S(1)}, u32[]{:S(2)}, u32[]{:S(2)}) %collective-permute-start.14) | collective-permute-done | bytes 458784 | tf_op jit(solution)/shard_map/ppermute | solution.py:319
  136.7 3.2 %collective-permute-done.16.down_a = bf16[7,8,32,128]{3,2,1,0:T(8,128)(2,1)S(1)} collective-permute-done((bf16[7,8,32,128]{3,2,1,0:T(8,128)(2,1)S(1)}, bf16[7,8,32,128]{3,2,1,0:T(8,128)(2,1)S(1)}, u32[]{:S(2)}, u32[]{:S(2)}) %collective-permute-start.16) | collective-permute-done | bytes 458784 | tf_op jit(solution)/shard_map/ppermute | solution.py:320
  139.9 1.9 %x_sum.1 = (bf16[2,7,64,128]{3,2,1,0:T(8,128)(2,1)S(1)}, bf16[2,7,64,128]{3,2,1,0:T(8,128)(2,1)}, bf16[2,7,64,128]{3,2,1,0:T(8,128)(2,1)}, bf16[2,7,64,128]{3,2,1,0:T(8,128)(2,1)}) custom-call(s32[5]{0:T(128)S(1)} %copy-done.4, bf16[7,8,32,128]{3,2,1,0:T(8,128)(2,1)S(1)} %copy-done, bf16[2,7,8,32,128]{4,3,2,1,0:T(8,128)(2,1)S(1)} %collective-permute-done.13.b_ref.up_a, ...), custom_call_target="tpu_custom_call" | custom-call | flops 2097152 | bytes 4194304 | tf_op jit(solution)/shard_map/x_sum/pallas_call | solution.py:233
  141.7 0.7 copy-done.2
  142.5 1.9 %collective-permute-start.18 = (bf16[2,7,64,128]{3,2,1,0:T(8,128)(2,1)}, bf16[2,7,64,128]{3,2,1,0:T(8,128)(2,1)S(1)}, u32[]{:S(2)}, u32[]{:S(2)}) collective-permute-start(bf16[2,7,64,128]{3,2,1,0:T(8,128)(2,1)} %get-tuple-element.28), channel_id=1, source_target_pairs={{0,64},{32,96},{64,0},{96,32},{128,192},{160,224},{192,128},{224,1... | collective-permute-start | bytes 688136 | tf_op jit(solution)/shard_map/ppermute | solution.py:359
  144.4 1.9 %collective-permute-start.19 = (bf16[2,7,64,128]{3,2,1,0:T(8,128)(2,1)}, bf16[2,7,64,128]{3,2,1,0:T(8,128)(2,1)S(1)}, u32[]{:S(2)}, u32[]{:S(2)}) collective-permute-start(bf16[2,7,64,128]{3,2,1,0:T(8,128)(2,1)} %get-tuple-element.29), channel_id=1, source_target_pairs={{0,96},{32,64},{64,32},{96,0},{128,224},{160,192},{192,160},{224,1... | collective-permute-start | bytes 688136 | tf_op jit(solution)/shard_map/ppermute | solution.py:359
  146.3 5.4 %collective-permute-start.20 = (bf16[2,7,64,128]{3,2,1,0:T(8,128)(2,1)}, bf16[2,7,64,128]{3,2,1,0:T(8,128)(2,1)S(1)}, u32[]{:S(2)}, u32[]{:S(2)}) collective-permute-start(bf16[2,7,64,128]{3,2,1,0:T(8,128)(2,1)} %get-tuple-element.30), channel_id=1, source_target_pairs={{0,32},{32,0},{64,96},{96,64},{128,160},{160,128},{192,224},{224,1... | collective-permute-start | bytes 688136 | tf_op jit(solution)/shard_map/ppermute | solution.py:359
  151.7 8.6 %all-to-all-done.parts_ref = bf16[16,24,2048]{2,1,0:T(8,128)(2,1)S(1)} async-done(((bf16[16,24,2048]{2,1,0:T(8,128)(2,1)}), bf16[16,24,2048]{2,1,0:T(8,128)(2,1)S(1)}, u32[]{:S(2)}, u32[]{:S(2)}) %all-to-all-start) | async-done | bytes 1572896 | tf_op jit(solution)/shard_map/all_to_all | solution.py:326
  160.4 0.4 total_terms.1
  160.9 4.3 %collective-permute-start.17 = (bf16[6,4096]{1,0:T(8,128)(2,1)S(1)}, bf16[6,4096]{1,0:T(8,128)(2,1)S(1)}, u32[]{:S(2)}, u32[]{:S(2)}) collective-permute-start(bf16[6,4096]{1,0:T(8,128)(2,1)S(1)} %broadcast_select_fusion.6), channel_id=1, source_target_pairs={{0,1},{1,0},{2,3},{3,2},{4,5},{5,4},{6,7},{7,6},{8,9},{9,8},{10,11... | collective-permute-start | bytes 147464 | tf_op jit(solution)/shard_map/ppermute | solution.py:334
  165.2 5.2 %collective-permute-done.18 = bf16[2,7,64,128]{3,2,1,0:T(8,128)(2,1)S(1)} collective-permute-done((bf16[2,7,64,128]{3,2,1,0:T(8,128)(2,1)}, bf16[2,7,64,128]{3,2,1,0:T(8,128)(2,1)S(1)}, u32[]{:S(2)}, u32[]{:S(2)}) %collective-permute-start.18) | collective-permute-done | bytes 229408 | tf_op jit(solution)/shard_map/ppermute | solution.py:359
  170.4 9.8 %collective-permute-done.19 = bf16[2,7,64,128]{3,2,1,0:T(8,128)(2,1)S(1)} collective-permute-done((bf16[2,7,64,128]{3,2,1,0:T(8,128)(2,1)}, bf16[2,7,64,128]{3,2,1,0:T(8,128)(2,1)S(1)}, u32[]{:S(2)}, u32[]{:S(2)}) %collective-permute-start.19) | collective-permute-done | bytes 229408 | tf_op jit(solution)/shard_map/ppermute | solution.py:359
  180.2 0.0 collective-permute-done.20
  180.2 0.1 add_convert_fusion
  180.3 0.7 slice_bitcast_fusion
  181.0 0.0 collective-permute-done.17
  181.1 0.7 pad_maximum_fusion.2
  (32 shorter events, 0.5 us)
Async XLA Ops:
  1.6 3.6 %collective-permute-start = (bf16[6,8192]{1,0:T(8,128)(2,1)S(1)}, bf16[6,8192]{1,0:T(8,128)(2,1)S(1)}, u32[]{:S(2)}, u32[]{:S(2)}) collective-permute-start(bf16[6,8192]{1,0:T(8,128)(2,1)S(1)} %broadcast_select_fusion.2), channel_id=1, source_target_pairs={{0,1},{1,0},{2,3},{3,2},{4,5},{5,4},{6,7},{7,6},{8,9},{9,8},{10,11... | collective-permute-start | bytes 294920 | tf_op jit(solution)/shard_map/ppermute | solution.py:288
  6.2 18.4 %collective-permute-start.1 = (bf16[24,4096]{1,0:T(8,128)(2,1)S(1)}, bf16[24,4096]{1,0:T(8,128)(2,1)S(1)}, u32[]{:S(2)}, u32[]{:S(2)}) collective-permute-start(bf16[24,4096]{1,0:T(8,128)(2,1)S(1)} %pad_maximum_fusion), channel_id=1, source_target_pairs={{0,16},{1,17},{2,18},{3,19},{4,20},{5,21},{6,22},{7,23},{8,24},{9,... | collective-permute-start | bytes 589832 | tf_op jit(solution)/shard_map/ppermute | solution.py:292
  24.8 13.2 %collective-permute-start.3 = (bf16[24,8192]{1,0:T(8,128)(2,1)S(1)}, bf16[24,8192]{1,0:T(8,128)(2,1)S(1)}, u32[]{:S(2)}, u32[]{:S(2)}) collective-permute-start(bf16[24,8192]{1,0:T(8,128)(2,1)S(1)} %maximum_maximum_fusion), channel_id=1, source_target_pairs={{0,14},{1,15},{2,0},{3,1},{4,2},{5,3},{6,4},{7,5},{8,6},{9,7},{10,... | collective-permute-start | bytes 1179656 | tf_op jit(solution)/shard_map/ppermute | solution.py:306
  27.8 12.2 %collective-permute-start.2 = (bf16[24,8192]{1,0:T(8,128)(2,1)S(1)}, bf16[24,8192]{1,0:T(8,128)(2,1)S(1)}, u32[]{:S(2)}, u32[]{:S(2)}) collective-permute-start(bf16[24,8192]{1,0:T(8,128)(2,1)S(1)} %maximum_maximum_fusion), channel_id=1, source_target_pairs={{0,2},{1,3},{2,4},{3,5},{4,6},{5,7},{6,8},{7,9},{8,10},{9,11},{10,... | collective-permute-start | bytes 1179656 | tf_op jit(solution)/shard_map/ppermute | solution.py:305
  38.0 12.3 %collective-permute-start.5 = (bf16[24,8192]{1,0:T(8,128)(2,1)S(1)}, bf16[24,8192]{1,0:T(8,128)(2,1)S(1)}, u32[]{:S(2)}, u32[]{:S(2)}) collective-permute-start(bf16[24,8192]{1,0:T(8,128)(2,1)S(1)} %collective-permute-done.3), channel_id=1, source_target_pairs={{0,14},{1,15},{2,0},{3,1},{4,2},{5,3},{6,4},{7,5},{8,6},{9,7},{10,... | collective-permute-start | bytes 1179656 | tf_op jit(solution)/shard_map/ppermute | solution.py:306
  40.0 12.3 %collective-permute-start.4 = (bf16[24,8192]{1,0:T(8,128)(2,1)S(1)}, bf16[24,8192]{1,0:T(8,128)(2,1)S(1)}, u32[]{:S(2)}, u32[]{:S(2)}) collective-permute-start(bf16[24,8192]{1,0:T(8,128)(2,1)S(1)} %collective-permute-done.2), channel_id=1, source_target_pairs={{0,2},{1,3},{2,4},{3,5},{4,6},{5,7},{6,8},{7,9},{8,10},{9,11},{10,... | collective-permute-start | bytes 1179656 | tf_op jit(solution)/shard_map/ppermute | solution.py:305
  50.3 11.4 %collective-permute-start.7 = (bf16[24,8192]{1,0:T(8,128)(2,1)S(1)}, bf16[24,8192]{1,0:T(8,128)(2,1)S(1)}, u32[]{:S(2)}, u32[]{:S(2)}) collective-permute-start(bf16[24,8192]{1,0:T(8,128)(2,1)S(1)} %collective-permute-done.5), channel_id=1, source_target_pairs={{0,14},{1,15},{2,0},{3,1},{4,2},{5,3},{6,4},{7,5},{8,6},{9,7},{10,... | collective-permute-start | bytes 1179656 | tf_op jit(solution)/shard_map/ppermute | solution.py:306
  52.3 11.4 %collective-permute-start.6 = (bf16[24,8192]{1,0:T(8,128)(2,1)S(1)}, bf16[24,8192]{1,0:T(8,128)(2,1)S(1)}, u32[]{:S(2)}, u32[]{:S(2)}) collective-permute-start(bf16[24,8192]{1,0:T(8,128)(2,1)S(1)} %collective-permute-done.4), channel_id=1, source_target_pairs={{0,2},{1,3},{2,4},{3,5},{4,6},{5,7},{6,8},{7,9},{8,10},{9,11},{10,... | collective-permute-start | bytes 1179656 | tf_op jit(solution)/shard_map/ppermute | solution.py:305
  61.7 12.5 %collective-permute-start.9 = (bf16[24,4096]{1,0:T(8,128)(2,1)S(1)}, bf16[24,4096]{1,0:T(8,128)(2,1)S(1)}, u32[]{:S(2)}, u32[]{:S(2)}) collective-permute-start(bf16[24,4096]{1,0:T(8,128)(2,1)S(1)} %slice.55), channel_id=1, source_target_pairs={{0,14},{1,15},{2,0},{3,1},{4,2},{5,3},{6,4},{7,5},{8,6},{9,7},{10,... | collective-permute-start | bytes 589832 | tf_op jit(solution)/shard_map/ppermute | solution.py:312
  63.7 10.5 %collective-permute-start.8 = (bf16[24,4096]{1,0:T(8,128)(2,1)S(1)}, bf16[24,4096]{1,0:T(8,128)(2,1)S(1)}, u32[]{:S(2)}, u32[]{:S(2)}) collective-permute-start(bf16[24,4096]{1,0:T(8,128)(2,1)S(1)} %slice.54), channel_id=1, source_target_pairs={{0,2},{1,3},{2,4},{3,5},{4,6},{5,7},{6,8},{7,9},{8,10},{9,11},{10,... | collective-permute-start | bytes 589832 | tf_op jit(solution)/shard_map/ppermute | solution.py:311
  68.3 11.1 %copy-start.8 = (bf16[6,24,8192]{2,1,0:T(8,128)(2,1)}, bf16[6,24,8192]{2,1,0:T(8,128)(2,1)S(1)}, u32[]{:S(2)}) copy-start(bf16[6,24,8192]{2,1,0:T(8,128)(2,1)S(1)} %bitcast_dynamic-update-slice_fusion.1) | copy-start | bytes 7077892
  68.3 11.1 %collective-permute-start.10 = (bf16[144,8192]{1,0:T(8,128)(2,1)S(1)}, bf16[144,8192]{1,0:T(8,128)(2,1)}, u32[]{:S(2)}, u32[]{:S(2)}) collective-permute-start(bf16[144,8192]{1,0:T(8,128)(2,1)S(1)} %bitcast.29), channel_id=1, source_target_pairs={{0,1},{1,0},{2,3},{3,2},{4,5},{5,4},{6,7},{7,6},{8,9},{9,8},{10,11... | collective-permute-start | bytes 7077896 | tf_op jit(solution)/shard_map/ppermute | solution.py:347
  74.2 5.2 %copy-start.9 = (bf16[2,24,8192]{2,1,0:T(8,128)(2,1)}, bf16[2,24,8192]{2,1,0:T(8,128)(2,1)S(1)}, u32[]{:S(2)}) copy-start(bf16[2,24,8192]{2,1,0:T(8,128)(2,1)S(1)} %bitcast_dynamic-update-slice_fusion.7) | copy-start | bytes 2359300
  74.2 5.2 %collective-permute-start.11 = (bf16[48,8192]{1,0:T(8,128)(2,1)S(1)}, bf16[48,8192]{1,0:T(8,128)(2,1)}, u32[]{:S(2)}, u32[]{:S(2)}) collective-permute-start(bf16[48,8192]{1,0:T(8,128)(2,1)S(1)} %bitcast.31), channel_id=1, source_target_pairs={{0,1},{1,0},{2,3},{3,2},{4,5},{5,4},{6,7},{7,6},{8,9},{9,8},{10,11... | collective-permute-start | bytes 2359304 | tf_op jit(solution)/shard_map/ppermute | solution.py:347
  94.8 9.2 %collective-permute-start.12 = (bf16[16,24,2048]{2,1,0:T(8,128)(2,1)}, bf16[16,24,2048]{2,1,0:T(8,128)(2,1)S(1)}, u32[]{:S(2)}, u32[]{:S(2)}) collective-permute-start(bf16[16,24,2048]{2,1,0:T(8,128)(2,1)} %get-tuple-element.18), channel_id=1, source_target_pairs={{0,1},{1,0},{2,3},{3,2},{4,5},{5,4},{6,7},{7,6},{8,9},{9,8},{10,11... | collective-permute-start | bytes 4718600 | tf_op jit(solution)/shard_map/ppermute | solution.py:325
  97.1 24.0 %collective-permute-start.13 = (bf16[2,7,8,32,128]{4,3,2,1,0:T(8,128)(2,1)}, bf16[2,7,8,32,128]{4,3,2,1,0:T(8,128)(2,1)S(1)}, u32[]{:S(2)}, u32[]{:S(2)}) collective-permute-start(bf16[2,7,8,32,128]{4,3,2,1,0:T(8,128)(2,1)} %get-tuple-element.20), channel_id=1, source_target_pairs={{0,128},{32,160},{64,192},{96,224},{128,0},{160,32},{192,64},{224,... | collective-permute-start | bytes 2752520 | tf_op jit(solution)/shard_map/ppermute | solution.py:317
  100.3 26.5 %collective-permute-start.15 = (bf16[2,7,8,32,128]{4,3,2,1,0:T(8,128)(2,1)}, bf16[2,7,8,32,128]{4,3,2,1,0:T(8,128)(2,1)S(1)}, u32[]{:S(2)}, u32[]{:S(2)}) collective-permute-start(bf16[2,7,8,32,128]{4,3,2,1,0:T(8,128)(2,1)} %get-tuple-element.24), channel_id=1, source_target_pairs={{0,384},{32,416},{64,448},{96,480},{128,256},{160,288},{192,320},{... | collective-permute-start | bytes 2752520 | tf_op jit(solution)/shard_map/ppermute | solution.py:318
  104.0 1.4 copy-start.5
  106.8 53.6 %all-to-all-start = ((bf16[16,24,2048]{2,1,0:T(8,128)(2,1)}), bf16[16,24,2048]{2,1,0:T(8,128)(2,1)S(1)}, u32[]{:S(2)}, u32[]{:S(2)}) async-start(bf16[16,24,2048]{2,1,0:T(8,128)(2,1)} %add_cores.1), calls=%async_computation | async-start | bytes 3145728 | tf_op jit(solution)/shard_map/all_to_all | solution.py:326
  121.1 1.0 copy-start.7
  122.2 4.6 %copy-start.6 = (bf16[7,8,32,128]{3,2,1,0:T(8,128)(2,1)S(1)}, bf16[7,8,32,128]{3,2,1,0:T(8,128)(2,1)}, u32[]{:S(2)}) copy-start(bf16[7,8,32,128]{3,2,1,0:T(8,128)(2,1)} %get-tuple-element.23.a_ref) | copy-start | bytes 1376260
  122.3 14.4 %collective-permute-start.14 = (bf16[7,8,32,128]{3,2,1,0:T(8,128)(2,1)S(1)}, bf16[7,8,32,128]{3,2,1,0:T(8,128)(2,1)S(1)}, u32[]{:S(2)}, u32[]{:S(2)}) collective-permute-start(bf16[7,8,32,128]{3,2,1,0:T(8,128)(2,1)S(1)} %add_up.1), channel_id=1, source_target_pairs={{0,384},{32,416},{64,448},{96,480},{128,256},{160,288},{192,320},{... | collective-permute-start | bytes 1376264 | tf_op jit(solution)/shard_map/ppermute | solution.py:319
  126.8 13.0 %copy-start = (bf16[7,8,32,128]{3,2,1,0:T(8,128)(2,1)S(1)}, bf16[7,8,32,128]{3,2,1,0:T(8,128)(2,1)}, u32[]{:S(2)}) copy-start(bf16[7,8,32,128]{3,2,1,0:T(8,128)(2,1)} %get-tuple-element.19.up_own) | copy-start | bytes 1376260
  126.8 13.0 %copy-start.1 = (bf16[7,8,32,128]{3,2,1,0:T(8,128)(2,1)S(1)}, bf16[7,8,32,128]{3,2,1,0:T(8,128)(2,1)}, u32[]{:S(2)}) copy-start(bf16[7,8,32,128]{3,2,1,0:T(8,128)(2,1)} %get-tuple-element.22.down_own) | copy-start | bytes 1376260
  126.8 13.0 %copy-start.4 = (s32[5]{0:T(128)S(1)}, s32[5]{0:T(128)}, u32[]{:S(2)}) copy-start(s32[5]{0:T(128)} %stack.23.place_ref) | copy-start | bytes 64
  127.0 12.9 %collective-permute-start.16 = (bf16[7,8,32,128]{3,2,1,0:T(8,128)(2,1)S(1)}, bf16[7,8,32,128]{3,2,1,0:T(8,128)(2,1)S(1)}, u32[]{:S(2)}, u32[]{:S(2)}) collective-permute-start(bf16[7,8,32,128]{3,2,1,0:T(8,128)(2,1)S(1)} %add_down.1), channel_id=1, source_target_pairs={{0,128},{32,160},{64,192},{96,224},{128,0},{160,32},{192,64},{224,... | collective-permute-start | bytes 1376264 | tf_op jit(solution)/shard_map/ppermute | solution.py:320
  141.7 0.7 copy-start.2
  142.5 27.9 %collective-permute-start.18 = (bf16[2,7,64,128]{3,2,1,0:T(8,128)(2,1)}, bf16[2,7,64,128]{3,2,1,0:T(8,128)(2,1)S(1)}, u32[]{:S(2)}, u32[]{:S(2)}) collective-permute-start(bf16[2,7,64,128]{3,2,1,0:T(8,128)(2,1)} %get-tuple-element.28), channel_id=1, source_target_pairs={{0,64},{32,96},{64,0},{96,32},{128,192},{160,224},{192,128},{224,1... | collective-permute-start | bytes 688136 | tf_op jit(solution)/shard_map/ppermute | solution.py:359
  144.4 35.8 %collective-permute-start.19 = (bf16[2,7,64,128]{3,2,1,0:T(8,128)(2,1)}, bf16[2,7,64,128]{3,2,1,0:T(8,128)(2,1)S(1)}, u32[]{:S(2)}, u32[]{:S(2)}) collective-permute-start(bf16[2,7,64,128]{3,2,1,0:T(8,128)(2,1)} %get-tuple-element.29), channel_id=1, source_target_pairs={{0,96},{32,64},{64,32},{96,0},{128,224},{160,192},{192,160},{224,1... | collective-permute-start | bytes 688136 | tf_op jit(solution)/shard_map/ppermute | solution.py:359
  146.3 33.9 %collective-permute-start.20 = (bf16[2,7,64,128]{3,2,1,0:T(8,128)(2,1)}, bf16[2,7,64,128]{3,2,1,0:T(8,128)(2,1)S(1)}, u32[]{:S(2)}, u32[]{:S(2)}) collective-permute-start(bf16[2,7,64,128]{3,2,1,0:T(8,128)(2,1)} %get-tuple-element.30), channel_id=1, source_target_pairs={{0,32},{32,0},{64,96},{96,64},{128,160},{160,128},{192,224},{224,1... | collective-permute-start | bytes 688136 | tf_op jit(solution)/shard_map/ppermute | solution.py:359
  160.4 19.8 %copy-start.3 = (bf16[2,7,64,128]{3,2,1,0:T(8,128)(2,1)S(1)}, bf16[2,7,64,128]{3,2,1,0:T(8,128)(2,1)}, u32[]{:S(2)}) copy-start(bf16[2,7,64,128]{3,2,1,0:T(8,128)(2,1)} %copy-done.2) | copy-start | bytes 688132
  160.9 20.1 %collective-permute-start.17 = (bf16[6,4096]{1,0:T(8,128)(2,1)S(1)}, bf16[6,4096]{1,0:T(8,128)(2,1)S(1)}, u32[]{:S(2)}, u32[]{:S(2)}) collective-permute-start(bf16[6,4096]{1,0:T(8,128)(2,1)S(1)} %broadcast_select_fusion.6), channel_id=1, source_target_pairs={{0,1},{1,0},{2,3},{3,2},{4,5},{5,4},{6,7},{7,6},{8,9},{9,8},{10,11... | collective-permute-start | bytes 147464 | tf_op jit(solution)/shard_map/ppermute | solution.py:334

commit v5 on v4

--- a/solution.py
+++ b/solution.py
@@ -356,7 +356,7 @@
     first = pieces[0]
     input_terms, first = lax.optimization_barrier((input_terms, first))
     grad_in = own_rows(input_terms, core)
-    pieces = [first] + [lax.ppermute(pieces[r], "seq", Z_TRADE[r]) for r in (2, 3, 1)]
+    pieces = [first] + [lax.ppermute(pieces[r], "seq", Z_TRADE[r]) for r in (3, 2, 1)]
     total = sum(piece.astype(jnp.float32) for piece in pieces).astype(jnp.bfloat16)
     grad_up, grad_down = total[0].reshape(shape), total[1].reshape(shape)
     return (grad_in, grad_up, grad_down)

time: 183 us -> 183 us (level)
  the two profiles are of different devices: /device:TPU:185 before, /device:TPU:8 now
where the time goes in v5:
time: 183 us; the launch traced here: 182 us
  starting transfers between devices  91.1 us (50%)
  waiting for transfers between devices  62.1 us (34%)
  Pallas kernels  19.2 us (10%)
  local copies, waits for them, and re-layouts  5.11 us (3%)
  other arithmetic  3.03 us (2%)
    ppermute x3, waiting for transfers between devices, local(): lax.ppermute(pieces[r], 'seq', Z_TRADE[r])  16 us
    pallas_call x1, Pallas kernels, block_parts(): pl.pallas_call(functools.partial(block_kernel, factor), in_specs=[SMEM] *...  15.3 us
    ppermute x3, starting transfers between devices, gather_rows(): down = lax.ppermute(down, 'tensor', Y_DOWN)  15 us
    all_to_all x1, starting transfers between devices, reduce_inputs(): lax.all_to_all(part, 'tensor', 0, 0, axis_index_groups=ROW_GROUPS, tiled=...  14.9 us
    ppermute x3, waiting for transfers between devices, gather_rows(): down = lax.ppermute(down, 'tensor', Y_DOWN)  14.5 us
    ppermute x3, starting transfers between devices, local(): lax.ppermute(pieces[r], 'seq', Z_TRADE[r])  14.3 us
    ppermute x1, starting transfers between devices, gather_rows(): other = lax.ppermute(pair, 'tensor', Z_PARTNER)  10.9 us
    ppermute x1, waiting for transfers between devices, reduce_weights_x(): up_odd = lax.ppermute(add_terms(up_odd, even, 20, 'add_up'), 'seq', X_ODD)  8.46 us
  transfers between devices with their start and end apart: 22, of which 14 were waited for; matrix products, arithmetic and copies ran while one was open for 1% of the time, Pallas kernels for 2%

profile of v5, /device:TPU:8, one launch (start us, length us, event | category | flops | bytes accessed | tf_op | source)
XLA Modules:
  0.0 181.6 jit_solution(1211404593309273695)
XLA Ops:
  0.6 0.9 broadcast_select_fusion.2
  1.6 1.9 %collective-permute-start = (bf16[6,8192]{1,0:T(8,128)(2,1)S(1)}, bf16[6,8192]{1,0:T(8,128)(2,1)S(1)}, u32[]{:S(2)}, u32[]{:S(2)}) collective-permute-start(bf16[6,8192]{1,0:T(8,128)(2,1)S(1)} %broadcast_select_fusion.2), channel_id=1, source_target_pairs={{0,1},{1,0},{2,3},{3,2},{4,5},{5,4},{6,7},{7,6},{8,9},{9,8},{10,11... | collective-permute-start | bytes 294920 | tf_op jit(solution)/shard_map/ppermute | solution.py:288
  3.5 1.3 collective-permute-done
  4.8 0.9 broadcast_select_fusion.1
  5.8 0.1 fusion
  5.9 0.1 pad_maximum_fusion
  5.9 10.9 %collective-permute-start.1 = (bf16[24,4096]{1,0:T(8,128)(2,1)S(1)}, bf16[24,4096]{1,0:T(8,128)(2,1)S(1)}, u32[]{:S(2)}, u32[]{:S(2)}) collective-permute-start(bf16[24,4096]{1,0:T(8,128)(2,1)S(1)} %pad_maximum_fusion), channel_id=1, source_target_pairs={{0,16},{1,17},{2,18},{3,19},{4,20},{5,21},{6,22},{7,23},{8,24},{9,... | collective-permute-start | bytes 589832 | tf_op jit(solution)/shard_map/ppermute | solution.py:292
  16.8 5.3 %collective-permute-done.1 = bf16[24,4096]{1,0:T(8,128)(2,1)S(1)} collective-permute-done((bf16[24,4096]{1,0:T(8,128)(2,1)S(1)}, bf16[24,4096]{1,0:T(8,128)(2,1)S(1)}, u32[]{:S(2)}, u32[]{:S(2)}) %collective-permute-start.1) | collective-permute-done | bytes 196640 | tf_op jit(solution)/shard_map/ppermute | solution.py:292
  22.2 0.1 maximum_maximum_fusion
  22.3 6.2 %collective-permute-start.3 = (bf16[24,8192]{1,0:T(8,128)(2,1)S(1)}, bf16[24,8192]{1,0:T(8,128)(2,1)S(1)}, u32[]{:S(2)}, u32[]{:S(2)}) collective-permute-start(bf16[24,8192]{1,0:T(8,128)(2,1)S(1)} %maximum_maximum_fusion), channel_id=1, source_target_pairs={{0,14},{1,15},{2,0},{3,1},{4,2},{5,3},{6,4},{7,5},{8,6},{9,7},{10,... | collective-permute-start | bytes 1179656 | tf_op jit(solution)/shard_map/ppermute | solution.py:306
  28.5 1.9 %collective-permute-start.2 = (bf16[24,8192]{1,0:T(8,128)(2,1)S(1)}, bf16[24,8192]{1,0:T(8,128)(2,1)S(1)}, u32[]{:S(2)}, u32[]{:S(2)}) collective-permute-start(bf16[24,8192]{1,0:T(8,128)(2,1)S(1)} %maximum_maximum_fusion), channel_id=1, source_target_pairs={{0,2},{1,3},{2,4},{3,5},{4,6},{5,7},{6,8},{7,9},{8,10},{9,11},{10,... | collective-permute-start | bytes 1179656 | tf_op jit(solution)/shard_map/ppermute | solution.py:305
  30.4 0.2 broadcast_in_dim.33
  30.7 5.6 %collective-permute-done.3 = bf16[24,8192]{1,0:T(8,128)(2,1)S(1)} collective-permute-done((bf16[24,8192]{1,0:T(8,128)(2,1)S(1)}, bf16[24,8192]{1,0:T(8,128)(2,1)S(1)}, u32[]{:S(2)}, u32[]{:S(2)}) %collective-permute-start.3) | collective-permute-done | bytes 393248 | tf_op jit(solution)/shard_map/ppermute | solution.py:306
  36.3 4.4 %collective-permute-start.5 = (bf16[24,8192]{1,0:T(8,128)(2,1)S(1)}, bf16[24,8192]{1,0:T(8,128)(2,1)S(1)}, u32[]{:S(2)}, u32[]{:S(2)}) collective-permute-start(bf16[24,8192]{1,0:T(8,128)(2,1)S(1)} %collective-permute-done.3), channel_id=1, source_target_pairs={{0,14},{1,15},{2,0},{3,1},{4,2},{5,3},{6,4},{7,5},{8,6},{9,7},{10,... | collective-permute-start | bytes 1179656 | tf_op jit(solution)/shard_map/ppermute | solution.py:306
  40.7 0.0 collective-permute-done.2
  40.7 1.9 %collective-permute-start.4 = (bf16[24,8192]{1,0:T(8,128)(2,1)S(1)}, bf16[24,8192]{1,0:T(8,128)(2,1)S(1)}, u32[]{:S(2)}, u32[]{:S(2)}) collective-permute-start(bf16[24,8192]{1,0:T(8,128)(2,1)S(1)} %collective-permute-done.2), channel_id=1, source_target_pairs={{0,2},{1,3},{2,4},{3,5},{4,6},{5,7},{6,8},{7,9},{8,10},{9,11},{10,... | collective-permute-start | bytes 1179656 | tf_op jit(solution)/shard_map/ppermute | solution.py:305
  42.7 4.8 %collective-permute-done.5 = bf16[24,8192]{1,0:T(8,128)(2,1)S(1)} collective-permute-done((bf16[24,8192]{1,0:T(8,128)(2,1)S(1)}, bf16[24,8192]{1,0:T(8,128)(2,1)S(1)}, u32[]{:S(2)}, u32[]{:S(2)}) %collective-permute-start.5) | collective-permute-done | bytes 393248 | tf_op jit(solution)/shard_map/ppermute | solution.py:306
  47.5 4.4 %collective-permute-start.7 = (bf16[24,8192]{1,0:T(8,128)(2,1)S(1)}, bf16[24,8192]{1,0:T(8,128)(2,1)S(1)}, u32[]{:S(2)}, u32[]{:S(2)}) collective-permute-start(bf16[24,8192]{1,0:T(8,128)(2,1)S(1)} %collective-permute-done.5), channel_id=1, source_target_pairs={{0,14},{1,15},{2,0},{3,1},{4,2},{5,3},{6,4},{7,5},{8,6},{9,7},{10,... | collective-permute-start | bytes 1179656 | tf_op jit(solution)/shard_map/ppermute | solution.py:306
  51.9 0.0 collective-permute-done.4
  51.9 1.9 %collective-permute-start.6 = (bf16[24,8192]{1,0:T(8,128)(2,1)S(1)}, bf16[24,8192]{1,0:T(8,128)(2,1)S(1)}, u32[]{:S(2)}, u32[]{:S(2)}) collective-permute-start(bf16[24,8192]{1,0:T(8,128)(2,1)S(1)} %collective-permute-done.4), channel_id=1, source_target_pairs={{0,2},{1,3},{2,4},{3,5},{4,6},{5,7},{6,8},{7,9},{8,10},{9,11},{10,... | collective-permute-start | bytes 1179656 | tf_op jit(solution)/shard_map/ppermute | solution.py:305
  54.0 4.1 %collective-permute-done.7 = bf16[24,8192]{1,0:T(8,128)(2,1)S(1)} collective-permute-done((bf16[24,8192]{1,0:T(8,128)(2,1)S(1)}, bf16[24,8192]{1,0:T(8,128)(2,1)S(1)}, u32[]{:S(2)}, u32[]{:S(2)}) %collective-permute-start.7) | collective-permute-done | bytes 393248 | tf_op jit(solution)/shard_map/ppermute | solution.py:306
  58.0 5.1 %collective-permute-start.9 = (bf16[24,4096]{1,0:T(8,128)(2,1)S(1)}, bf16[24,4096]{1,0:T(8,128)(2,1)S(1)}, u32[]{:S(2)}, u32[]{:S(2)}) collective-permute-start(bf16[24,4096]{1,0:T(8,128)(2,1)S(1)} %slice.55), channel_id=1, source_target_pairs={{0,14},{1,15},{2,0},{3,1},{4,2},{5,3},{6,4},{7,5},{8,6},{9,7},{10,... | collective-permute-start | bytes 589832 | tf_op jit(solution)/shard_map/ppermute | solution.py:312
  63.1 0.5 collective-permute-done.6
  63.6 1.9 %collective-permute-start.8 = (bf16[24,4096]{1,0:T(8,128)(2,1)S(1)}, bf16[24,4096]{1,0:T(8,128)(2,1)S(1)}, u32[]{:S(2)}, u32[]{:S(2)}) collective-permute-start(bf16[24,4096]{1,0:T(8,128)(2,1)S(1)} %slice.54), channel_id=1, source_target_pairs={{0,2},{1,3},{2,4},{3,5},{4,6},{5,7},{6,8},{7,9},{8,10},{9,11},{10,... | collective-permute-start | bytes 589832 | tf_op jit(solution)/shard_map/ppermute | solution.py:311
  65.6 1.9 %collective-permute-start.10 = (bf16[144,8192]{1,0:T(8,128)(2,1)S(1)}, bf16[144,8192]{1,0:T(8,128)(2,1)}, u32[]{:S(2)}, u32[]{:S(2)}) collective-permute-start(bf16[144,8192]{1,0:T(8,128)(2,1)S(1)} %bitcast.29), channel_id=1, source_target_pairs={{0,1},{1,0},{2,3},{3,2},{4,5},{5,4},{6,7},{7,6},{8,9},{9,8},{10,11... | collective-permute-start | bytes 7077896 | tf_op jit(solution)/shard_map/ppermute | solution.py:347
  67.5 0.1 broadcast_in_dim.40
  67.6 4.8 %collective-permute-done.8 = bf16[24,4096]{1,0:T(8,128)(2,1)S(1)} collective-permute-done((bf16[24,4096]{1,0:T(8,128)(2,1)S(1)}, bf16[24,4096]{1,0:T(8,128)(2,1)S(1)}, u32[]{:S(2)}, u32[]{:S(2)}) %collective-permute-start.8) | collective-permute-done | bytes 196640 | tf_op jit(solution)/shard_map/ppermute | solution.py:311
  72.4 0.0 collective-permute-done.9
  72.5 1.9 %collective-permute-start.11 = (bf16[48,8192]{1,0:T(8,128)(2,1)S(1)}, bf16[48,8192]{1,0:T(8,128)(2,1)}, u32[]{:S(2)}, u32[]{:S(2)}) collective-permute-start(bf16[48,8192]{1,0:T(8,128)(2,1)S(1)} %bitcast.31), channel_id=1, source_target_pairs={{0,1},{1,0},{2,3},{3,2},{4,5},{5,4},{6,7},{7,6},{8,9},{9,8},{10,11... | collective-permute-start | bytes 2359304 | tf_op jit(solution)/shard_map/ppermute | solution.py:347
  74.4 0.6 stack.23.place_ref
  75.0 1.8 collective-permute-done.11.other_b
  76.8 0.0 collective-permute-done.10.other_a
  76.8 15.3 %block_parts.1 = (bf16[16,24,2048]{2,1,0:T(8,128)(2,1)}, bf16[16,24,2048]{2,1,0:T(8,128)(2,1)}, bf16[2,7,8,32,128]{4,3,2,1,0:T(8,128)(2,1)}, bf16[2,7,8,32,128]{...) custom-call(s32[5]{0:T(128)} %stack.23.place_ref, ...), custom_call_target="tpu_custom_call" | custom-call | flops 1761607680 | bytes 16777216 | tf_op jit(solution)/shard_map/block_parts/pallas_call | solution.py:204
  92.1 2.0 %collective-permute-start.12 = (bf16[16,24,2048]{2,1,0:T(8,128)(2,1)}, bf16[16,24,2048]{2,1,0:T(8,128)(2,1)S(1)}, u32[]{:S(2)}, u32[]{:S(2)}) collective-permute-start(bf16[16,24,2048]{2,1,0:T(8,128)(2,1)} %get-tuple-element.18), channel_id=1, source_target_pairs={{0,1},{1,0},{2,3},{3,2},{4,5},{5,4},{6,7},{7,6},{8,9},{9,8},{10,11... | collective-permute-start | bytes 4718600 | tf_op jit(solution)/shard_map/ppermute | solution.py:325
  94.1 3.0 %collective-permute-start.13 = (bf16[2,7,8,32,128]{4,3,2,1,0:T(8,128)(2,1)}, bf16[2,7,8,32,128]{4,3,2,1,0:T(8,128)(2,1)S(1)}, u32[]{:S(2)}, u32[]{:S(2)}) collective-permute-start(bf16[2,7,8,32,128]{4,3,2,1,0:T(8,128)(2,1)} %get-tuple-element.20), channel_id=1, source_target_pairs={{0,128},{32,160},{64,192},{96,224},{128,0},{160,32},{192,64},{224,... | collective-permute-start | bytes 2752520 | tf_op jit(solution)/shard_map/ppermute | solution.py:317
  97.1 4.0 %collective-permute-start.15 = (bf16[2,7,8,32,128]{4,3,2,1,0:T(8,128)(2,1)}, bf16[2,7,8,32,128]{4,3,2,1,0:T(8,128)(2,1)S(1)}, u32[]{:S(2)}, u32[]{:S(2)}) collective-permute-start(bf16[2,7,8,32,128]{4,3,2,1,0:T(8,128)(2,1)} %get-tuple-element.24), channel_id=1, source_target_pairs={{0,384},{32,416},{64,448},{96,480},{128,256},{160,288},{192,320},{... | collective-permute-start | bytes 2752520 | tf_op jit(solution)/shard_map/ppermute | solution.py:318
  101.1 0.0 collective-permute-done.12.b_ref
  101.1 1.4 copy-done.5
  102.5 1.4 add_cores.1
  103.9 14.9 %all-to-all-start = ((bf16[16,24,2048]{2,1,0:T(8,128)(2,1)}), bf16[16,24,2048]{2,1,0:T(8,128)(2,1)S(1)}, u32[]{:S(2)}, u32[]{:S(2)}) async-start(bf16[16,24,2048]{2,1,0:T(8,128)(2,1)} %add_cores.1), calls=%async_computation | async-start | bytes 3145728 | tf_op jit(solution)/shard_map/all_to_all | solution.py:326
  118.8 0.1 collective-permute-done.13.b_ref.up_a
  118.9 1.0 copy-done.7
  119.9 0.1 add_up.1
  120.0 4.3 %collective-permute-start.14 = (bf16[7,8,32,128]{3,2,1,0:T(8,128)(2,1)S(1)}, bf16[7,8,32,128]{3,2,1,0:T(8,128)(2,1)S(1)}, u32[]{:S(2)}, u32[]{:S(2)}) collective-permute-start(bf16[7,8,32,128]{3,2,1,0:T(8,128)(2,1)S(1)} %add_up.1), channel_id=1, source_target_pairs={{0,384},{32,416},{64,448},{96,480},{128,256},{160,288},{192,320},{... | collective-permute-start | bytes 1376264 | tf_op jit(solution)/shard_map/ppermute | solution.py:319
  124.4 0.0 collective-permute-done.15.b_ref.down_b
  124.4 0.1 add_down.1
  124.5 2.3 %collective-permute-start.16 = (bf16[7,8,32,128]{3,2,1,0:T(8,128)(2,1)S(1)}, bf16[7,8,32,128]{3,2,1,0:T(8,128)(2,1)S(1)}, u32[]{:S(2)}, u32[]{:S(2)}) collective-permute-start(bf16[7,8,32,128]{3,2,1,0:T(8,128)(2,1)S(1)} %add_down.1), channel_id=1, source_target_pairs={{0,128},{32,160},{64,192},{96,224},{128,0},{160,32},{192,64},{224,... | collective-permute-start | bytes 1376264 | tf_op jit(solution)/shard_map/ppermute | solution.py:320
  126.8 8.5 %collective-permute-done.14.up_b = bf16[7,8,32,128]{3,2,1,0:T(8,128)(2,1)S(1)} collective-permute-done((bf16[7,8,32,128]{3,2,1,0:T(8,128)(2,1)S(1)}, bf16[7,8,32,128]{3,2,1,0:T(8,128)(2,1)S(1)}, u32[]{:S(2)}, u32[]{:S(2)}) %collective-permute-start.14) | collective-permute-done | bytes 458784 | tf_op jit(solution)/shard_map/ppermute | solution.py:319
  135.2 3.0 %collective-permute-done.16.down_a = bf16[7,8,32,128]{3,2,1,0:T(8,128)(2,1)S(1)} collective-permute-done((bf16[7,8,32,128]{3,2,1,0:T(8,128)(2,1)S(1)}, bf16[7,8,32,128]{3,2,1,0:T(8,128)(2,1)S(1)}, u32[]{:S(2)}, u32[]{:S(2)}) %collective-permute-start.16) | collective-permute-done | bytes 458784 | tf_op jit(solution)/shard_map/ppermute | solution.py:320
  138.3 1.9 %x_sum.1 = (bf16[2,7,64,128]{3,2,1,0:T(8,128)(2,1)S(1)}, bf16[2,7,64,128]{3,2,1,0:T(8,128)(2,1)}, bf16[2,7,64,128]{3,2,1,0:T(8,128)(2,1)}, bf16[2,7,64,128]{3,2,1,0:T(8,128)(2,1)}) custom-call(s32[5]{0:T(128)S(1)} %copy-done.4, bf16[7,8,32,128]{3,2,1,0:T(8,128)(2,1)S(1)} %copy-done, bf16[2,7,8,32,128]{4,3,2,1,0:T(8,128)(2,1)S(1)} %collective-permute-done.13.b_ref.up_a, ...), custom_call_target="tpu_custom_call" | custom-call | flops 2097152 | bytes 4194304 | tf_op jit(solution)/shard_map/x_sum/pallas_call | solution.py:233
  140.2 0.7 copy-done.2
  140.9 7.1 %collective-permute-start.18 = (bf16[2,7,64,128]{3,2,1,0:T(8,128)(2,1)}, bf16[2,7,64,128]{3,2,1,0:T(8,128)(2,1)S(1)}, u32[]{:S(2)}, u32[]{:S(2)}) collective-permute-start(bf16[2,7,64,128]{3,2,1,0:T(8,128)(2,1)} %get-tuple-element.28), channel_id=1, source_target_pairs={{0,96},{32,64},{64,32},{96,0},{128,224},{160,192},{192,160},{224,1... | collective-permute-start | bytes 688136 | tf_op jit(solution)/shard_map/ppermute | solution.py:359
  148.0 4.7 %collective-permute-start.19 = (bf16[2,7,64,128]{3,2,1,0:T(8,128)(2,1)}, bf16[2,7,64,128]{3,2,1,0:T(8,128)(2,1)S(1)}, u32[]{:S(2)}, u32[]{:S(2)}) collective-permute-start(bf16[2,7,64,128]{3,2,1,0:T(8,128)(2,1)} %get-tuple-element.29), channel_id=1, source_target_pairs={{0,64},{32,96},{64,0},{96,32},{128,192},{160,224},{192,128},{224,1... | collective-permute-start | bytes 688136 | tf_op jit(solution)/shard_map/ppermute | solution.py:359
  152.7 2.5 %collective-permute-start.20 = (bf16[2,7,64,128]{3,2,1,0:T(8,128)(2,1)}, bf16[2,7,64,128]{3,2,1,0:T(8,128)(2,1)S(1)}, u32[]{:S(2)}, u32[]{:S(2)}) collective-permute-start(bf16[2,7,64,128]{3,2,1,0:T(8,128)(2,1)} %get-tuple-element.30), channel_id=1, source_target_pairs={{0,32},{32,0},{64,96},{96,64},{128,160},{160,128},{192,224},{224,1... | collective-permute-start | bytes 688136 | tf_op jit(solution)/shard_map/ppermute | solution.py:359
  155.2 6.3 %all-to-all-done.parts_ref = bf16[16,24,2048]{2,1,0:T(8,128)(2,1)S(1)} async-done(((bf16[16,24,2048]{2,1,0:T(8,128)(2,1)}), bf16[16,24,2048]{2,1,0:T(8,128)(2,1)S(1)}, u32[]{:S(2)}, u32[]{:S(2)}) %all-to-all-start) | async-done | bytes 1572896 | tf_op jit(solution)/shard_map/all_to_all | solution.py:326
  161.5 0.4 total_terms.1
  162.0 1.9 %collective-permute-start.17 = (bf16[6,4096]{1,0:T(8,128)(2,1)S(1)}, bf16[6,4096]{1,0:T(8,128)(2,1)S(1)}, u32[]{:S(2)}, u32[]{:S(2)}) collective-permute-start(bf16[6,4096]{1,0:T(8,128)(2,1)S(1)} %broadcast_select_fusion.6), channel_id=1, source_target_pairs={{0,1},{1,0},{2,3},{3,2},{4,5},{5,4},{6,7},{7,6},{8,9},{9,8},{10,11... | collective-permute-start | bytes 147464 | tf_op jit(solution)/shard_map/ppermute | solution.py:334
  164.0 1.7 collective-permute-done.18
  165.7 14.3 %collective-permute-done.19 = bf16[2,7,64,128]{3,2,1,0:T(8,128)(2,1)S(1)} collective-permute-done((bf16[2,7,64,128]{3,2,1,0:T(8,128)(2,1)}, bf16[2,7,64,128]{3,2,1,0:T(8,128)(2,1)S(1)}, u32[]{:S(2)}, u32[]{:S(2)}) %collective-permute-start.19) | collective-permute-done | bytes 229408 | tf_op jit(solution)/shard_map/ppermute | solution.py:359
  180.0 0.0 collective-permute-done.20
  180.0 0.1 add_convert_fusion
  180.2 0.7 slice_bitcast_fusion
  180.9 0.0 collective-permute-done.17
  180.9 0.7 pad_maximum_fusion.2
  (32 shorter events, 0.5 us)
Async XLA Ops:
  1.6 3.2 %collective-permute-start = (bf16[6,8192]{1,0:T(8,128)(2,1)S(1)}, bf16[6,8192]{1,0:T(8,128)(2,1)S(1)}, u32[]{:S(2)}, u32[]{:S(2)}) collective-permute-start(bf16[6,8192]{1,0:T(8,128)(2,1)S(1)} %broadcast_select_fusion.2), channel_id=1, source_target_pairs={{0,1},{1,0},{2,3},{3,2},{4,5},{5,4},{6,7},{7,6},{8,9},{9,8},{10,11... | collective-permute-start | bytes 294920 | tf_op jit(solution)/shard_map/ppermute | solution.py:288
  5.9 16.2 %collective-permute-start.1 = (bf16[24,4096]{1,0:T(8,128)(2,1)S(1)}, bf16[24,4096]{1,0:T(8,128)(2,1)S(1)}, u32[]{:S(2)}, u32[]{:S(2)}) collective-permute-start(bf16[24,4096]{1,0:T(8,128)(2,1)S(1)} %pad_maximum_fusion), channel_id=1, source_target_pairs={{0,16},{1,17},{2,18},{3,19},{4,20},{5,21},{6,22},{7,23},{8,24},{9,... | collective-permute-start | bytes 589832 | tf_op jit(solution)/shard_map/ppermute | solution.py:292
  22.3 14.0 %collective-permute-start.3 = (bf16[24,8192]{1,0:T(8,128)(2,1)S(1)}, bf16[24,8192]{1,0:T(8,128)(2,1)S(1)}, u32[]{:S(2)}, u32[]{:S(2)}) collective-permute-start(bf16[24,8192]{1,0:T(8,128)(2,1)S(1)} %maximum_maximum_fusion), channel_id=1, source_target_pairs={{0,14},{1,15},{2,0},{3,1},{4,2},{5,3},{6,4},{7,5},{8,6},{9,7},{10,... | collective-permute-start | bytes 1179656 | tf_op jit(solution)/shard_map/ppermute | solution.py:306
  28.5 12.2 %collective-permute-start.2 = (bf16[24,8192]{1,0:T(8,128)(2,1)S(1)}, bf16[24,8192]{1,0:T(8,128)(2,1)S(1)}, u32[]{:S(2)}, u32[]{:S(2)}) collective-permute-start(bf16[24,8192]{1,0:T(8,128)(2,1)S(1)} %maximum_maximum_fusion), channel_id=1, source_target_pairs={{0,2},{1,3},{2,4},{3,5},{4,6},{5,7},{6,8},{7,9},{8,10},{9,11},{10,... | collective-permute-start | bytes 1179656 | tf_op jit(solution)/shard_map/ppermute | solution.py:305
  36.3 11.3 %collective-permute-start.5 = (bf16[24,8192]{1,0:T(8,128)(2,1)S(1)}, bf16[24,8192]{1,0:T(8,128)(2,1)S(1)}, u32[]{:S(2)}, u32[]{:S(2)}) collective-permute-start(bf16[24,8192]{1,0:T(8,128)(2,1)S(1)} %collective-permute-done.3), channel_id=1, source_target_pairs={{0,14},{1,15},{2,0},{3,1},{4,2},{5,3},{6,4},{7,5},{8,6},{9,7},{10,... | collective-permute-start | bytes 1179656 | tf_op jit(solution)/shard_map/ppermute | solution.py:306
  40.7 11.2 %collective-permute-start.4 = (bf16[24,8192]{1,0:T(8,128)(2,1)S(1)}, bf16[24,8192]{1,0:T(8,128)(2,1)S(1)}, u32[]{:S(2)}, u32[]{:S(2)}) collective-permute-start(bf16[24,8192]{1,0:T(8,128)(2,1)S(1)} %collective-permute-done.2), channel_id=1, source_target_pairs={{0,2},{1,3},{2,4},{3,5},{4,6},{5,7},{6,8},{7,9},{8,10},{9,11},{10,... | collective-permute-start | bytes 1179656 | tf_op jit(solution)/shard_map/ppermute | solution.py:305
  47.5 10.5 %collective-permute-start.7 = (bf16[24,8192]{1,0:T(8,128)(2,1)S(1)}, bf16[24,8192]{1,0:T(8,128)(2,1)S(1)}, u32[]{:S(2)}, u32[]{:S(2)}) collective-permute-start(bf16[24,8192]{1,0:T(8,128)(2,1)S(1)} %collective-permute-done.5), channel_id=1, source_target_pairs={{0,14},{1,15},{2,0},{3,1},{4,2},{5,3},{6,4},{7,5},{8,6},{9,7},{10,... | collective-permute-start | bytes 1179656 | tf_op jit(solution)/shard_map/ppermute | solution.py:306
  51.9 11.6 %collective-permute-start.6 = (bf16[24,8192]{1,0:T(8,128)(2,1)S(1)}, bf16[24,8192]{1,0:T(8,128)(2,1)S(1)}, u32[]{:S(2)}, u32[]{:S(2)}) collective-permute-start(bf16[24,8192]{1,0:T(8,128)(2,1)S(1)} %collective-permute-done.4), channel_id=1, source_target_pairs={{0,2},{1,3},{2,4},{3,5},{4,6},{5,7},{6,8},{7,9},{8,10},{9,11},{10,... | collective-permute-start | bytes 1179656 | tf_op jit(solution)/shard_map/ppermute | solution.py:305
  58.0 14.4 %collective-permute-start.9 = (bf16[24,4096]{1,0:T(8,128)(2,1)S(1)}, bf16[24,4096]{1,0:T(8,128)(2,1)S(1)}, u32[]{:S(2)}, u32[]{:S(2)}) collective-permute-start(bf16[24,4096]{1,0:T(8,128)(2,1)S(1)} %slice.55), channel_id=1, source_target_pairs={{0,14},{1,15},{2,0},{3,1},{4,2},{5,3},{6,4},{7,5},{8,6},{9,7},{10,... | collective-permute-start | bytes 589832 | tf_op jit(solution)/shard_map/ppermute | solution.py:312
  63.6 8.8 %collective-permute-start.8 = (bf16[24,4096]{1,0:T(8,128)(2,1)S(1)}, bf16[24,4096]{1,0:T(8,128)(2,1)S(1)}, u32[]{:S(2)}, u32[]{:S(2)}) collective-permute-start(bf16[24,4096]{1,0:T(8,128)(2,1)S(1)} %slice.54), channel_id=1, source_target_pairs={{0,2},{1,3},{2,4},{3,5},{4,6},{5,7},{6,8},{7,9},{8,10},{9,11},{10,... | collective-permute-start | bytes 589832 | tf_op jit(solution)/shard_map/ppermute | solution.py:311
  65.6 11.2 %copy-start.8 = (bf16[6,24,8192]{2,1,0:T(8,128)(2,1)}, bf16[6,24,8192]{2,1,0:T(8,128)(2,1)S(1)}, u32[]{:S(2)}) copy-start(bf16[6,24,8192]{2,1,0:T(8,128)(2,1)S(1)} %bitcast_dynamic-update-slice_fusion.1) | copy-start | bytes 7077892
  65.6 11.2 %collective-permute-start.10 = (bf16[144,8192]{1,0:T(8,128)(2,1)S(1)}, bf16[144,8192]{1,0:T(8,128)(2,1)}, u32[]{:S(2)}, u32[]{:S(2)}) collective-permute-start(bf16[144,8192]{1,0:T(8,128)(2,1)S(1)} %bitcast.29), channel_id=1, source_target_pairs={{0,1},{1,0},{2,3},{3,2},{4,5},{5,4},{6,7},{7,6},{8,9},{9,8},{10,11... | collective-permute-start | bytes 7077896 | tf_op jit(solution)/shard_map/ppermute | solution.py:347
  72.4 4.3 %copy-start.9 = (bf16[2,24,8192]{2,1,0:T(8,128)(2,1)}, bf16[2,24,8192]{2,1,0:T(8,128)(2,1)S(1)}, u32[]{:S(2)}) copy-start(bf16[2,24,8192]{2,1,0:T(8,128)(2,1)S(1)} %bitcast_dynamic-update-slice_fusion.7) | copy-start | bytes 2359300
  72.5 4.3 %collective-permute-start.11 = (bf16[48,8192]{1,0:T(8,128)(2,1)S(1)}, bf16[48,8192]{1,0:T(8,128)(2,1)}, u32[]{:S(2)}, u32[]{:S(2)}) collective-permute-start(bf16[48,8192]{1,0:T(8,128)(2,1)S(1)} %bitcast.31), channel_id=1, source_target_pairs={{0,1},{1,0},{2,3},{3,2},{4,5},{5,4},{6,7},{7,6},{8,9},{9,8},{10,11... | collective-permute-start | bytes 2359304 | tf_op jit(solution)/shard_map/ppermute | solution.py:347
  92.1 9.0 %collective-permute-start.12 = (bf16[16,24,2048]{2,1,0:T(8,128)(2,1)}, bf16[16,24,2048]{2,1,0:T(8,128)(2,1)S(1)}, u32[]{:S(2)}, u32[]{:S(2)}) collective-permute-start(bf16[16,24,2048]{2,1,0:T(8,128)(2,1)} %get-tuple-element.18), channel_id=1, source_target_pairs={{0,1},{1,0},{2,3},{3,2},{4,5},{5,4},{6,7},{7,6},{8,9},{9,8},{10,11... | collective-permute-start | bytes 4718600 | tf_op jit(solution)/shard_map/ppermute | solution.py:325
  94.1 24.8 %collective-permute-start.13 = (bf16[2,7,8,32,128]{4,3,2,1,0:T(8,128)(2,1)}, bf16[2,7,8,32,128]{4,3,2,1,0:T(8,128)(2,1)S(1)}, u32[]{:S(2)}, u32[]{:S(2)}) collective-permute-start(bf16[2,7,8,32,128]{4,3,2,1,0:T(8,128)(2,1)} %get-tuple-element.20), channel_id=1, source_target_pairs={{0,128},{32,160},{64,192},{96,224},{128,0},{160,32},{192,64},{224,... | collective-permute-start | bytes 2752520 | tf_op jit(solution)/shard_map/ppermute | solution.py:317
  97.1 27.3 %collective-permute-start.15 = (bf16[2,7,8,32,128]{4,3,2,1,0:T(8,128)(2,1)}, bf16[2,7,8,32,128]{4,3,2,1,0:T(8,128)(2,1)S(1)}, u32[]{:S(2)}, u32[]{:S(2)}) collective-permute-start(bf16[2,7,8,32,128]{4,3,2,1,0:T(8,128)(2,1)} %get-tuple-element.24), channel_id=1, source_target_pairs={{0,384},{32,416},{64,448},{96,480},{128,256},{160,288},{192,320},{... | collective-permute-start | bytes 2752520 | tf_op jit(solution)/shard_map/ppermute | solution.py:318
  101.1 1.4 copy-start.5
  103.9 57.6 %all-to-all-start = ((bf16[16,24,2048]{2,1,0:T(8,128)(2,1)}), bf16[16,24,2048]{2,1,0:T(8,128)(2,1)S(1)}, u32[]{:S(2)}, u32[]{:S(2)}) async-start(bf16[16,24,2048]{2,1,0:T(8,128)(2,1)} %add_cores.1), calls=%async_computation | async-start | bytes 3145728 | tf_op jit(solution)/shard_map/all_to_all | solution.py:326
  118.9 1.0 copy-start.7
  119.9 4.5 %copy-start.6 = (bf16[7,8,32,128]{3,2,1,0:T(8,128)(2,1)S(1)}, bf16[7,8,32,128]{3,2,1,0:T(8,128)(2,1)}, u32[]{:S(2)}) copy-start(bf16[7,8,32,128]{3,2,1,0:T(8,128)(2,1)} %get-tuple-element.23.a_ref) | copy-start | bytes 1376260
  120.0 15.2 %collective-permute-start.14 = (bf16[7,8,32,128]{3,2,1,0:T(8,128)(2,1)S(1)}, bf16[7,8,32,128]{3,2,1,0:T(8,128)(2,1)S(1)}, u32[]{:S(2)}, u32[]{:S(2)}) collective-permute-start(bf16[7,8,32,128]{3,2,1,0:T(8,128)(2,1)S(1)} %add_up.1), channel_id=1, source_target_pairs={{0,384},{32,416},{64,448},{96,480},{128,256},{160,288},{192,320},{... | collective-permute-start | bytes 1376264 | tf_op jit(solution)/shard_map/ppermute | solution.py:319
  124.4 13.9 %copy-start = (bf16[7,8,32,128]{3,2,1,0:T(8,128)(2,1)S(1)}, bf16[7,8,32,128]{3,2,1,0:T(8,128)(2,1)}, u32[]{:S(2)}) copy-start(bf16[7,8,32,128]{3,2,1,0:T(8,128)(2,1)} %get-tuple-element.19.up_own) | copy-start | bytes 1376260
  124.4 13.9 %copy-start.1 = (bf16[7,8,32,128]{3,2,1,0:T(8,128)(2,1)S(1)}, bf16[7,8,32,128]{3,2,1,0:T(8,128)(2,1)}, u32[]{:S(2)}) copy-start(bf16[7,8,32,128]{3,2,1,0:T(8,128)(2,1)} %get-tuple-element.22.down_own) | copy-start | bytes 1376260
  124.4 13.9 %copy-start.4 = (s32[5]{0:T(128)S(1)}, s32[5]{0:T(128)}, u32[]{:S(2)}) copy-start(s32[5]{0:T(128)} %stack.23.place_ref) | copy-start | bytes 64
  124.5 13.7 %collective-permute-start.16 = (bf16[7,8,32,128]{3,2,1,0:T(8,128)(2,1)S(1)}, bf16[7,8,32,128]{3,2,1,0:T(8,128)(2,1)S(1)}, u32[]{:S(2)}, u32[]{:S(2)}) collective-permute-start(bf16[7,8,32,128]{3,2,1,0:T(8,128)(2,1)S(1)} %add_down.1), channel_id=1, source_target_pairs={{0,128},{32,160},{64,192},{96,224},{128,0},{160,32},{192,64},{224,... | collective-permute-start | bytes 1376264 | tf_op jit(solution)/shard_map/ppermute | solution.py:320
  140.2 0.7 copy-start.2
  140.9 24.8 %collective-permute-start.18 = (bf16[2,7,64,128]{3,2,1,0:T(8,128)(2,1)}, bf16[2,7,64,128]{3,2,1,0:T(8,128)(2,1)S(1)}, u32[]{:S(2)}, u32[]{:S(2)}) collective-permute-start(bf16[2,7,64,128]{3,2,1,0:T(8,128)(2,1)} %get-tuple-element.28), channel_id=1, source_target_pairs={{0,96},{32,64},{64,32},{96,0},{128,224},{160,192},{192,160},{224,1... | collective-permute-start | bytes 688136 | tf_op jit(solution)/shard_map/ppermute | solution.py:359
  148.0 32.0 %collective-permute-start.19 = (bf16[2,7,64,128]{3,2,1,0:T(8,128)(2,1)}, bf16[2,7,64,128]{3,2,1,0:T(8,128)(2,1)S(1)}, u32[]{:S(2)}, u32[]{:S(2)}) collective-permute-start(bf16[2,7,64,128]{3,2,1,0:T(8,128)(2,1)} %get-tuple-element.29), channel_id=1, source_target_pairs={{0,64},{32,96},{64,0},{96,32},{128,192},{160,224},{192,128},{224,1... | collective-permute-start | bytes 688136 | tf_op jit(solution)/shard_map/ppermute | solution.py:359
  152.7 27.3 %collective-permute-start.20 = (bf16[2,7,64,128]{3,2,1,0:T(8,128)(2,1)}, bf16[2,7,64,128]{3,2,1,0:T(8,128)(2,1)S(1)}, u32[]{:S(2)}, u32[]{:S(2)}) collective-permute-start(bf16[2,7,64,128]{3,2,1,0:T(8,128)(2,1)} %get-tuple-element.30), channel_id=1, source_target_pairs={{0,32},{32,0},{64,96},{96,64},{128,160},{160,128},{192,224},{224,1... | collective-permute-start | bytes 688136 | tf_op jit(solution)/shard_map/ppermute | solution.py:359
  161.5 18.5 %copy-start.3 = (bf16[2,7,64,128]{3,2,1,0:T(8,128)(2,1)S(1)}, bf16[2,7,64,128]{3,2,1,0:T(8,128)(2,1)}, u32[]{:S(2)}) copy-start(bf16[2,7,64,128]{3,2,1,0:T(8,128)(2,1)} %copy-done.2) | copy-start | bytes 688132
  162.0 18.8 %collective-permute-start.17 = (bf16[6,4096]{1,0:T(8,128)(2,1)S(1)}, bf16[6,4096]{1,0:T(8,128)(2,1)S(1)}, u32[]{:S(2)}, u32[]{:S(2)}) collective-permute-start(bf16[6,4096]{1,0:T(8,128)(2,1)S(1)} %broadcast_select_fusion.6), channel_id=1, source_target_pairs={{0,1},{1,0},{2,3},{3,2},{4,5},{5,4},{6,7},{7,6},{8,9},{9,8},{10,11... | collective-permute-start | bytes 147464 | tf_op jit(solution)/shard_map/ppermute | solution.py:334
